TPU v7x, 32 devices: a whole 2x2x4 slice. The times are simulated.
32 devices in a mesh: il: 4 (over x, core), xl: 8 (over z, y).
Axes of the slice: x: 2, y: 2, z: 4, core: 2. Of those that a mesh axis runs over, the one named last changes fastest.
Arguments:
- traces: bfloat16 [245760, 128], P(('il', 'xl')), may hold values from -6 to 6
- filter_taps: float32 [12, 64], replicated, may hold values from -1.5 to 1.5
- slot_block: int32 [32, 32, 7], P(('il', 'xl')), may hold values from 0 to 59
- slot_cells: int32 [32, 32, 7, 128], P(('il', 'xl')), may hold values from -1 to 1535
- pair_count: int32 [32, 32], P(('il', 'xl')), may hold values from 0 to 7, as said below
Outputs:
- structure_tensor: float32 [6, 128, 384, 128], P(None, 'il', 'xl')
- adjoint_traces: float32 [245760, 128], P(('il', 'xl'))
Inputs may be any that keep to these rules, and one draw needn't show every extreme that they name: Slots 0 to pair_count[e, d] - 1 of device e toward tile d are live; at most 7, and for some tiles every device sends 7 live slots.
All inputs are finite; a program needn't handle non-finite values.
Results may differ from a plain program's by a relative error of at most 0.0004.
The roundings to bfloat16 on the way count: a program that leaves them out, or rounds other values in their place, can miss the bound.
Values may be sent and summed in bfloat16 or wider, within the bound.
No kernel may reach another device: no remote copies, remote signals or barrier semaphores. Data moves between devices by JAX's collectives and lax.ppermute only.
A program may use at most 128 MiB of HBM per device.

v0:
```python
import jax
import jax.numpy as jnp
from jax import lax
from jax.sharding import PartitionSpec as P

CIL = 32
CXL = 48


def with_halo(block, sides, width):
    for axis, dim in sides:
        count = lax.axis_size(axis)
        forward = [(i, i + 1) for i in range(count - 1)]
        backward = [(target, source) for source, target in forward]
        low = lax.ppermute(
            lax.slice_in_dim(block, block.shape[dim] - width, None, axis=dim), axis, forward
        )
        high = lax.ppermute(lax.slice_in_dim(block, 0, width, axis=dim), axis, backward)
        block = jnp.concatenate([low, block, high], axis=dim)
    return block


def filter_matrices(filter_taps, samples):
    lag_table = (
        jnp.arange(samples, dtype=jnp.int32)[None, :]
        - jnp.arange(samples, dtype=jnp.int32)[:, None]
    )
    tap_count = filter_taps.shape[1]
    inside = (lag_table >= 0) & (lag_table < tap_count)
    picked = filter_taps[:, jnp.clip(lag_table, 0, tap_count - 1)]
    return jnp.where(inside[None], picked, 0.0).astype(jnp.bfloat16)


def cycle_box(values, rows_out, cols_out):
    box_total = jnp.zeros((rows_out, cols_out, values.shape[2]), jnp.float32)
    for row_shift in range(3):
        for col_shift in range(3):
            box_total = (
                box_total
                + values[row_shift : row_shift + rows_out, col_shift : col_shift + cols_out]
            )
    return box_total / 9.0


def local(traces, filter_taps, slot_block, slot_cells, pair_count):
    count_il = lax.axis_size("il")
    count_xl = lax.axis_size("xl")
    devices = count_il * count_xl
    samples = traces.shape[1]
    row_block = slot_cells.shape[3]
    capacity = slot_block.shape[2]
    surveys = filter_taps.shape[0]
    blocks_here = traces.shape[0] // row_block
    cell_count = CIL * CXL
    group_size = 16
    slot_total = devices * capacity
    group_count = slot_total // group_size
    matrices = filter_matrices(filter_taps, samples)
    by_survey = traces.reshape(surveys, blocks_here // surveys * row_block, samples)
    filtered = jnp.einsum("sru,sut->srt", by_survey, matrices, preferred_element_type=jnp.float32)
    filtered = filtered.astype(jnp.bfloat16).reshape(blocks_here, row_block, samples)
    block_ids = slot_block[0].reshape(-1)
    outgoing = jnp.take(filtered, block_ids, axis=0).reshape(devices, capacity, row_block, samples)
    slot_live = jnp.arange(capacity, dtype=jnp.int32)[None, :] < pair_count[0][:, None]
    out_cells = jnp.where(slot_live[:, :, None], slot_cells[0], -1)
    incoming, in_cells = (
        lax.all_to_all(outgoing, ("il", "xl"), split_axis=0, concat_axis=0, tiled=True),
        lax.all_to_all(out_cells, ("il", "xl"), split_axis=0, concat_axis=0, tiled=True),
    )
    incoming = incoming.reshape(slot_total, row_block, samples)
    in_cells = in_cells.reshape(slot_total, row_block)
    cell_line = jnp.arange(cell_count, dtype=jnp.int32)

    def one_hot(group_cells):
        return (cell_line[:, None] == group_cells.reshape(1, -1)).astype(jnp.bfloat16)

    def add_group(running, group_blocks, group_cells):
        stacked, fold_counts = running
        selector = one_hot(group_cells)
        stacked = stacked + jnp.dot(
            selector, group_blocks.reshape(-1, samples), preferred_element_type=jnp.float32
        )
        fold_counts = fold_counts + jnp.sum(selector, axis=1, dtype=jnp.float32)
        return (stacked, fold_counts)

    initial = (jnp.zeros((cell_count, samples), jnp.float32), jnp.zeros((cell_count,), jnp.float32))

    def scan_step(running, scan_item):
        return (add_group(running, scan_item[0], scan_item[1]), None)

    (stacked, fold_counts), unused = lax.scan(
        scan_step,
        initial,
        (
            incoming.reshape(group_count, group_size, row_block, samples),
            in_cells.reshape(group_count, group_size, row_block),
        ),
    )
    stack_image = stacked / jnp.maximum(fold_counts, 1.0)[:, None]
    image_half = stack_image.astype(jnp.bfloat16)

    def read_group(group_cells):
        selector = one_hot(group_cells)
        picked = lax.dot_general(
            selector, image_half, (((0,), (0,)), ((), ())), preferred_element_type=jnp.float32
        )
        return picked.astype(jnp.bfloat16).reshape(group_size, row_block, samples)

    answer = lax.map(read_group, in_cells.reshape(group_count, group_size, row_block)).reshape(
        slot_total, row_block, samples
    )
    returned = lax.all_to_all(
        answer.reshape(devices, capacity, row_block, samples),
        ("il", "xl"),
        split_axis=0,
        concat_axis=0,
        tiled=True,
    )
    returned = returned.reshape(slot_total, row_block, samples)
    out_valid = (out_cells >= 0).reshape(slot_total, row_block, 1)
    zero_half = jnp.zeros((), jnp.bfloat16)
    sent_part = jnp.where(out_valid, outgoing.reshape(slot_total, row_block, samples), zero_half)
    back_part = jnp.where(out_valid, returned, zero_half)
    selector_rows = (
        block_ids[:, None] == jnp.arange(blocks_here, dtype=jnp.int32)[None, :]
    ).astype(jnp.bfloat16)
    residual = jnp.einsum(
        "sb,sit->bit", selector_rows, sent_part, preferred_element_type=jnp.float32
    )
    residual = residual - jnp.einsum(
        "sb,sit->bit", selector_rows, back_part, preferred_element_type=jnp.float32
    )
    residual_half = residual.astype(jnp.bfloat16).reshape(surveys, -1, samples)
    adjoint_traces = jnp.einsum(
        "srt,sut->sru", residual_half, matrices, preferred_element_type=jnp.float32
    ).reshape(traces.shape)
    tile_image = stack_image.reshape(CIL, CXL, samples)
    padded = with_halo(tile_image, (("il", 0), ("xl", 1)), 2)
    padded_time = jnp.pad(padded, ((0, 0), (0, 0), (1, 1)))
    grad_il = (padded[2:, 1:-1] - padded[:-2, 1:-1]) * 0.5
    grad_xl = (padded[1:-1, 2:] - padded[1:-1, :-2]) * 0.5
    grad_time = (padded_time[1:-1, 1:-1, 2:] - padded_time[1:-1, 1:-1, :-2]) * 0.5
    rows_il = lax.axis_index("il") * CIL + jnp.arange(CIL + 2, dtype=jnp.int32) - 1
    rows_xl = lax.axis_index("xl") * CXL + jnp.arange(CXL + 2, dtype=jnp.int32) - 1
    inside_il = ((rows_il >= 0) & (rows_il < CIL * count_il)).astype(jnp.float32)
    inside_xl = ((rows_xl >= 0) & (rows_xl < CXL * count_xl)).astype(jnp.float32)
    cycle_mask = inside_il[:, None, None] * inside_xl[None, :, None]
    factor_pairs = (
        (grad_il, grad_il),
        (grad_xl, grad_xl),
        (grad_time, grad_time),
        (grad_il, grad_xl),
        (grad_il, grad_time),
        (grad_xl, grad_time),
    )
    structure_tensor = jnp.stack(
        [
            cycle_box(left_part * right_part * cycle_mask, CIL, CXL)
            for left_part, right_part in factor_pairs
        ]
    )
    return (structure_tensor, adjoint_traces)


def solution(mesh):
    return jax.shard_map(
        local,
        mesh=mesh,
        in_specs=(
            P(("il", "xl"), None),
            P(),
            P(("il", "xl"), None, None),
            P(("il", "xl"), None, None, None),
            P(("il", "xl"), None),
        ),
        out_specs=(P(None, "il", "xl", None), P(("il", "xl"), None)),
        check_vma=False,
    )
```

profile of v0, /device:TPU:0, one launch (start us, length us, event | category | flops | bytes accessed | tf_op | source)
XLA Modules:
  0.0 588.4 jit_solution(13812488324231730556)
XLA Ops:
  1.5 1.7 bitcast_select_fusion.1
  3.2 7.3 %all-to-all-start = ((s32[32,7,128]{2,1,0:T(8,128)}), s32[32,7,128]{2,1,0:T(8,128)S(1)}, u32[]{:S(2)}, u32[]{:S(2)}) async-start(s32[32,7,128]{2,1,0:T(8,128)} %bitcast_select_fusion.1), calls=%async_computation | async-start | bytes 262144 | tf_op jit(solution)/shard_map/all_to_all | solution.py:68
  12.8 57.9 %gather_fusion = bf16[16384,12]{1,0:T(8,128)(2,1)} fusion(bf16[12,64]{0,1:T(8,128)(2,1)S(1)} %copy.41, s32[16384]{0:T(1024)S(1)} %fusion.45), kind=kCustom, calls=%fused_computation | custom fusion | bytes 851968 | tf_op jit(solution)/shard_map/gather | solution.py:30
  70.7 3.8 copy.42
  74.5 2.1 convert_bitcast_fusion
  76.6 2.8 copy.44
  79.7 8.3 %gather_fusion.1 = bf16[224,128,128]{2,1,0:T(8,128)(2,1)} fusion(bf16[60,128,128]{2,1,0:T(8,128)(2,1)S(1)} %bitcast.83, s32[1024]{0:T(1024)S(1)} %pad_clamp_fusion), kind=kCustom, calls=%fused_computation.1 | custom fusion | bytes 14680960 | tf_op jit(solution)/shard_map/jit(_take)/gather | solution.py:63
  88.0 6.8 %broadcast_select_fusion = bf16[32,7,128,128]{3,2,1,0:T(8,128)(2,1)} fusion(bf16[32,7,128,128]{3,2,1,0:T(8,128)(2,1)} %bitcast.82, pred[32,7]{1,0:T(8,128)(4,1)S(1)} %copy.40), kind=kLoop, calls=%fused_computation.25 | loop fusion | flops 3670016 | bytes 14680288 | tf_op jit(solution)/shard_map/jit(_take)/select_n | solution.py:63
  94.8 6.1 %all-to-all-start.1 = ((bf16[32,7,128,128]{3,2,1,0:T(8,128)(2,1)}), bf16[32,7,128,128]{3,2,1,0:T(8,128)(2,1)}, u32[]{:S(2)}, u32[]{:S(2)}) async-start(bf16[32,7,128,128]{3,2,1,0:T(8,128)(2,1)} %broadcast_select_fusion), calls=%async_computation.1 | async-start | bytes 14680064 | tf_op jit(solution)/shard_map/all_to_all | solution.py:67
  101.0 166.3 %all-to-all-done.1 = bf16[32,7,128,128]{3,2,1,0:T(8,128)(2,1)} async-done(((bf16[32,7,128,128]{3,2,1,0:T(8,128)(2,1)}), bf16[32,7,128,128]{3,2,1,0:T(8,128)(2,1)}, u32[]{:S(2)}, u32[]{:S(2)}) %all-to-all-start.1) | async-done | bytes 7340064 | tf_op jit(solution)/shard_map/all_to_all | solution.py:67
  267.3 69.8 %while.25 = (s32[]{:T(128)}, f32[1536,128]{1,0:T(8,128)S(1)}, f32[1536]{0:T(1024)S(1)}, s32[14,16,128]{2,1,0:T(8,128)S(1)}, bf16[14,16,128,128]{3,2,1,0:T(8,128)(2,1)}, /*index=5*/s32[]{:T(128)}, s32[]{:T(128)}) while((s32[]{:T(128)}, f32[1536,128]{1,0:T(8,128)S(1)}, f32[1536]{0:T(1024)S(1)}, s32[14,16,128]{2,1,0:T(8,128)S(1)}, ...), condition=%wide.region_2.3_spmd.clone, body=%wide.region_0.2_spmd.clone.sunk | while | flops 821429760 | bytes 3203168 | solution.py:91
  268.4 2.5 fusion.69
  270.9 1.3 convert_reduce_fusion.2
  273.4 2.5 fusion.69
  275.9 1.3 convert_reduce_fusion.2
  278.4 2.5 fusion.69
  280.9 1.3 convert_reduce_fusion.2
  283.4 2.5 fusion.69
  285.9 1.3 convert_reduce_fusion.2
  288.4 2.5 fusion.69
  290.9 1.3 convert_reduce_fusion.2
  293.4 2.5 fusion.69
  295.9 1.3 convert_reduce_fusion.2
  298.3 2.5 fusion.69
  300.9 1.3 convert_reduce_fusion.2
  303.3 2.5 fusion.69
  305.8 1.3 convert_reduce_fusion.2
  308.3 2.5 fusion.69
  310.8 1.3 convert_reduce_fusion.2
  313.3 2.5 fusion.69
  315.8 1.3 convert_reduce_fusion.2
  318.3 2.5 fusion.69
  320.8 1.3 convert_reduce_fusion.2
  323.3 2.5 fusion.69
  325.8 1.3 convert_reduce_fusion.2
  328.3 2.5 fusion.69
  330.8 1.3 convert_reduce_fusion.2
  333.2 2.5 fusion.69
  337.4 60.5 %while.24 = (s32[]{:T(128)}, bf16[14,16,128,128]{3,2,1,0:T(8,128)(2,1)}, s32[14,16,128]{2,1,0:T(8,128)S(1)}, bf16[1536,128]{1,0:T(8,128)(2,1)S(1)}, s32[]{:T(128)}) while((s32[]{:T(128)}, bf16[14,16,128,128]{3,2,1,0:T(8,128)(2,1)}, s32[14,16,128]{2,1,0:T(8,128)S(1)}, bf16[1536,128]{1,0:T(8,128)(2,1)S(1)}, s32[]{:T(128)}) %tuple.56), condition=%wide.region_4.5_spmd.clone, body=%wide.region_3.4_spmd.clone.sunk | while | flops 808714240 | bytes 1991233 | solution.py:109
  337.4 3.4 fusion.67
  341.7 3.4 fusion.67
  346.1 3.4 fusion.67
  350.4 3.4 fusion.67
  354.7 3.4 fusion.67
  359.1 3.4 fusion.67
  363.4 3.4 fusion.67
  367.7 3.4 fusion.67
  372.0 3.4 fusion.67
  376.3 3.4 fusion.67
  380.6 3.4 fusion.67
  384.9 3.4 fusion.67
  389.2 3.4 fusion.67
  393.6 3.4 fusion.67
  397.9 3.8 all-to-all-start.2
  402.1 2.0 collective-permute-start
  405.5 2.8 collective-permute-done.1
  408.3 3.4 collective-permute-start.2
  413.1 28.8 %collective-permute-done.2 = f32[36,2,128]{2,1,0:T(2,128)S(1)} collective-permute-done((f32[36,2,128]{2,1,0:T(2,128)S(1)}, f32[36,2,128]{2,1,0:T(2,128)S(1)}, u32[]{:S(2)}, u32[]{:S(2)}) %collective-permute-start.2) | collective-permute-done | bytes 36896 | tf_op jit(solution)/shard_map/ppermute | solution.py:15
  442.0 2.1 multiply_multiply_fusion
  451.9 116.5 %all-to-all-done.2 = bf16[32,7,128,128]{3,2,1,0:T(8,128)(2,1)} async-done(((bf16[32,7,128,128]{3,2,1,0:T(8,128)(2,1)}), bf16[32,7,128,128]{3,2,1,0:T(8,128)(2,1)}, u32[]{:S(2)}, u32[]{:S(2)}) %all-to-all-start.2) | async-done | bytes 7340064 | tf_op jit(solution)/shard_map/all_to_all | solution.py:112
  568.4 6.9 %select_select_fusion = (bf16[224,128,128]{2,1,0:T(8,128)(2,1)S(1)}, bf16[224,128,128]{2,1,0:T(8,128)(2,1)S(1)}) fusion(bf16[224,128,128]{2,1,0:T(8,128)(2,1)} %gather_fusion.1, pred[224]{0:T(512)(128)(4,1)S(1)} %compare_and_fusion.1, pred[224,128]{1,0:T(8,128)(4,1)S(1)} %select_compare_fusion, bf16[32,7,128,128]{3,2,1,0:T(8,128)(2,1)} %all-to-all-done.2), kind=kLoop, calls=%fused_computation.24 | loop fusion | flops 11010048 | bytes 29389024 | tf_op jit(solution)/shard_map/jit(_where)/select_n | solution.py:122
  575.3 4.4 fusion.11
  579.8 4.8 subtract_convert_fusion
  585.8 2.6 fusion.41
  (118 shorter events, 44.9 us)
Async XLA Ops:
  0.6 73.9 %copy-start = (bf16[7680,128]{1,0:T(8,128)(2,1)S(1)}, bf16[7680,128]{1,0:T(8,128)(2,1)}, u32[]{:S(2)}) copy-start(bf16[7680,128]{1,0:T(8,128)(2,1)} %param.9) | copy-start | bytes 5898244
  3.2 91.6 %all-to-all-start = ((s32[32,7,128]{2,1,0:T(8,128)}), s32[32,7,128]{2,1,0:T(8,128)S(1)}, u32[]{:S(2)}, u32[]{:S(2)}) async-start(s32[32,7,128]{2,1,0:T(8,128)} %bitcast_select_fusion.1), calls=%async_computation | async-start | bytes 262144 | tf_op jit(solution)/shard_map/all_to_all | solution.py:68
  94.8 172.5 %all-to-all-start.1 = ((bf16[32,7,128,128]{3,2,1,0:T(8,128)(2,1)}), bf16[32,7,128,128]{3,2,1,0:T(8,128)(2,1)}, u32[]{:S(2)}, u32[]{:S(2)}) async-start(bf16[32,7,128,128]{3,2,1,0:T(8,128)(2,1)} %broadcast_select_fusion), calls=%async_computation.1 | async-start | bytes 14680064 | tf_op jit(solution)/shard_map/all_to_all | solution.py:67
  397.9 3.9 copy-start.2
  397.9 170.5 %all-to-all-start.2 = ((bf16[32,7,128,128]{3,2,1,0:T(8,128)(2,1)}), bf16[32,7,128,128]{3,2,1,0:T(8,128)(2,1)}, u32[]{:S(2)}, u32[]{:S(2)}) async-start(bf16[32,7,128,128]{3,2,1,0:T(8,128)(2,1)} %bitcast.21), calls=%async_computation.2 | async-start | bytes 14680064 | tf_op jit(solution)/shard_map/all_to_all | solution.py:112
  402.1 3.4 collective-permute-start
  404.0 4.3 collective-permute-start.1
  408.3 33.6 %collective-permute-start.2 = (f32[36,2,128]{2,1,0:T(2,128)S(1)}, f32[36,2,128]{2,1,0:T(2,128)S(1)}, u32[]{:S(2)}, u32[]{:S(2)}) collective-permute-start(f32[36,2,128]{2,1,0:T(2,128)S(1)} %get-tuple-element.121), channel_id=1, source_target_pairs={{0,1},{1,2},{2,3},{3,4},{4,5},{5,6},{6,7},{8,9},{9,10},{10,11},{11... | collective-permute-start | bytes 110600 | tf_op jit(solution)/shard_map/ppermute | solution.py:15
  411.7 30.2 %collective-permute-start.3 = (f32[36,2,128]{2,1,0:T(2,128)S(1)}, f32[36,2,128]{2,1,0:T(2,128)S(1)}, u32[]{:S(2)}, u32[]{:S(2)}) collective-permute-start(f32[36,2,128]{2,1,0:T(2,128)S(1)} %get-tuple-element.122), channel_id=1, source_target_pairs={{1,0},{2,1},{3,2},{4,3},{5,4},{6,5},{7,6},{9,8},{10,9},{11,10},{12... | collective-permute-start | bytes 110600 | tf_op jit(solution)/shard_map/ppermute | solution.py:18
  579.8 8.7 %copy-start.1 = (bf16[7680,128]{1,0:T(8,128)(2,1)S(1)}, bf16[7680,128]{1,0:T(8,128)(2,1)}, u32[]{:S(2)}) copy-start(bf16[7680,128]{1,0:T(8,128)(2,1)} %param.9) | copy-start | bytes 5898244
where the time goes:
time: 594 us; the launch traced here: 588 us
  waiting for transfers between devices  314 us (53%)
  local copies, waits for them, and re-layouts  104 us (18%)
  matrix products  97.3 us (16%)
  other arithmetic  46 us (8%)
  starting transfers between devices  25.2 us (4%)
    all_to_all x1, waiting for transfers between devices, local(): lax.all_to_all(outgoing, ('il', 'xl'), split_axis=0, concat_axis=0, tiled...  166 us
    all_to_all x1, waiting for transfers between devices, local(): lax.all_to_all(answer.reshape(devices, capacity, row_block, samples), ('i...  117 us
    gather x2, local copies, waits for them, and re-layouts, filter_matrices(): picked = filter_taps[:, jnp.clip(lag_table, 0, tap_count - 1)]  61.7 us
    dot_general x14, matrix products, read_group(): lax.dot_general(selector, image_half, (((0,), (0,)), ((), ())), preferred...  48.2 us
    dot_general x14, matrix products, add_group(): jnp.dot(selector, group_blocks.reshape(-1, samples), preferred_element_ty...  35.2 us
    ppermute x2, waiting for transfers between devices, with_halo(): lax.ppermute(lax.slice_in_dim(block, block.shape[dim] - width, None, axis...  28.8 us
    reduce_sum x14, other arithmetic, add_group(): fold_counts = fold_counts + jnp.sum(selector, axis=1, dtype=jnp.float32)  18.5 us
    dynamic_slice x14, local copies, waits for them, and re-layouts, local(): lax.scan(scan_step, initial, (incoming.reshape(group_count, group_size, r...  15.2 us
  transfers between devices with their start and end apart: 7, of which 4 were waited for; matrix products, arithmetic and copies ran while one was open for 16% of the time, Pallas kernels for 0%

commit v1 on v0

--- a/solution.py
+++ b/solution.py
@@ -1,15 +1,301 @@
+import functools
+
 import jax
 import jax.numpy as jnp
 from jax import lax
+from jax.experimental import pallas as pl
+from jax.experimental.pallas import tpu as pltpu
+from jax.sharding import Mesh
 from jax.sharding import PartitionSpec as P
 
 CIL = 32
 CXL = 48
+CELLS = CIL * CXL
+HALF = CELLS // 2
+MIB = 1 << 20
+IN_SMEM = pl.BlockSpec(memory_space=pltpu.SMEM)
+IN_VMEM = pl.BlockSpec(memory_space=pltpu.VMEM)
+IN_ANY = pl.BlockSpec(memory_space=pl.ANY)
+
+
+def hot(cells, shape, axis):
+    line = lax.broadcasted_iota(jnp.int32, shape, axis)
+    return jnp.where(line == cells, 1.0, 0.0).astype(jnp.bfloat16)
+
+
+def lower(cells):
+    return jnp.where(cells >= HALF, cells - HALF, cells)
+
+
+def filter_kernel(taps, low_in, high_in, low_out, high_out, matrices):
+    step = pl.program_id(0)
+    samples = low_in.shape[2]
+    row = lax.broadcasted_iota(jnp.int32, (samples, samples), 0)
+    col = lax.broadcasted_iota(jnp.int32, (samples, samples), 1)
+    for part, (source, target) in enumerate(((low_in, low_out), (high_in, high_out))):
+        survey = step + part * pl.num_programs(0)
+        line = jnp.broadcast_to(taps[survey], (samples, samples))
+        band = pltpu.roll(line, 0, 1, stride=1, stride_axis=0)
+        matrix = jnp.where(col >= row, band, 0.0).astype(jnp.bfloat16)
+        matrices[part, 0] = matrix
+        target[0] = jnp.dot(source[0], matrix, preferred_element_type=jnp.float32).astype(
+            jnp.bfloat16
+        )
+
+
+def filter_call(traces, filter_taps):
+    surveys, tap_count = filter_taps.shape
+    samples = traces.shape[1]
+    rows = traces.shape[0] // surveys
+    steps = surveys // 2
+    by_survey = traces.reshape(surveys, rows, samples)
+    taps = jnp.pad(filter_taps, ((0, 0), (0, samples - tap_count))).reshape(surveys, 1, samples)
+    low, high, matrices = pl.pallas_call(
+        filter_kernel,
+        grid=(steps,),
+        in_specs=[
+            pl.BlockSpec((surveys, 1, samples), lambda i: (0, 0, 0)),
+            pl.BlockSpec((1, rows, samples), lambda i: (i, 0, 0)),
+            pl.BlockSpec((1, rows, samples), lambda i: (i + steps, 0, 0)),
+        ],
+        out_specs=[
+            pl.BlockSpec((1, rows, samples), lambda i: (i, 0, 0)),
+            pl.BlockSpec((1, rows, samples), lambda i: (i, 0, 0)),
+            pl.BlockSpec((2, 1, samples, samples), lambda i: (0, i, 0, 0)),
+        ],
+        out_shape=[
+            jax.ShapeDtypeStruct((steps, rows, samples), jnp.bfloat16),
+            jax.ShapeDtypeStruct((steps, rows, samples), jnp.bfloat16),
+            jax.ShapeDtypeStruct((2, steps, samples, samples), jnp.bfloat16),
+        ],
+        name="filter",
+    )(taps, by_survey, by_survey)
+    return (
+        low.reshape(steps * rows, samples),
+        high.reshape(steps * rows, samples),
+        matrices.reshape(surveys, samples, samples),
+    )
+
+
+def stack_kernel(sources, tiles, block_rows, first, order, counts, blocks, cells, *refs):
+    group = 8
+    pieces = refs[: 2 * sources]
+    refs = refs[2 * sources :]
+    if first:
+        out, held, live, sems = refs
+    else:
+        before, out, held, live, sems = refs
+    rows = pieces[0].shape[0]
+    copies = [
+        pltpu.make_async_copy(piece, held.at[pl.ds(i * rows, rows)], sems.at[i])
+        for i, piece in enumerate(pieces)
+    ]
+    for copy in copies:
+        copy.start()
+    out[...] = jnp.zeros_like(out) if first else before[...]
+    for copy in copies:
+        copy.wait()
+
+    def tile_step(tile, unused):
+        def add_source(source, n):
+            base = order[source] * tiles + tile
+
+            def add_slot(c, n):
+                live[n] = base * 8 + c
+                live[n + 256] = blocks[base * 8 + c] * block_rows + source * (2 * rows)
+                return n + 1
+
+            return lax.fori_loop(0, counts[base], add_slot, n)
+
+        n = lax.fori_loop(0, sources, add_source, 0)
+
+        def one_group(g, unused):
+            picked = []
+            for i in range(group):
+                at = g * group + i
+                entry = live[jnp.minimum(at, n - 1)]
+                picked.append(jnp.where(at < n, cells[pl.ds(entry, 1), :], -1))
+            columns = jnp.concatenate(picked, axis=0).T
+            data = []
+            for i in range(group):
+                start = live[256 + jnp.minimum(g * group + i, n - 1)]
+                block = held[pl.ds(pl.multiple_of(start, block_rows), block_rows), :]
+                upper = columns[:, i : i + 1] >= HALF
+                zero = jnp.zeros_like(block)
+                data.append(
+                    jnp.concatenate(
+                        [jnp.where(upper, zero, block), jnp.where(upper, block, zero)], axis=1
+                    )
+                )
+            data = jnp.concatenate(data, axis=0)
+            line = jnp.concatenate(picked, axis=1)
+            width = line.shape[1]
+            selector = hot(lower(line), (HALF, width), 0)
+            out[tile, :HALF] += jnp.dot(selector, data, preferred_element_type=jnp.float32)
+            inline = ((line >> 4) * 171) >> 9
+            cross = line - CXL * inline
+            out[tile, HALF:, :128] += lax.dot_general(
+                hot(cross, (CXL, width), 0),
+                hot(inline, (128, width), 0),
+                (((1,), (1,)), ((), ())),
+                preferred_element_type=jnp.float32,
+            )
+            return 0
+
+        lax.fori_loop(0, (n + group - 1) // group, one_group, 0)
+        return 0
+
+    lax.fori_loop(0, tiles, tile_step, 0)
+
+
+def stack_call(order, counts, blocks, cells, pieces, before, tiles, block_rows):
+    sources = len(pieces) // 2
+    first = before is None
+    rows = pieces[0].shape[0]
+    extra = [] if first else [before]
+    return pl.pallas_call(
+        functools.partial(stack_kernel, sources, tiles, block_rows, first),
+        out_shape=jax.ShapeDtypeStruct((tiles, HALF + CXL, 256), jnp.float32),
+        in_specs=[IN_SMEM] * 3 + [IN_VMEM] + [IN_ANY] * len(pieces) + [IN_VMEM] * len(extra),
+        out_specs=IN_VMEM,
+        scratch_shapes=[
+            pltpu.VMEM((sources * 2 * rows, 128), jnp.bfloat16),
+            pltpu.SMEM((512,), jnp.int32),
+            pltpu.SemaphoreType.DMA((len(pieces),)),
+        ],
+        compiler_params=pltpu.CompilerParams(vmem_limit_bytes=40 * MIB),
+        cost_estimate=pl.CostEstimate(
+            flops=sources * tiles * 7 * 2 * HALF * 128 * 256,
+            bytes_accessed=len(pieces) * rows * 256 + 8 * MIB,
+            transcendentals=0,
+        ),
+        name="stack",
+    )(order, counts, blocks, cells, *pieces, *extra)
+
+
+def image_kernel(stack, image, packed):
+    for a in range(CIL):
+        fold = jnp.maximum(stack[HALF:, a : a + 1], 1.0)
+        side = a // (CIL // 2)
+        low = (a - side * (CIL // 2)) * CXL
+        value = stack[low : low + CXL, side * 128 : side * 128 + 128] / fold
+        image[a * CXL : (a + 1) * CXL] = value
+        packed[low : low + CXL, side * 128 : side * 128 + 128] = value.astype(jnp.bfloat16)
+
+
+def image_call(stack):
+    return pl.pallas_call(
+        image_kernel,
+        out_shape=[
+            jax.ShapeDtypeStruct((CELLS, 128), jnp.float32),
+            jax.ShapeDtypeStruct((HALF, 256), jnp.bfloat16),
+        ],
+        in_specs=[IN_VMEM],
+        out_specs=[IN_VMEM, IN_VMEM],
+        name="image",
+    )(stack)
+
+
+def read_kernel(tiles, block_rows, first, order, counts, blocks, cells, low, high, *refs):
+    group = 4
+    images = refs[:tiles]
+    refs = refs[tiles:]
+    if first:
+        out, held, own, sems = refs
+    else:
+        before, out, held, own, sems = refs
+    rows = low.shape[0]
+    copies = [
+        pltpu.make_async_copy(image, held.at[i], sems.at[i]) for i, image in enumerate(images)
+    ]
+    copies += [
+        pltpu.make_async_copy(part, own.at[pl.ds(i * rows, rows)], sems.at[tiles + i])
+        for i, part in enumerate((low, high))
+    ]
+    for copy in copies:
+        copy.start()
+    out[...] = jnp.zeros_like(out) if first else before[...]
+    for copy in copies:
+        copy.wait()
+
+    def tile_step(j, unused):
+        tile = order[j]
+        n = counts[tile]
+        columns = cells[pl.ds(pl.multiple_of(tile * 8, 8), 8), :].T
+        for g in range(8 // group):
+
+            @pl.when(n > g * group)
+            def _():
+                picks = [columns[:, g * group + i : g * group + i + 1] for i in range(group)]
+                selector = jnp.concatenate(
+                    [hot(lower(pick), (block_rows, HALF), 1) for pick in picks], axis=0
+                )
+                got = jnp.dot(selector, held[j], preferred_element_type=jnp.float32)
+                for i, pick in enumerate(picks):
+                    start = blocks[tile * 8 + g * group + i] * block_rows
+                    here = pl.ds(pl.multiple_of(start, block_rows), block_rows)
+                    part = got[i * block_rows : (i + 1) * block_rows]
+                    value = jnp.where(pick >= HALF, part[:, 128:], part[:, :128])
+                    mine = own[here, :].astype(jnp.float32)
+                    out[here, :] += jnp.where(pick >= 0, mine, 0.0) - value
+
+        return 0
+
+    lax.fori_loop(0, tiles, tile_step, 0)
+
+
+def read_call(order, counts, blocks, cells, low, high, images, before, block_rows):
+    tiles = len(images)
+    first = before is None
+    rows = low.shape[0]
+    extra = [] if first else [before]
+    return pl.pallas_call(
+        functools.partial(read_kernel, tiles, block_rows, first),
+        out_shape=jax.ShapeDtypeStruct((2 * rows, 128), jnp.float32),
+        in_specs=[IN_SMEM] * 3 + [IN_VMEM] + [IN_ANY] * (2 + tiles) + [IN_VMEM] * len(extra),
+        out_specs=IN_VMEM,
+        scratch_shapes=[
+            pltpu.VMEM((tiles, HALF, 256), jnp.bfloat16),
+            pltpu.VMEM((2 * rows, 128), jnp.bfloat16),
+            pltpu.SemaphoreType.DMA((tiles + 2,)),
+        ],
+        compiler_params=pltpu.CompilerParams(vmem_limit_bytes=40 * MIB),
+        cost_estimate=pl.CostEstimate(
+            flops=tiles * 7 * 2 * HALF * 128 * 256,
+            bytes_accessed=16 * MIB,
+            transcendentals=0,
+        ),
+        name="read",
+    )(order, counts, blocks, cells, low, high, *images, *extra)
+
+
+def adjoint_kernel(residual, matrix, out):
+    out[0] = lax.dot_general(
+        residual[0].astype(jnp.bfloat16),
+        matrix[0],
+        (((1,), (1,)), ((), ())),
+        preferred_element_type=jnp.float32,
+    )
+
+
+def adjoint_call(residual, matrices):
+    surveys, samples, unused = matrices.shape
+    rows = residual.shape[0] // surveys
+    return pl.pallas_call(
+        adjoint_kernel,
+        grid=(surveys,),
+        in_specs=[
+            pl.BlockSpec((1, rows, samples), lambda i: (i, 0, 0)),
+            pl.BlockSpec((1, samples, samples), lambda i: (i, 0, 0)),
+        ],
+        out_specs=pl.BlockSpec((1, rows, samples), lambda i: (i, 0, 0)),
+        out_shape=jax.ShapeDtypeStruct((surveys, rows, samples), jnp.float32),
+        name="adjoint",
+    )(residual.reshape(surveys, rows, samples), matrices).reshape(residual.shape)
 
 
 def with_halo(block, sides, width):
-    for axis, dim in sides:
-        count = lax.axis_size(axis)
+    for axis, count, dim in sides:
         forward = [(i, i + 1) for i in range(count - 1)]
         backward = [(target, source) for source, target in forward]
         low = lax.ppermute(
@@ -18,17 +304,6 @@
         high = lax.ppermute(lax.slice_in_dim(block, 0, width, axis=dim), axis, backward)
         block = jnp.concatenate([low, block, high], axis=dim)
     return block
-
-
-def filter_matrices(filter_taps, samples):
-    lag_table = (
-        jnp.arange(samples, dtype=jnp.int32)[None, :]
-        - jnp.arange(samples, dtype=jnp.int32)[:, None]
-    )
-    tap_count = filter_taps.shape[1]
-    inside = (lag_table >= 0) & (lag_table < tap_count)
-    picked = filter_taps[:, jnp.clip(lag_table, 0, tap_count - 1)]
-    return jnp.where(inside[None], picked, 0.0).astype(jnp.bfloat16)
 
 
 def cycle_box(values, rows_out, cols_out):
@@ -40,6 +315,134 @@
                 + values[row_shift : row_shift + rows_out, col_shift : col_shift + cols_out]
             )
     return box_total / 9.0
+
+
+def tensor(tile_image, il, xl):
+    axis_il, count_il, at_il = il
+    axis_xl, count_xl, at_xl = xl
+    padded = with_halo(tile_image, ((axis_il, count_il, 0), (axis_xl, count_xl, 1)), 2)
+    padded_time = jnp.pad(padded, ((0, 0), (0, 0), (1, 1)))
+    grad_il = (padded[2:, 1:-1] - padded[:-2, 1:-1]) * 0.5
+    grad_xl = (padded[1:-1, 2:] - padded[1:-1, :-2]) * 0.5
+    grad_time = (padded_time[1:-1, 1:-1, 2:] - padded_time[1:-1, 1:-1, :-2]) * 0.5
+    rows_il = at_il * CIL + jnp.arange(CIL + 2, dtype=jnp.int32) - 1
+    rows_xl = at_xl * CXL + jnp.arange(CXL + 2, dtype=jnp.int32) - 1
+    inside_il = ((rows_il >= 0) & (rows_il < CIL * count_il)).astype(jnp.float32)
+    inside_xl = ((rows_xl >= 0) & (rows_xl < CXL * count_xl)).astype(jnp.float32)
+    cycle_mask = inside_il[:, None, None] * inside_xl[None, :, None]
+    factor_pairs = (
+        (grad_il, grad_il),
+        (grad_xl, grad_xl),
+        (grad_time, grad_time),
+        (grad_il, grad_xl),
+        (grad_il, grad_time),
+        (grad_xl, grad_time),
+    )
+    return jnp.stack(
+        [
+            cycle_box(left_part * right_part * cycle_mask, CIL, CXL)
+            for left_part, right_part in factor_pairs
+        ]
+    )
+
+
+SWAP = [(0, 1), (1, 0)]
+
+
+def over(axis, value):
+    return lax.ppermute(value, axis, SWAP)
+
+
+def along_z(value, step):
+    return lax.ppermute(value, "z", [(i, (i + step) % 4) for i in range(4)])
+
+
+def local_planes(traces, filter_taps, slot_block, slot_cells, pair_count):
+    row_block = slot_cells.shape[3]
+    capacity = slot_block.shape[2]
+    x, core, z, y = (lax.axis_index(name) for name in ("x", "c", "z", "y"))
+
+    def place(at_x, at_core, at_z, at_y):
+        return ((at_x * 2 + at_core) * 4 + at_z) * 2 + at_y
+
+    low, high, matrices = filter_call(traces, filter_taps)
+
+    slot_live = jnp.arange(capacity, dtype=jnp.int32)[None, :] < pair_count[0][:, None]
+    out_cells = jnp.where(slot_live[:, :, None], slot_cells[0], -1)
+    numbers = jnp.concatenate([slot_block[0], pair_count[0][:, None]], axis=1)
+    numbers = jnp.pad(numbers, ((0, 0), (0, row_block - 8)))
+    slots = jnp.concatenate([out_cells, numbers[:, None, :]], axis=1)
+    by_column = slots.reshape(2, 2, 4, 2, 8, row_block).transpose(0, 1, 3, 2, 4, 5)
+    arrived = lax.all_to_all(
+        by_column.reshape(8, 4, 8, row_block), ("x", "c", "y"), 0, 0, tiled=True
+    )
+    in_cells = arrived.reshape(256, row_block)
+    in_numbers = arrived[:, :, 7, :8].reshape(32, 8)
+    in_counts = in_numbers[:, 7]
+    in_blocks = in_numbers.reshape(256)
+
+    x0, y1 = over("x", low), over("y", high)
+    x1, y0 = over("x", high), over("y", low)
+    d0, d1 = over("y", x0), over("x", y1)
+
+    def column(*sources):
+        return jnp.stack([(at_x * 2 + at_core) * 2 + at_y for at_x, at_core, at_y in sources])
+
+    other = 1 - core
+    stack = None
+    for pieces, spots in (
+        (([low, high],), ((x, y),)),
+        (([x0, x1], [y0, y1]), ((1 - x, y), (x, 1 - y))),
+        (([d0, d1],), ((1 - x, 1 - y),)),
+    ):
+        operands, sources = [], []
+        for pair, (at_x, at_y) in zip(pieces, spots, strict=True):
+            operands += pair + [over("c", part) for part in pair]
+            sources += [(at_x, core, at_y), (at_x, other, at_y)]
+        stack = stack_call(
+            column(*sources), in_counts, in_blocks, in_cells, operands, stack, 4, row_block
+        )
+    total = lax.psum_scatter(stack, "z", scatter_dimension=0, tiled=True)[0]
+    image, packed = image_call(total)
+
+    structure_tensor = tensor(
+        image.reshape(CIL, CXL, 128),
+        (("x", "c"), 4, x * 2 + core),
+        (("z", "y"), 8, z * 2 + y),
+    )
+
+    own_counts = pair_count[0]
+    own_blocks = numbers[:, :8].reshape(256)
+    own_cells = jnp.pad(out_cells, ((0, 0), (0, 1), (0, 0)), constant_values=-1)
+    own_cells = own_cells.reshape(256, row_block)
+    residual = None
+    layers = [(packed, 0)] + [(along_z(packed, step), step) for step in (1, 3, 2)]
+    for turn, (layer, step) in enumerate(layers):
+        from_x, from_y = over("x", layer), over("y", layer)
+        diagonal = over("y", from_x) if turn % 2 == 0 else over("x", from_y)
+        mine = [layer, from_x, from_y, diagonal]
+        spots = [(x, y), (1 - x, y), (x, 1 - y), (1 - x, 1 - y)]
+        images = mine + [over("c", part) for part in mine]
+        at_z = lax.rem(z + 4 - step, 4)
+        order = jnp.stack(
+            [place(at_x, core, at_z, at_y) for at_x, at_y in spots]
+            + [place(at_x, other, at_z, at_y) for at_x, at_y in spots]
+        )
+        residual = read_call(
+            order, own_counts, own_blocks, own_cells, low, high, images, residual, row_block
+        )
+    return (structure_tensor, adjoint_call(residual, matrices))
+
+
+def filter_matrices(filter_taps, samples):
+    lag_table = (
+        jnp.arange(samples, dtype=jnp.int32)[None, :]
+        - jnp.arange(samples, dtype=jnp.int32)[:, None]
+    )
+    tap_count = filter_taps.shape[1]
+    inside = (lag_table >= 0) & (lag_table < tap_count)
+    picked = filter_taps[:, jnp.clip(lag_table, 0, tap_count - 1)]
+    return jnp.where(inside[None], picked, 0.0).astype(jnp.bfloat16)
 
 
 def local(traces, filter_taps, slot_block, slot_cells, pair_count):
@@ -134,45 +537,31 @@
     adjoint_traces = jnp.einsum(
         "srt,sut->sru", residual_half, matrices, preferred_element_type=jnp.float32
     ).reshape(traces.shape)
-    tile_image = stack_image.reshape(CIL, CXL, samples)
-    padded = with_halo(tile_image, (("il", 0), ("xl", 1)), 2)
-    padded_time = jnp.pad(padded, ((0, 0), (0, 0), (1, 1)))
-    grad_il = (padded[2:, 1:-1] - padded[:-2, 1:-1]) * 0.5
-    grad_xl = (padded[1:-1, 2:] - padded[1:-1, :-2]) * 0.5
-    grad_time = (padded_time[1:-1, 1:-1, 2:] - padded_time[1:-1, 1:-1, :-2]) * 0.5
-    rows_il = lax.axis_index("il") * CIL + jnp.arange(CIL + 2, dtype=jnp.int32) - 1
-    rows_xl = lax.axis_index("xl") * CXL + jnp.arange(CXL + 2, dtype=jnp.int32) - 1
-    inside_il = ((rows_il >= 0) & (rows_il < CIL * count_il)).astype(jnp.float32)
-    inside_xl = ((rows_xl >= 0) & (rows_xl < CXL * count_xl)).astype(jnp.float32)
-    cycle_mask = inside_il[:, None, None] * inside_xl[None, :, None]
-    factor_pairs = (
-        (grad_il, grad_il),
-        (grad_xl, grad_xl),
-        (grad_time, grad_time),
-        (grad_il, grad_xl),
-        (grad_il, grad_time),
-        (grad_xl, grad_time),
-    )
-    structure_tensor = jnp.stack(
-        [
-            cycle_box(left_part * right_part * cycle_mask, CIL, CXL)
-            for left_part, right_part in factor_pairs
-        ]
+    structure_tensor = tensor(
+        stack_image.reshape(CIL, CXL, samples),
+        ("il", count_il, lax.axis_index("il")),
+        ("xl", count_xl, lax.axis_index("xl")),
     )
     return (structure_tensor, adjoint_traces)
 
 
 def solution(mesh):
+    inner, names, body = mesh, (("il",), ("xl",)), local
+    if mesh.devices.shape == (4, 8):
+        inner = Mesh(mesh.devices.reshape(2, 2, 4, 2), ("x", "c", "z", "y"))
+        names, body = (("x", "c"), ("z", "y")), local_planes
+    il, xl = names
+    both = il + xl
     return jax.shard_map(
-        local,
-        mesh=mesh,
+        body,
+        mesh=inner,
         in_specs=(
-            P(("il", "xl"), None),
+            P(both, None),
             P(),
-            P(("il", "xl"), None, None),
-            P(("il", "xl"), None, None, None),
-            P(("il", "xl"), None),
+            P(both, None, None),
+            P(both, None, None, None),
+            P(both, None),
         ),
-        out_specs=(P(None, "il", "xl", None), P(("il", "xl"), None)),
+        out_specs=(P(None, il, xl, None), P(both, None)),
         check_vma=False,
     )

time: 594 us -> 340 us (0.57)
  waiting for transfers between devices: 314 us -> 169 us
  matrix products: 97.3 us -> 0 us
  local copies, waits for them, and re-layouts: 104 us -> 15.7 us
  Pallas kernels: 0 us -> 77.5 us
  other arithmetic: 46 us -> 12.1 us
  starting transfers between devices: 25.2 us -> 47 us
  between operations: 0.94 us -> 14.6 us
    all_to_all x3 -> x1, waiting for transfers between devices: 283 us -> 0.62 us  [local_planes(): lax.all_to_all(by_column.reshape(8, 4, 8, row_block), ('x', 'c', 'y'), 0,...]
    dot_general x32 -> x0, matrix products: 97.3 us -> none  [the longest x14 48.2 us: read_group(): lax.dot_general(selector, image_half, (((0,), (0,)), ((), ())), preferred...]
    ppermute x0 -> x45, waiting for transfers between devices: none -> 95.4 us  [the longest x42 71.4 us: over(): return lax.ppermute(value, axis, SWAP)]
    pallas_call x0 -> x10, Pallas kernels: none -> 77.5 us  [the longest x4 31.5 us: read_call(): pl.pallas_call(functools.partial(read_kernel, tiles, block_rows, first),...]
    reduce_scatter x0 -> x1, waiting for transfers between devices: none -> 70.1 us  [local_planes(): total = lax.psum_scatter(stack, 'z', scatter_dimension=0, tiled=True)[0]]
    gather x3 -> x0, local copies, waits for them, and re-layouts: 70 us -> none  [the longest x2 61.7 us: filter_matrices(): picked = filter_taps[:, jnp.clip(lag_table, 0, tap_count - 1)]]
    ppermute x0 -> x45, starting transfers between devices: none -> 37.2 us  [the longest x42 30.2 us: over(): return lax.ppermute(value, axis, SWAP)]
    ppermute x2, waiting for transfers between devices: 28.8 us -> 0.01 us  [with_halo(): lax.ppermute(lax.slice_in_dim(block, block.shape[dim] - width, None, axis...]
  transfers between devices with their start and end apart: 7 -> 51, of which waited for: 4 -> 16; matrix products, arithmetic and copies ran while one was open for 16% -> 5% of each run, Pallas kernels for 0% -> 13%
where the time goes in v1:
time: 340 us; the launch traced here: 336 us
  waiting for transfers between devices  169 us (50%)
  Pallas kernels  77.5 us (23%)
  starting transfers between devices  47 us (14%)
  local copies, waits for them, and re-layouts  15.7 us (5%)
  between operations  14.6 us (4%)
  other arithmetic  12.1 us (4%)
    ppermute x42, waiting for transfers between devices, over(): return lax.ppermute(value, axis, SWAP)  71.4 us
    reduce_scatter x1, waiting for transfers between devices, local_planes(): total = lax.psum_scatter(stack, 'z', scatter_dimension=0, tiled=True)[0]  70.1 us
    pallas_call x4, Pallas kernels, read_call(): pl.pallas_call(functools.partial(read_kernel, tiles, block_rows, first),...  31.5 us
    ppermute x42, starting transfers between devices, over(): return lax.ppermute(value, axis, SWAP)  30.2 us
    pallas_call x3, Pallas kernels, stack_call(): pl.pallas_call(functools.partial(stack_kernel, sources, tiles, block_rows...  28.7 us
    ppermute x3, waiting for transfers between devices, along_z(): return lax.ppermute(value, 'z', [(i, (i + step) % 4) for i in range(4)])  23.9 us
    unnamed x37, local copies, waits for them, and re-layouts  12.6 us
    pallas_call x1, Pallas kernels, adjoint_call(): pl.pallas_call(adjoint_kernel, grid=(surveys,), in_specs=[pl.BlockSpec((1...  9.18 us
  transfers between devices with their start and end apart: 51, of which 16 were waited for; matrix products, arithmetic and copies ran while one was open for 5% of the time, Pallas kernels for 13%

profile of v1, /device:TPU:0, one launch (start us, length us, event | category | flops | bytes accessed | tf_op | source)
XLA Modules:
  0.0 335.5 jit_solution(14290647924856807607)
XLA Ops:
  8.5 5.6 %filter.1 = (bf16[6,640,128]{2,1,0:T(8,128)(2,1)}, bf16[6,640,128]{2,1,0:T(8,128)(2,1)}, bf16[2,6,128,128]{3,2,1,0:T(8,128)(2,1)}) custom-call(f32[12,1,128]{2,1,0:T(1,128)} %reshape.132.taps, bf16[12,640,128]{2,1,0:T(8,128)(2,1)} %bitcast.122, bf16[12,640,128]{2,1,0:T(8,128)(2,1)} %bitcast.123), custom_call_target="tpu_custom_call" | custom-call | tf_op jit(solution)/shard_map/filter/pallas_call | solution.py:53
  14.6 2.6 collective-permute-start.2
  17.1 1.5 collective-permute-start
  19.1 0.9 copy-done.6
  20.8 19.3 %collective-permute-done.2.refs_5_ = bf16[3840,128]{1,0:T(8,128)(2,1)} collective-permute-done((bf16[3840,128]{1,0:T(8,128)(2,1)}, bf16[3840,128]{1,0:T(8,128)(2,1)}, u32[]{:S(2)}, u32[]{:S(2)}) %collective-permute-start.2) | collective-permute-done | bytes 983072 | tf_op jit(solution)/shard_map/ppermute | solution.py:353
  40.1 2.0 collective-permute-done.refs_0_
  42.1 1.0 copy-done.8
  43.1 1.9 collective-permute-start.3
  47.0 1.3 reduce.5
  48.5 12.6 %collective-permute-done.9.refs_4_ = bf16[3840,128]{1,0:T(8,128)(2,1)} collective-permute-done((bf16[3840,128]{1,0:T(8,128)(2,1)}, bf16[3840,128]{1,0:T(8,128)(2,1)}, u32[]{:S(2)}, u32[]{:S(2)}) %collective-permute-start.9) | collective-permute-done | bytes 983072 | tf_op jit(solution)/shard_map/ppermute | solution.py:353
  61.1 2.0 collective-permute-done.6.refs_1_
  63.1 0.9 copy-done.10
  64.6 1.0 copy_select_fusion
  66.3 3.4 %all-to-all-start = ((s32[8,4,8,128]{3,1,2,0:T(4,128)}), s32[8,4,8,128]{3,1,2,0:T(4,128)S(1)}, u32[]{:S(2)}, u32[]{:S(2)}) async-start(s32[8,4,8,128]{3,1,2,0:T(4,128)} %bitcast.6), calls=%async_computation | async-start | bytes 262144 | tf_op jit(solution)/shard_map/all_to_all | solution.py:376
  69.9 12.2 %collective-permute-done.1.refs_0_ = bf16[3840,128]{1,0:T(8,128)(2,1)S(1)} collective-permute-done((bf16[3840,128]{1,0:T(8,128)(2,1)}, bf16[3840,128]{1,0:T(8,128)(2,1)S(1)}, u32[]{:S(2)}, u32[]{:S(2)}) %collective-permute-start.1) | collective-permute-done | bytes 983072 | tf_op jit(solution)/shard_map/ppermute | solution.py:353
  82.1 1.9 collective-permute-done.3.refs_1_
  85.0 1.2 copy-done.1
  86.2 1.2 copy-done.3
  87.4 1.2 copy-done.7
  88.6 1.2 copy-done.9
  89.8 6.0 %stack.219.refs_8_ = f32[4,816,256]{2,1,0:T(8,128)S(1)} custom-call(s32[2]{0:T(128)S(1)} %pad_add_fusion.4.order, s32[32]{0:T(128)S(1)} %slice_reduce_fusion.counts, s32[256]{0:T(256)S(1)} %reshape_reshape_squeeze.3.blocks, s32[256,128]{1,0:T(8,128)S(1)} %bitcast.109, bf16[3840,128]{1,0:T(8,128)(2,1)S(1)} %bitcast.96, bf16[3840,128]{1,0:T(8,128)(2,1)S(1)} %bitcast.104, ...), custom_call_target="tpu_custom_call" | custom-call | flops 2818572288 | bytes 12320768 | tf_op jit(solution)/shard_map/stack/pallas_call | solution.py:156
  95.8 1.7 copy-done.13
  97.6 13.6 %stack.220.refs_4_ = f32[4,816,256]{2,1,0:T(8,128)S(1)} custom-call(s32[4]{0:T(128)S(1)} %pad_add_fusion.3.order, s32[32]{0:T(128)S(1)} %slice_reduce_fusion.counts, s32[256]{0:T(256)S(1)} %reshape_reshape_squeeze.3.blocks, s32[256,128]{1,0:T(8,128)S(1)} %bitcast.110, bf16[3840,128]{1,0:T(8,128)(2,1)} %collective-permute-done.refs_0_, ...), custom_call_target="tpu_custom_call" | custom-call | flops 5637144576 | bytes 16252928 | tf_op jit(solution)/shard_map/stack/pallas_call | solution.py:156
  111.2 9.2 %stack.221 = f32[4,816,256]{2,1,0:T(8,128)} custom-call(s32[2]{0:T(128)S(1)} %pad_add_fusion.2.order, s32[32]{0:T(128)S(1)} %slice_reduce_fusion.counts, s32[256]{0:T(256)S(1)} %reshape_reshape_squeeze.3.blocks, s32[256,128]{1,0:T(8,128)S(1)} %bitcast.111, bf16[3840,128]{1,0:T(8,128)(2,1)S(1)} %collective-permute-done.1.refs_0_, ...), custom_call_target="tpu_custom_call" | custom-call | flops 2818572288 | bytes 12320768 | tf_op jit(solution)/shard_map/stack/pallas_call | solution.py:156
  120.6 70.1 %reduce-scatter.2.cloned.1.call-done = f32[1,816,256]{2,1,0:T(8,128)} async-done(((f32[4,816,256]{2,1,0:T(8,128)}), f32[1,816,256]{2,1,0:T(8,128)}) %reduce-scatter.2.cloned.1.call-update) | async-done | bytes 835600 | tf_op jit(solution)/shard_map/reduce_scatter | solution.py:405
  190.7 2.5 image.1
  193.1 1.4 collective-permute-start.42
  194.6 1.5 collective-permute-start.43
  196.1 0.8 fusion.23
  196.9 1.3 collective-permute-start.14
  198.2 1.3 collective-permute-start.15
  199.7 2.4 collective-permute-done.15
  202.1 1.0 pad_maximum_fusion.9
  203.1 2.5 collective-permute-start.16
  205.6 1.3 collective-permute-start.17
  207.4 3.2 collective-permute-start.45
  210.7 3.4 %collective-permute-start.34 = (bf16[768,256]{1,0:T(8,128)(2,1)}, bf16[768,256]{1,0:T(8,128)(2,1)S(1)}, u32[]{:S(2)}, u32[]{:S(2)}) collective-permute-start(bf16[768,256]{1,0:T(8,128)(2,1)} %get-tuple-element.10.refs_0_), channel_id=1, source_target_pairs={{0,2},{2,4},{4,6},{6,0},{1,3},{3,5},{5,7},{7,1},{8,10},{10,12},{12... | collective-permute-start | bytes 1179656 | tf_op jit(solution)/shard_map/ppermute | solution.py:357
  214.1 1.6 collective-permute-start.26
  215.7 1.2 pad_maximum_fusion
  216.9 2.0 collective-permute-start.18
  219.2 3.3 multiply_multiply_fusion
  222.5 0.9 collective-permute-start.46
  223.4 2.2 collective-permute-done.34.refs_0_
  225.6 1.5 collective-permute-start.36
  227.0 6.4 %collective-permute-done.26.refs_0_ = bf16[768,256]{1,0:T(8,128)(2,1)S(1)} collective-permute-done((bf16[768,256]{1,0:T(8,128)(2,1)}, bf16[768,256]{1,0:T(8,128)(2,1)S(1)}, u32[]{:S(2)}, u32[]{:S(2)}) %collective-permute-start.26) | collective-permute-done | bytes 393248 | tf_op jit(solution)/shard_map/ppermute | solution.py:357
  233.4 1.5 collective-permute-start.35
  234.9 15.3 %collective-permute-done.18.refs_0_ = bf16[768,256]{1,0:T(8,128)(2,1)S(1)} collective-permute-done((bf16[768,256]{1,0:T(8,128)(2,1)}, bf16[768,256]{1,0:T(8,128)(2,1)S(1)}, u32[]{:S(2)}, u32[]{:S(2)}) %collective-permute-start.18) | collective-permute-done | bytes 393248 | tf_op jit(solution)/shard_map/ppermute | solution.py:357
  251.7 1.6 collective-permute-start.27
  253.3 1.2 collective-permute-start.28
  254.5 0.9 collective-permute-start.20
  256.6 7.1 %collective-permute-done.27.refs_1_ = bf16[768,256]{1,0:T(8,128)(2,1)S(1)} collective-permute-done((bf16[768,256]{1,0:T(8,128)(2,1)S(1)}, bf16[768,256]{1,0:T(8,128)(2,1)S(1)}, u32[]{:S(2)}, u32[]{:S(2)}) %collective-permute-start.27) | collective-permute-done | bytes 393248 | tf_op jit(solution)/shard_map/ppermute | solution.py:353
  263.7 1.5 collective-permute-start.37
  265.8 6.7 %collective-permute-done.20.refs_2_ = bf16[768,256]{1,0:T(8,128)(2,1)S(1)} collective-permute-done((bf16[768,256]{1,0:T(8,128)(2,1)S(1)}, bf16[768,256]{1,0:T(8,128)(2,1)S(1)}, u32[]{:S(2)}, u32[]{:S(2)}) %collective-permute-start.20) | collective-permute-done | bytes 393248 | tf_op jit(solution)/shard_map/ppermute | solution.py:353
  272.8 1.2 collective-permute-start.29
  274.7 4.9 %collective-permute-done.37.refs_3_ = bf16[768,256]{1,0:T(8,128)(2,1)S(1)} collective-permute-done((bf16[768,256]{1,0:T(8,128)(2,1)S(1)}, bf16[768,256]{1,0:T(8,128)(2,1)S(1)}, u32[]{:S(2)}, u32[]{:S(2)}) %collective-permute-start.37) | collective-permute-done | bytes 393248 | tf_op jit(solution)/shard_map/ppermute | solution.py:353
  279.6 1.5 collective-permute-start.21
  281.8 2.7 collective-permute-done.29.refs_3_
  284.4 8.1 %read.4.refs_8_ = f32[7680,128]{1,0:T(8,128)S(1)} custom-call(s32[8]{0:T(128)S(1)} %stack.218.order, s32[32]{0:T(128)S(1)} %bitcast.114, s32[256]{0:T(256)S(1)} %reshape.137.blocks, s32[256,128]{1,0:T(8,128)S(1)} %pad_bitcast_fusion.cells, bf16[3840,128]{1,0:T(8,128)(2,1)S(1)} %bitcast.97, bf16[3840,128]{1,0:T(8,128)(2,1)S(1)} %bitcast.105, ...), custom_call_target="tpu_custom_call" | custom-call | flops 2818572288 | bytes 16777216 | tf_op jit(solution)/shard_map/read/pallas_call | solution.py:252
  292.5 1.0 collective-permute-start.22
  294.1 8.1 %read.5.refs_8_ = f32[7680,128]{1,0:T(8,128)S(1)} custom-call(s32[8]{0:T(128)S(1)} %stack.209.order, s32[32]{0:T(128)S(1)} %bitcast.115, s32[256]{0:T(256)S(1)} %reshape.137.blocks, s32[256,128]{1,0:T(8,128)S(1)} %pad_bitcast_fusion.cells, bf16[3840,128]{1,0:T(8,128)(2,1)S(1)} %bitcast.98, bf16[3840,128]{1,0:T(8,128)(2,1)S(1)} %bitcast.106, ...), custom_call_target="tpu_custom_call" | custom-call | flops 2818572288 | bytes 16777216 | tf_op jit(solution)/shard_map/read/pallas_call | solution.py:252
  302.2 8.9 %read.6.refs_8_ = f32[7680,128]{1,0:T(8,128)S(1)} custom-call(s32[8]{0:T(128)S(1)} %stack.200.order, s32[32]{0:T(128)S(1)} %bitcast.116, s32[256]{0:T(256)S(1)} %reshape.137.blocks, s32[256,128]{1,0:T(8,128)S(1)} %pad_bitcast_fusion.cells, bf16[3840,128]{1,0:T(8,128)(2,1)S(1)} %bitcast.99, bf16[3840,128]{1,0:T(8,128)(2,1)S(1)} %bitcast.107, ...), custom_call_target="tpu_custom_call" | custom-call | flops 2818572288 | bytes 16777216 | tf_op jit(solution)/shard_map/read/pallas_call | solution.py:252
  311.2 6.4 %read.7 = f32[7680,128]{1,0:T(8,128)S(1)} custom-call(s32[8]{0:T(128)S(1)} %stack.191.order, s32[32]{0:T(128)S(1)} %bitcast.117, s32[256]{0:T(256)S(1)} %reshape.137.blocks, s32[256,128]{1,0:T(8,128)S(1)} %pad_bitcast_fusion.cells, bf16[3840,128]{1,0:T(8,128)(2,1)S(1)} %bitcast.100, bf16[3840,128]{1,0:T(8,128)(2,1)S(1)} %bitcast.108, ...), custom_call_target="tpu_custom_call" | custom-call | flops 2818572288 | bytes 16777216 | tf_op jit(solution)/shard_map/read/pallas_call | solution.py:252
  317.6 1.9 copy-done
  319.5 9.2 %adjoint.1 = f32[12,640,128]{2,1,0:T(8,128)} custom-call(f32[12,640,128]{2,1,0:T(8,128)} %bitcast.92, bf16[12,128,128]{2,1,0:T(8,128)(2,1)} %bitcast.127), custom_call_target="tpu_custom_call" | custom-call | tf_op jit(solution)/shard_map/adjoint/pallas_call | solution.py:284
  (127 shorter events, 14.0 us)
Async XLA Ops:
  14.1 5.0 %collective-permute-start.12 = (bf16[3840,128]{1,0:T(8,128)(2,1)}, bf16[3840,128]{1,0:T(8,128)(2,1)S(1)}, u32[]{:S(2)}, u32[]{:S(2)}) collective-permute-start(bf16[3840,128]{1,0:T(8,128)(2,1)} %bitcast.93), channel_id=1, source_target_pairs={{0,8},{8,0},{1,9},{9,1},{2,10},{10,2},{3,11},{11,3},{4,12},{12,4},... | collective-permute-start | bytes 2949128 | tf_op jit(solution)/shard_map/ppermute | solution.py:353
  14.6 25.5 %collective-permute-start.2 = (bf16[3840,128]{1,0:T(8,128)(2,1)}, bf16[3840,128]{1,0:T(8,128)(2,1)}, u32[]{:S(2)}, u32[]{:S(2)}) collective-permute-start(bf16[3840,128]{1,0:T(8,128)(2,1)} %bitcast.101), channel_id=1, source_target_pairs={{0,1},{1,0},{2,3},{3,2},{4,5},{5,4},{6,7},{7,6},{8,9},{9,8},{10,11... | collective-permute-start | bytes 2949128 | tf_op jit(solution)/shard_map/ppermute | solution.py:353
  17.1 24.9 %collective-permute-start = (bf16[3840,128]{1,0:T(8,128)(2,1)}, bf16[3840,128]{1,0:T(8,128)(2,1)}, u32[]{:S(2)}, u32[]{:S(2)}) collective-permute-start(bf16[3840,128]{1,0:T(8,128)(2,1)} %bitcast.94), channel_id=1, source_target_pairs={{0,16},{16,0},{1,17},{17,1},{2,18},{18,2},{3,19},{19,3},{4,20},{20... | collective-permute-start | bytes 2949128 | tf_op jit(solution)/shard_map/ppermute | solution.py:353
  18.6 23.5 %collective-permute-start.13 = (bf16[3840,128]{1,0:T(8,128)(2,1)}, bf16[3840,128]{1,0:T(8,128)(2,1)S(1)}, u32[]{:S(2)}, u32[]{:S(2)}) collective-permute-start(bf16[3840,128]{1,0:T(8,128)(2,1)} %bitcast.102), channel_id=1, source_target_pairs={{0,8},{8,0},{1,9},{9,1},{2,10},{10,2},{3,11},{11,3},{4,12},{12,4},... | collective-permute-start | bytes 2949128 | tf_op jit(solution)/shard_map/ppermute | solution.py:353
  18.6 42.5 %collective-permute-start.9 = (bf16[3840,128]{1,0:T(8,128)(2,1)}, bf16[3840,128]{1,0:T(8,128)(2,1)}, u32[]{:S(2)}, u32[]{:S(2)}) collective-permute-start(bf16[3840,128]{1,0:T(8,128)(2,1)} %bitcast.95), channel_id=1, source_target_pairs={{0,1},{1,0},{2,3},{3,2},{4,5},{5,4},{6,7},{7,6},{8,9},{9,8},{10,11... | collective-permute-start | bytes 2949128 | tf_op jit(solution)/shard_map/ppermute | solution.py:353
  20.1 43.0 %collective-permute-start.6 = (bf16[3840,128]{1,0:T(8,128)(2,1)}, bf16[3840,128]{1,0:T(8,128)(2,1)}, u32[]{:S(2)}, u32[]{:S(2)}) collective-permute-start(bf16[3840,128]{1,0:T(8,128)(2,1)} %bitcast.103), channel_id=1, source_target_pairs={{0,16},{16,0},{1,17},{17,1},{2,18},{18,2},{3,19},{19,3},{4,20},{20... | collective-permute-start | bytes 2949128 | tf_op jit(solution)/shard_map/ppermute | solution.py:353
  40.1 23.1 %collective-permute-start.11 = (bf16[3840,128]{1,0:T(8,128)(2,1)}, bf16[3840,128]{1,0:T(8,128)(2,1)S(1)}, u32[]{:S(2)}, u32[]{:S(2)}) collective-permute-start(bf16[3840,128]{1,0:T(8,128)(2,1)} %collective-permute-done.2.refs_5_), channel_id=1, source_target_pairs={{0,8},{8,0},{1,9},{9,1},{2,10},{10,2},{3,11},{11,3},{4,12},{12,4},... | collective-permute-start | bytes 2949128 | tf_op jit(solution)/shard_map/ppermute | solution.py:353
  42.0 40.0 %collective-permute-start.1 = (bf16[3840,128]{1,0:T(8,128)(2,1)}, bf16[3840,128]{1,0:T(8,128)(2,1)S(1)}, u32[]{:S(2)}, u32[]{:S(2)}) collective-permute-start(bf16[3840,128]{1,0:T(8,128)(2,1)} %collective-permute-done.refs_0_), channel_id=1, source_target_pairs={{0,1},{1,0},{2,3},{3,2},{4,5},{5,4},{6,7},{7,6},{8,9},{9,8},{10,11... | collective-permute-start | bytes 2949128 | tf_op jit(solution)/shard_map/ppermute | solution.py:353
  43.1 40.9 %collective-permute-start.3 = (bf16[3840,128]{1,0:T(8,128)(2,1)}, bf16[3840,128]{1,0:T(8,128)(2,1)S(1)}, u32[]{:S(2)}, u32[]{:S(2)}) collective-permute-start(bf16[3840,128]{1,0:T(8,128)(2,1)} %collective-permute-done.2.refs_5_), channel_id=1, source_target_pairs={{0,16},{16,0},{1,17},{17,1},{2,18},{18,2},{3,19},{19,3},{4,20},{20... | collective-permute-start | bytes 2949128 | tf_op jit(solution)/shard_map/ppermute | solution.py:353
  61.1 36.4 %collective-permute-start.7 = (bf16[3840,128]{1,0:T(8,128)(2,1)}, bf16[3840,128]{1,0:T(8,128)(2,1)}, u32[]{:S(2)}, u32[]{:S(2)}) collective-permute-start(bf16[3840,128]{1,0:T(8,128)(2,1)} %collective-permute-done.refs_0_), channel_id=1, source_target_pairs={{0,8},{8,0},{1,9},{9,1},{2,10},{10,2},{3,11},{11,3},{4,12},{12,4},... | collective-permute-start | bytes 2949128 | tf_op jit(solution)/shard_map/ppermute | solution.py:353
  63.1 34.4 %collective-permute-start.10 = (bf16[3840,128]{1,0:T(8,128)(2,1)}, bf16[3840,128]{1,0:T(8,128)(2,1)}, u32[]{:S(2)}, u32[]{:S(2)}) collective-permute-start(bf16[3840,128]{1,0:T(8,128)(2,1)} %collective-permute-done.9.refs_4_), channel_id=1, source_target_pairs={{0,8},{8,0},{1,9},{9,1},{2,10},{10,2},{3,11},{11,3},{4,12},{12,4},... | collective-permute-start | bytes 2949128 | tf_op jit(solution)/shard_map/ppermute | solution.py:353
  64.1 33.5 %collective-permute-start.8 = (bf16[3840,128]{1,0:T(8,128)(2,1)}, bf16[3840,128]{1,0:T(8,128)(2,1)}, u32[]{:S(2)}, u32[]{:S(2)}) collective-permute-start(bf16[3840,128]{1,0:T(8,128)(2,1)} %collective-permute-done.6.refs_1_), channel_id=1, source_target_pairs={{0,8},{8,0},{1,9},{9,1},{2,10},{10,2},{3,11},{11,3},{4,12},{12,4},... | collective-permute-start | bytes 2949128 | tf_op jit(solution)/shard_map/ppermute | solution.py:353
  66.3 18.5 %all-to-all-start = ((s32[8,4,8,128]{3,1,2,0:T(4,128)}), s32[8,4,8,128]{3,1,2,0:T(4,128)S(1)}, u32[]{:S(2)}, u32[]{:S(2)}) async-start(s32[8,4,8,128]{3,1,2,0:T(4,128)} %bitcast.6), calls=%async_computation | async-start | bytes 262144 | tf_op jit(solution)/shard_map/all_to_all | solution.py:376
  69.6 121.0 %reduce-scatter.2.cloned.1.call-start = ((), (), s32[]{:S(2)}) async-start(), calls=%async_computation.2 | async-start | bytes 4177920 | tf_op jit(solution)/shard_map/reduce_scatter | solution.py:405
  82.1 29.1 %collective-permute-start.4 = (bf16[3840,128]{1,0:T(8,128)(2,1)S(1)}, bf16[3840,128]{1,0:T(8,128)(2,1)S(1)}, u32[]{:S(2)}, u32[]{:S(2)}) collective-permute-start(bf16[3840,128]{1,0:T(8,128)(2,1)S(1)} %collective-permute-done.1.refs_0_), channel_id=1, source_target_pairs={{0,8},{8,0},{1,9},{9,1},{2,10},{10,2},{3,11},{11,3},{4,12},{12,4},... | collective-permute-start | bytes 2949128 | tf_op jit(solution)/shard_map/ppermute | solution.py:353
  84.0 27.2 %collective-permute-start.5 = (bf16[3840,128]{1,0:T(8,128)(2,1)S(1)}, bf16[3840,128]{1,0:T(8,128)(2,1)}, u32[]{:S(2)}, u32[]{:S(2)}) collective-permute-start(bf16[3840,128]{1,0:T(8,128)(2,1)S(1)} %collective-permute-done.3.refs_1_), channel_id=1, source_target_pairs={{0,8},{8,0},{1,9},{9,1},{2,10},{10,2},{3,11},{11,3},{4,12},{12,4},... | collective-permute-start | bytes 2949128 | tf_op jit(solution)/shard_map/ppermute | solution.py:353
  85.0 1.2 copy-start.1
  86.2 1.2 copy-start.3
  87.4 1.2 copy-start.7
  89.8 7.7 %copy-start.11 = (bf16[3840,128]{1,0:T(8,128)(2,1)S(1)}, bf16[3840,128]{1,0:T(8,128)(2,1)}, u32[]{:S(2)}) copy-start(bf16[3840,128]{1,0:T(8,128)(2,1)} %copy-done.10) | copy-start | bytes 2949124
  95.8 1.7 copy-start.13
  111.2 9.3 %copy-start.5 = (s32[1,32]{1,0:T(1,128)S(1)}, s32[1,32]{1,0:T(1,128)}, u32[]{:S(2)}) copy-start(s32[1,32]{1,0:T(1,128)} %param.9) | copy-start | bytes 388
  111.2 9.3 %copy-start.15 = (s32[1,32,7,128]{3,1,2,0:T(8,128)S(1)}, s32[1,32,7,128]{3,1,2,0:T(8,128)}, u32[]{:S(2)}) copy-start(s32[1,32,7,128]{3,1,2,0:T(8,128)} %param.8) | copy-start | bytes 344068
  193.1 23.8 %collective-permute-start.42 = (bf16[768,256]{1,0:T(8,128)(2,1)}, bf16[768,256]{1,0:T(8,128)(2,1)S(1)}, u32[]{:S(2)}, u32[]{:S(2)}) collective-permute-start(bf16[768,256]{1,0:T(8,128)(2,1)} %get-tuple-element.10.refs_0_), channel_id=1, source_target_pairs={{0,16},{16,0},{1,17},{17,1},{2,18},{18,2},{3,19},{19,3},{4,20},{20... | collective-permute-start | bytes 1179656 | tf_op jit(solution)/shard_map/ppermute | solution.py:353
  194.6 24.3 %collective-permute-start.43 = (bf16[768,256]{1,0:T(8,128)(2,1)}, bf16[768,256]{1,0:T(8,128)(2,1)S(1)}, u32[]{:S(2)}, u32[]{:S(2)}) collective-permute-start(bf16[768,256]{1,0:T(8,128)(2,1)} %get-tuple-element.10.refs_0_), channel_id=1, source_target_pairs={{0,1},{1,0},{2,3},{3,2},{4,5},{5,4},{6,7},{7,6},{8,9},{9,8},{10,11... | collective-permute-start | bytes 1179656 | tf_op jit(solution)/shard_map/ppermute | solution.py:353
  196.9 2.7 collective-permute-start.14
  198.2 3.9 %collective-permute-start.15 = (f32[2,48,128]{2,1,0:T(8,128)S(1)}, f32[2,48,128]{2,1,0:T(8,128)S(1)}, u32[]{:S(2)}, u32[]{:S(2)}) collective-permute-start(f32[2,48,128]{2,1,0:T(8,128)S(1)} %bitcast.130), channel_id=1, source_target_pairs={{8,0},{16,8},{24,16},{9,1},{17,9},{25,17},{10,2},{18,10},{26,18},{... | collective-permute-start | bytes 147464 | tf_op jit(solution)/shard_map/ppermute | solution.py:304
  203.1 7.6 %collective-permute-start.16 = (f32[36,2,128]{2,1,0:T(2,128)S(1)}, f32[36,2,128]{2,1,0:T(2,128)S(1)}, u32[]{:S(2)}, u32[]{:S(2)}) collective-permute-start(f32[36,2,128]{2,1,0:T(2,128)S(1)} %get-tuple-element.18), channel_id=1, source_target_pairs={{0,1},{1,2},{2,3},{3,4},{4,5},{5,6},{6,7},{8,9},{9,10},{10,11},{11... | collective-permute-start | bytes 110600 | tf_op jit(solution)/shard_map/ppermute | solution.py:301
  205.6 8.5 %collective-permute-start.17 = (f32[36,2,128]{2,1,0:T(2,128)S(1)}, f32[36,2,128]{2,1,0:T(2,128)S(1)}, u32[]{:S(2)}, u32[]{:S(2)}) collective-permute-start(f32[36,2,128]{2,1,0:T(2,128)S(1)} %get-tuple-element.19), channel_id=1, source_target_pairs={{1,0},{2,1},{3,2},{4,3},{5,4},{6,5},{7,6},{9,8},{10,9},{11,10},{12... | collective-permute-start | bytes 110600 | tf_op jit(solution)/shard_map/ppermute | solution.py:304
  207.4 42.9 %copy-start.14 = (f32[1536,128]{1,0:T(8,128)S(1)}, f32[1536,128]{1,0:T(8,128)}, u32[]{:S(2)}) copy-start(f32[1536,128]{1,0:T(8,128)} %get-tuple-element.9) | copy-start | bytes 2359300
  207.4 15.1 %collective-permute-start.45 = (bf16[768,256]{1,0:T(8,128)(2,1)}, bf16[768,256]{1,0:T(8,128)(2,1)S(1)}, u32[]{:S(2)}, u32[]{:S(2)}) collective-permute-start(bf16[768,256]{1,0:T(8,128)(2,1)} %get-tuple-element.10.refs_0_), channel_id=1, source_target_pairs={{0,8},{8,0},{1,9},{9,1},{2,10},{10,2},{3,11},{11,3},{4,12},{12,4},... | collective-permute-start | bytes 1179656 | tf_op jit(solution)/shard_map/ppermute | solution.py:353
  210.7 14.9 %collective-permute-start.34 = (bf16[768,256]{1,0:T(8,128)(2,1)}, bf16[768,256]{1,0:T(8,128)(2,1)S(1)}, u32[]{:S(2)}, u32[]{:S(2)}) collective-permute-start(bf16[768,256]{1,0:T(8,128)(2,1)} %get-tuple-element.10.refs_0_), channel_id=1, source_target_pairs={{0,2},{2,4},{4,6},{6,0},{1,3},{3,5},{5,7},{7,1},{8,10},{10,12},{12... | collective-permute-start | bytes 1179656 | tf_op jit(solution)/shard_map/ppermute | solution.py:357
  214.1 19.3 %collective-permute-start.26 = (bf16[768,256]{1,0:T(8,128)(2,1)}, bf16[768,256]{1,0:T(8,128)(2,1)S(1)}, u32[]{:S(2)}, u32[]{:S(2)}) collective-permute-start(bf16[768,256]{1,0:T(8,128)(2,1)} %get-tuple-element.10.refs_0_), channel_id=1, source_target_pairs={{0,6},{2,0},{4,2},{6,4},{1,7},{3,1},{5,3},{7,5},{8,14},{10,8},{12,... | collective-permute-start | bytes 1179656 | tf_op jit(solution)/shard_map/ppermute | solution.py:357
  216.9 33.3 %collective-permute-start.18 = (bf16[768,256]{1,0:T(8,128)(2,1)}, bf16[768,256]{1,0:T(8,128)(2,1)S(1)}, u32[]{:S(2)}, u32[]{:S(2)}) collective-permute-start(bf16[768,256]{1,0:T(8,128)(2,1)} %get-tuple-element.10.refs_0_), channel_id=1, source_target_pairs={{0,4},{2,6},{4,0},{6,2},{1,5},{3,7},{5,1},{7,3},{8,12},{10,14},{12... | collective-permute-start | bytes 1179656 | tf_op jit(solution)/shard_map/ppermute | solution.py:357
  218.9 31.9 %collective-permute-start.44 = (bf16[768,256]{1,0:T(8,128)(2,1)S(1)}, bf16[768,256]{1,0:T(8,128)(2,1)S(1)}, u32[]{:S(2)}, u32[]{:S(2)}) collective-permute-start(bf16[768,256]{1,0:T(8,128)(2,1)S(1)} %collective-permute-done.42.refs_1_), channel_id=1, source_target_pairs={{0,1},{1,0},{2,3},{3,2},{4,5},{5,4},{6,7},{7,6},{8,9},{9,8},{10,11... | collective-permute-start | bytes 1179656 | tf_op jit(solution)/shard_map/ppermute | solution.py:353
  222.5 29.2 %collective-permute-start.46 = (bf16[768,256]{1,0:T(8,128)(2,1)S(1)}, bf16[768,256]{1,0:T(8,128)(2,1)S(1)}, u32[]{:S(2)}, u32[]{:S(2)}) collective-permute-start(bf16[768,256]{1,0:T(8,128)(2,1)S(1)} %collective-permute-done.42.refs_1_), channel_id=1, source_target_pairs={{0,8},{8,0},{1,9},{9,1},{2,10},{10,2},{3,11},{11,3},{4,12},{12,4},... | collective-permute-start | bytes 1179656 | tf_op jit(solution)/shard_map/ppermute | solution.py:353
  225.6 28.9 %collective-permute-start.36 = (bf16[768,256]{1,0:T(8,128)(2,1)S(1)}, bf16[768,256]{1,0:T(8,128)(2,1)S(1)}, u32[]{:S(2)}, u32[]{:S(2)}) collective-permute-start(bf16[768,256]{1,0:T(8,128)(2,1)S(1)} %collective-permute-done.34.refs_0_), channel_id=1, source_target_pairs={{0,1},{1,0},{2,3},{3,2},{4,5},{5,4},{6,7},{7,6},{8,9},{9,8},{10,11... | collective-permute-start | bytes 1179656 | tf_op jit(solution)/shard_map/ppermute | solution.py:353
  233.4 21.0 %collective-permute-start.35 = (bf16[768,256]{1,0:T(8,128)(2,1)S(1)}, bf16[768,256]{1,0:T(8,128)(2,1)S(1)}, u32[]{:S(2)}, u32[]{:S(2)}) collective-permute-start(bf16[768,256]{1,0:T(8,128)(2,1)S(1)} %collective-permute-done.34.refs_0_), channel_id=1, source_target_pairs={{0,16},{16,0},{1,17},{17,1},{2,18},{18,2},{3,19},{19,3},{4,20},{20... | collective-permute-start | bytes 1179656 | tf_op jit(solution)/shard_map/ppermute | solution.py:353
  250.3 3.0 collective-permute-start.47
  250.8 4.9 %collective-permute-start.38 = (bf16[768,256]{1,0:T(8,128)(2,1)S(1)}, bf16[768,256]{1,0:T(8,128)(2,1)S(1)}, u32[]{:S(2)}, u32[]{:S(2)}) collective-permute-start(bf16[768,256]{1,0:T(8,128)(2,1)S(1)} %collective-permute-done.34.refs_0_), channel_id=1, source_target_pairs={{0,8},{8,0},{1,9},{9,1},{2,10},{10,2},{3,11},{11,3},{4,12},{12,4},... | collective-permute-start | bytes 1179656 | tf_op jit(solution)/shard_map/ppermute | solution.py:353
  251.7 12.0 %collective-permute-start.27 = (bf16[768,256]{1,0:T(8,128)(2,1)S(1)}, bf16[768,256]{1,0:T(8,128)(2,1)S(1)}, u32[]{:S(2)}, u32[]{:S(2)}) collective-permute-start(bf16[768,256]{1,0:T(8,128)(2,1)S(1)} %collective-permute-done.26.refs_0_), channel_id=1, source_target_pairs={{0,16},{16,0},{1,17},{17,1},{2,18},{18,2},{3,19},{19,3},{4,20},{20... | collective-permute-start | bytes 1179656 | tf_op jit(solution)/shard_map/ppermute | solution.py:353
  253.3 12.0 %collective-permute-start.28 = (bf16[768,256]{1,0:T(8,128)(2,1)S(1)}, bf16[768,256]{1,0:T(8,128)(2,1)S(1)}, u32[]{:S(2)}, u32[]{:S(2)}) collective-permute-start(bf16[768,256]{1,0:T(8,128)(2,1)S(1)} %collective-permute-done.26.refs_0_), channel_id=1, source_target_pairs={{0,1},{1,0},{2,3},{3,2},{4,5},{5,4},{6,7},{7,6},{8,9},{9,8},{10,11... | collective-permute-start | bytes 1179656 | tf_op jit(solution)/shard_map/ppermute | solution.py:353
  254.4 10.8 %collective-permute-start.30 = (bf16[768,256]{1,0:T(8,128)(2,1)S(1)}, bf16[768,256]{1,0:T(8,128)(2,1)S(1)}, u32[]{:S(2)}, u32[]{:S(2)}) collective-permute-start(bf16[768,256]{1,0:T(8,128)(2,1)S(1)} %collective-permute-done.26.refs_0_), channel_id=1, source_target_pairs={{0,8},{8,0},{1,9},{9,1},{2,10},{10,2},{3,11},{11,3},{4,12},{12,4},... | collective-permute-start | bytes 1179656 | tf_op jit(solution)/shard_map/ppermute | solution.py:353
  254.5 18.0 %collective-permute-start.20 = (bf16[768,256]{1,0:T(8,128)(2,1)S(1)}, bf16[768,256]{1,0:T(8,128)(2,1)S(1)}, u32[]{:S(2)}, u32[]{:S(2)}) collective-permute-start(bf16[768,256]{1,0:T(8,128)(2,1)S(1)} %collective-permute-done.18.refs_0_), channel_id=1, source_target_pairs={{0,1},{1,0},{2,3},{3,2},{4,5},{5,4},{6,7},{7,6},{8,9},{9,8},{10,11... | collective-permute-start | bytes 1179656 | tf_op jit(solution)/shard_map/ppermute | solution.py:353
  255.7 17.1 %collective-permute-start.19 = (bf16[768,256]{1,0:T(8,128)(2,1)S(1)}, bf16[768,256]{1,0:T(8,128)(2,1)S(1)}, u32[]{:S(2)}, u32[]{:S(2)}) collective-permute-start(bf16[768,256]{1,0:T(8,128)(2,1)S(1)} %collective-permute-done.18.refs_0_), channel_id=1, source_target_pairs={{0,16},{16,0},{1,17},{17,1},{2,18},{18,2},{3,19},{19,3},{4,20},{20... | collective-permute-start | bytes 1179656 | tf_op jit(solution)/shard_map/ppermute | solution.py:353
  263.7 15.9 %collective-permute-start.37 = (bf16[768,256]{1,0:T(8,128)(2,1)S(1)}, bf16[768,256]{1,0:T(8,128)(2,1)S(1)}, u32[]{:S(2)}, u32[]{:S(2)}) collective-permute-start(bf16[768,256]{1,0:T(8,128)(2,1)S(1)} %collective-permute-done.36.refs_2_), channel_id=1, source_target_pairs={{0,16},{16,0},{1,17},{17,1},{2,18},{18,2},{3,19},{19,3},{4,20},{20... | collective-permute-start | bytes 1179656 | tf_op jit(solution)/shard_map/ppermute | solution.py:353
  265.3 15.9 %collective-permute-start.40 = (bf16[768,256]{1,0:T(8,128)(2,1)S(1)}, bf16[768,256]{1,0:T(8,128)(2,1)S(1)}, u32[]{:S(2)}, u32[]{:S(2)}) collective-permute-start(bf16[768,256]{1,0:T(8,128)(2,1)S(1)} %collective-permute-done.36.refs_2_), channel_id=1, source_target_pairs={{0,8},{8,0},{1,9},{9,1},{2,10},{10,2},{3,11},{11,3},{4,12},{12,4},... | collective-permute-start | bytes 1179656 | tf_op jit(solution)/shard_map/ppermute | solution.py:353
  265.3 9.2 %collective-permute-start.48 = (bf16[768,256]{1,0:T(8,128)(2,1)S(1)}, bf16[768,256]{1,0:T(8,128)(2,1)S(1)}, u32[]{:S(2)}, u32[]{:S(2)}) collective-permute-start(bf16[768,256]{1,0:T(8,128)(2,1)S(1)} %collective-permute-done.44.refs_3_), channel_id=1, source_target_pairs={{0,8},{8,0},{1,9},{9,1},{2,10},{10,2},{3,11},{11,3},{4,12},{12,4},... | collective-permute-start | bytes 1179656 | tf_op jit(solution)/shard_map/ppermute | solution.py:353
  272.5 7.2 %collective-permute-start.39 = (bf16[768,256]{1,0:T(8,128)(2,1)S(1)}, bf16[768,256]{1,0:T(8,128)(2,1)S(1)}, u32[]{:S(2)}, u32[]{:S(2)}) collective-permute-start(bf16[768,256]{1,0:T(8,128)(2,1)S(1)} %collective-permute-done.35.refs_1_), channel_id=1, source_target_pairs={{0,8},{8,0},{1,9},{9,1},{2,10},{10,2},{3,11},{11,3},{4,12},{12,4},... | collective-permute-start | bytes 1179656 | tf_op jit(solution)/shard_map/ppermute | solution.py:353
  272.8 11.6 %collective-permute-start.29 = (bf16[768,256]{1,0:T(8,128)(2,1)S(1)}, bf16[768,256]{1,0:T(8,128)(2,1)S(1)}, u32[]{:S(2)}, u32[]{:S(2)}) collective-permute-start(bf16[768,256]{1,0:T(8,128)(2,1)S(1)} %collective-permute-done.27.refs_1_), channel_id=1, source_target_pairs={{0,1},{1,0},{2,3},{3,2},{4,5},{5,4},{6,7},{7,6},{8,9},{9,8},{10,11... | collective-permute-start | bytes 1179656 | tf_op jit(solution)/shard_map/ppermute | solution.py:353
  274.4 10.0 %copy-start.2 = (bf16[6,640,128]{2,1,0:T(8,128)(2,1)S(1)}, bf16[6,640,128]{2,1,0:T(8,128)(2,1)}, u32[]{:S(2)}) copy-start(bf16[6,640,128]{2,1,0:T(8,128)(2,1)} %get-tuple-element.7) | copy-start | bytes 2949124
  274.4 10.0 %copy-start.4 = (bf16[6,640,128]{2,1,0:T(8,128)(2,1)S(1)}, bf16[6,640,128]{2,1,0:T(8,128)(2,1)}, u32[]{:S(2)}) copy-start(bf16[6,640,128]{2,1,0:T(8,128)(2,1)} %get-tuple-element.8) | copy-start | bytes 2949124
  274.4 10.0 %copy-start.12 = (bf16[768,256]{1,0:T(8,128)(2,1)S(1)}, bf16[768,256]{1,0:T(8,128)(2,1)}, u32[]{:S(2)}) copy-start(bf16[768,256]{1,0:T(8,128)(2,1)} %get-tuple-element.10.refs_0_) | copy-start | bytes 1179652
  274.4 18.1 %collective-permute-start.31 = (bf16[768,256]{1,0:T(8,128)(2,1)S(1)}, bf16[768,256]{1,0:T(8,128)(2,1)S(1)}, u32[]{:S(2)}, u32[]{:S(2)}) collective-permute-start(bf16[768,256]{1,0:T(8,128)(2,1)S(1)} %collective-permute-done.27.refs_1_), channel_id=1, source_target_pairs={{0,8},{8,0},{1,9},{9,1},{2,10},{10,2},{3,11},{11,3},{4,12},{12,4},... | collective-permute-start | bytes 1179656 | tf_op jit(solution)/shard_map/ppermute | solution.py:353
  279.6 13.9 %collective-permute-start.32 = (bf16[768,256]{1,0:T(8,128)(2,1)S(1)}, bf16[768,256]{1,0:T(8,128)(2,1)S(1)}, u32[]{:S(2)}, u32[]{:S(2)}) collective-permute-start(bf16[768,256]{1,0:T(8,128)(2,1)S(1)} %collective-permute-done.28.refs_2_), channel_id=1, source_target_pairs={{0,8},{8,0},{1,9},{9,1},{2,10},{10,2},{3,11},{11,3},{4,12},{12,4},... | collective-permute-start | bytes 1179656 | tf_op jit(solution)/shard_map/ppermute | solution.py:353
  279.6 14.0 %collective-permute-start.21 = (bf16[768,256]{1,0:T(8,128)(2,1)S(1)}, bf16[768,256]{1,0:T(8,128)(2,1)S(1)}, u32[]{:S(2)}, u32[]{:S(2)}) collective-permute-start(bf16[768,256]{1,0:T(8,128)(2,1)S(1)} %collective-permute-done.20.refs_2_), channel_id=1, source_target_pairs={{0,16},{16,0},{1,17},{17,1},{2,18},{18,2},{3,19},{19,3},{4,20},{20... | collective-permute-start | bytes 1179656 | tf_op jit(solution)/shard_map/ppermute | solution.py:353
  281.2 12.9 %collective-permute-start.41 = (bf16[768,256]{1,0:T(8,128)(2,1)S(1)}, bf16[768,256]{1,0:T(8,128)(2,1)S(1)}, u32[]{:S(2)}, u32[]{:S(2)}) collective-permute-start(bf16[768,256]{1,0:T(8,128)(2,1)S(1)} %collective-permute-done.37.refs_3_), channel_id=1, source_target_pairs={{0,8},{8,0},{1,9},{9,1},{2,10},{10,2},{3,11},{11,3},{4,12},{12,4},... | collective-permute-start | bytes 1179656 | tf_op jit(solution)/shard_map/ppermute | solution.py:353
  281.7 2.7 copy-start.16
  284.4 17.8 %collective-permute-start.33 = (bf16[768,256]{1,0:T(8,128)(2,1)S(1)}, bf16[768,256]{1,0:T(8,128)(2,1)S(1)}, u32[]{:S(2)}, u32[]{:S(2)}) collective-permute-start(bf16[768,256]{1,0:T(8,128)(2,1)S(1)} %collective-permute-done.29.refs_3_), channel_id=1, source_target_pairs={{0,8},{8,0},{1,9},{9,1},{2,10},{10,2},{3,11},{11,3},{4,12},{12,4},... | collective-permute-start | bytes 1179656 | tf_op jit(solution)/shard_map/ppermute | solution.py:353
  292.5 18.6 %collective-permute-start.22 = (bf16[768,256]{1,0:T(8,128)(2,1)S(1)}, bf16[768,256]{1,0:T(8,128)(2,1)S(1)}, u32[]{:S(2)}, u32[]{:S(2)}) collective-permute-start(bf16[768,256]{1,0:T(8,128)(2,1)S(1)} %collective-permute-done.18.refs_0_), channel_id=1, source_target_pairs={{0,8},{8,0},{1,9},{9,1},{2,10},{10,2},{3,11},{11,3},{4,12},{12,4},... | collective-permute-start | bytes 1179656 | tf_op jit(solution)/shard_map/ppermute | solution.py:353
  293.5 17.7 %collective-permute-start.24 = (bf16[768,256]{1,0:T(8,128)(2,1)S(1)}, bf16[768,256]{1,0:T(8,128)(2,1)S(1)}, u32[]{:S(2)}, u32[]{:S(2)}) collective-permute-start(bf16[768,256]{1,0:T(8,128)(2,1)S(1)} %collective-permute-done.20.refs_2_), channel_id=1, source_target_pairs={{0,8},{8,0},{1,9},{9,1},{2,10},{10,2},{3,11},{11,3},{4,12},{12,4},... | collective-permute-start | bytes 1179656 | tf_op jit(solution)/shard_map/ppermute | solution.py:353
  293.6 17.6 %collective-permute-start.23 = (bf16[768,256]{1,0:T(8,128)(2,1)S(1)}, bf16[768,256]{1,0:T(8,128)(2,1)S(1)}, u32[]{:S(2)}, u32[]{:S(2)}) collective-permute-start(bf16[768,256]{1,0:T(8,128)(2,1)S(1)} %collective-permute-done.19.refs_1_), channel_id=1, source_target_pairs={{0,8},{8,0},{1,9},{9,1},{2,10},{10,2},{3,11},{11,3},{4,12},{12,4},... | collective-permute-start | bytes 1179656 | tf_op jit(solution)/shard_map/ppermute | solution.py:353
  294.0 17.1 %collective-permute-start.25 = (bf16[768,256]{1,0:T(8,128)(2,1)S(1)}, bf16[768,256]{1,0:T(8,128)(2,1)S(1)}, u32[]{:S(2)}, u32[]{:S(2)}) collective-permute-start(bf16[768,256]{1,0:T(8,128)(2,1)S(1)} %collective-permute-done.21.refs_3_), channel_id=1, source_target_pairs={{0,8},{8,0},{1,9},{9,1},{2,10},{10,2},{3,11},{11,3},{4,12},{12,4},... | collective-permute-start | bytes 1179656 | tf_op jit(solution)/shard_map/ppermute | solution.py:353
  317.6 1.9 copy-start
  (4 other events, 4.1 us)
Sparse Core Ops, SparseCore 0:
  120.5 70.0 reduce-scatter.1

commit v2 on v1

v2 whole, which is shorter than its diff:
```python
import functools

import jax
import jax.numpy as jnp
from jax import lax
from jax.experimental import pallas as pl
from jax.experimental.pallas import tpu as pltpu
from jax.sharding import Mesh
from jax.sharding import PartitionSpec as P

CIL = 32
CXL = 48
CELLS = CIL * CXL
QUARTER = CELLS // 4
FOLD = CXL // 3
MIB = 1 << 20
IN_SMEM = pl.BlockSpec(memory_space=pltpu.SMEM)
IN_VMEM = pl.BlockSpec(memory_space=pltpu.VMEM)
IN_ANY = pl.BlockSpec(memory_space=pl.ANY)


def hot(cells, shape, axis):
    line = lax.broadcasted_iota(jnp.int32, shape, axis)
    return jnp.where(line == cells, 1.0, 0.0).astype(jnp.bfloat16)


def quarter_of(cells):
    return sum((cells >= q * QUARTER).astype(jnp.int32) for q in (1, 2, 3))


def low_lanes(shape):
    return lax.broadcasted_iota(jnp.int32, shape, len(shape) - 1) < 64


def swap_lanes(value):
    return pltpu.roll(value, 64, 1)


def tie(value, *tokens):
    def kernel(*refs):
        pass

    return pl.pallas_call(
        kernel,
        out_shape=jax.ShapeDtypeStruct(value.shape, value.dtype),
        in_specs=[IN_ANY] * (1 + len(tokens)),
        out_specs=IN_ANY,
        input_output_aliases={0: 0},
        name="tie",
    )(value, *tokens)


def filter_kernel(half, taps, source, *targets):
    each, rows, samples = source.shape
    row = lax.broadcasted_iota(jnp.int32, (samples, samples), 0)
    col = lax.broadcasted_iota(jnp.int32, (samples, samples), 1)
    for i in range(each):
        line = jnp.broadcast_to(taps[i], (samples, samples))
        band = pltpu.roll(line, 0, 1, stride=1, stride_axis=0)
        matrix = jnp.where(col >= row, band, 0.0).astype(jnp.bfloat16)
        value = jnp.dot(source[i], matrix, preferred_element_type=jnp.float32)
        if half == 0:
            targets[1][i] = matrix
        else:
            targets[1][i] = value.astype(jnp.bfloat16)
        for block in range(rows // 128):
            top = value[block * 128 : block * 128 + 64]
            bottom = value[block * 128 + 64 : block * 128 + 128]
            left = low_lanes(top.shape)
            if half == 0:
                packed = jnp.where(left, top, swap_lanes(bottom))
            else:
                packed = jnp.where(left, swap_lanes(top), bottom)
            targets[0][i, block * 64 : block * 64 + 64] = packed.astype(jnp.bfloat16)


def filter_call(half, traces, taps):
    surveys, unused, samples = taps.shape
    rows = traces.shape[0] // surveys
    each = 3
    second = (each, samples, samples) if half == 0 else (each, rows, samples)
    return pl.pallas_call(
        functools.partial(filter_kernel, half),
        grid=(surveys // each,),
        in_specs=[
            pl.BlockSpec((each, 1, samples), lambda i: (i, 0, 0)),
            pl.BlockSpec((each, rows, samples), lambda i: (i, 0, 0)),
        ],
        out_specs=[
            pl.BlockSpec((each, rows // 2, samples), lambda i: (i, 0, 0)),
            pl.BlockSpec(second, lambda i: (i, 0, 0)),
        ],
        out_shape=[
            jax.ShapeDtypeStruct((surveys, rows // 2, samples), jnp.bfloat16),
            jax.ShapeDtypeStruct((surveys,) + second[1:], jnp.bfloat16),
        ],
        name=f"filter_{half}",
    )(taps, traces.reshape(surveys, rows, samples))


def stack_kernel(spec, tile_order, source_order, counts, blocks, cells, *refs):
    sizes, sources, tiles, with_fold, first, last = spec
    group = 8
    pieces = refs[: len(sizes)]
    refs = refs[len(sizes) :]
    if not first:
        before, refs = refs[0], refs[1:]
    outs = refs[: tiles if last else 1]
    held, total, live, sems = refs[len(outs) :]
    copies = []
    start = 0
    for i, rows in enumerate(sizes):
        copies.append(
            pltpu.make_async_copy(pieces[i], held.at[pl.ds(start, rows)], sems.at[i])
        )
        start += rows
    per_source = start // sources
    for copy in copies:
        copy.start()
    total[...] = jnp.zeros_like(total) if first else before[...]
    for copy in copies:
        copy.wait()

    def tile_step(tile, unused):
        def add_source(source, n):
            base = source_order[source] * tiles + tile_order[tile]

            def add_slot(c, n):
                live[n] = base * 8 + c
                live[n + 128] = blocks[base * 8 + c] * 64 + source * per_source
                return n + 1

            return lax.fori_loop(0, counts[base], add_slot, n)

        n = lax.fori_loop(0, sources, add_source, 0)

        def one_group(g, unused):
            picked = []
            for i in range(group):
                at = g * group + i
                entry = live[jnp.minimum(at, n - 1)]
                picked.append(jnp.where(at < n, cells[pl.ds(entry, 1), :], -1))
            rows = jnp.concatenate(picked, axis=0)
            columns = quarter_of(rows).T
            data = []
            left = low_lanes((64, 128))
            lane_group = 1 - low_lanes((128, 128)).astype(jnp.int32)
            for i in range(group):
                at = live[128 + jnp.minimum(g * group + i, n - 1)]
                block = held[pl.ds(pl.multiple_of(at, 64), 64), :].astype(jnp.float32)
                turned = swap_lanes(block)
                both = jnp.concatenate(
                    [jnp.where(left, block, turned), jnp.where(left, turned, block)], axis=0
                )
                spot = columns[:, i : i + 1] - lane_group
                data.append(
                    jnp.concatenate(
                        [jnp.where(spot == 0, both, 0.0), jnp.where(spot == 2, both, 0.0)], axis=1
                    ).astype(jnp.bfloat16)
                )
            data = jnp.concatenate(data, axis=0)
            line = jnp.concatenate(picked, axis=1)
            width = line.shape[1]
            selector = hot(line - QUARTER * quarter_of(line), (QUARTER, width), 0)
            total[tile, :QUARTER] += jnp.dot(selector, data, preferred_element_type=jnp.float32)
            if with_fold:
                inline = ((line >> 4) * 171) >> 9
                cross = line - CXL * inline
                row = jnp.where(line >= 0, cross & 15, -1)
                lane = inline + 32 * (cross >> 4)
                total[tile, QUARTER:, :128] += lax.dot_general(
                    hot(row, (FOLD, width), 0),
                    hot(lane, (128, width), 0),
                    (((1,), (1,)), ((), ())),
                    preferred_element_type=jnp.float32,
                )
            return 0

        lax.fori_loop(0, (n + group - 1) // group, one_group, 0)
        return 0

    lax.fori_loop(0, tiles, tile_step, 0)
    if last:
        for tile in range(tiles):
            outs[tile][...] = total[tile]
    else:
        outs[0][...] = total[...]


def stack_call(orders, slots, pieces, sources, before, tiles, with_fold, last):
    first = before is None
    sizes = tuple(piece.shape[0] for piece in pieces)
    rows = QUARTER + (FOLD if with_fold else 0)
    extra = [] if first else [before]
    whole = jax.ShapeDtypeStruct((tiles, rows, 256), jnp.float32)
    out_shape = [jax.ShapeDtypeStruct((rows, 256), jnp.float32)] * tiles if last else [whole]
    return pl.pallas_call(
        functools.partial(stack_kernel, (sizes, sources, tiles, with_fold, first, last)),
        out_shape=out_shape,
        in_specs=[IN_SMEM] * 4 + [IN_VMEM] + [IN_ANY] * len(pieces) + [IN_VMEM] * len(extra),
        out_specs=[IN_VMEM] * len(out_shape),
        scratch_shapes=[
            pltpu.VMEM((sum(sizes), 128), jnp.bfloat16),
            pltpu.VMEM(whole.shape, jnp.float32),
            pltpu.SMEM((256,), jnp.int32),
            pltpu.SemaphoreType.DMA((len(pieces),)),
        ],
        compiler_params=pltpu.CompilerParams(vmem_limit_bytes=32 * MIB),
        cost_estimate=pl.CostEstimate(
            flops=sources * tiles * 2 * 2 * QUARTER * 128 * 256,
            bytes_accessed=sum(sizes) * 256 + 4 * MIB,
            transcendentals=0,
        ),
        name="stack",
    )(*orders, *slots, *pieces, *extra)


def image_kernel(half, *refs):
    parts = refs[:4]
    if half == 0:
        packed, value_out, fold_out = refs[4:]
        fold = sum(part[QUARTER:] for part in parts)
        fold_out[...] = fold
    else:
        fold_in, before, packed, image = refs[4:]
        fold = fold_in[...]
    fold = jnp.maximum(fold, 1.0)
    left = low_lanes((CXL, 128))
    for a in range(CIL // 4):
        here = slice(a * CXL, (a + 1) * CXL)
        columns = []
        for q in range(4):
            lane = q * (CIL // 4) + a
            columns.append(
                jnp.concatenate(
                    [fold[:, 32 * j + lane : 32 * j + lane + 1] for j in range(3)], axis=0
                )
            )
        for side in range(2):
            lanes = slice(128 * side, 128 * side + 128)
            total = (parts[0][here, lanes] + parts[1][here, lanes]) + (
                parts[2][here, lanes] + parts[3][here, lanes]
            )
            value = total / jnp.where(left, columns[2 * side], columns[2 * side + 1])
            packed[here, lanes] = value.astype(jnp.bfloat16)
            if half == 0:
                value_out[here, lanes] = value
            else:
                earlier = before[here, lanes]
                even, odd = 2 * side * QUARTER + a * CXL, (2 * side + 1) * QUARTER + a * CXL
                image[even : even + CXL] = jnp.where(left, earlier, swap_lanes(value))
                image[odd : odd + CXL] = jnp.where(left, swap_lanes(earlier), value)


def image_call(half, parts, extra):
    packed = jax.ShapeDtypeStruct((QUARTER, 256), jnp.bfloat16)
    if half == 0:
        out_shape = [
            packed,
            jax.ShapeDtypeStruct((QUARTER, 256), jnp.float32),
            jax.ShapeDtypeStruct((FOLD, 256), jnp.float32),
        ]
    else:
        out_shape = [packed, jax.ShapeDtypeStruct((CELLS, 128), jnp.float32)]
    return pl.pallas_call(
        functools.partial(image_kernel, half),
        out_shape=out_shape,
        in_specs=[IN_VMEM] * (len(parts) + len(extra)),
        out_specs=[IN_VMEM] * len(out_shape),
        name=f"image_{half}",
    )(*parts, *extra)


def read_kernel(spec, order, counts, blocks, cells, own, *refs):
    sizes, half, first, last = spec
    group = 4
    tiles = sum(sizes) // QUARTER
    pieces = refs[: len(sizes)]
    refs = refs[len(sizes) :]
    if last:
        matrices, refs = refs[0], refs[1:]
    if not first:
        before, refs = refs[0], refs[1:]
    out, held, mine, total, sems = refs
    copies = [pltpu.make_async_copy(own, mine, sems.at[0])]
    start = 0
    for i, rows in enumerate(sizes):
        copies.append(
            pltpu.make_async_copy(pieces[i], held.at[pl.ds(start, rows)], sems.at[i + 1])
        )
        start += rows
    for copy in copies:
        copy.start()
    total[...] = jnp.zeros_like(total) if first else before[...]
    for copy in copies:
        copy.wait()
    left = low_lanes((128, 128))
    inside = left if half == 0 else jnp.logical_not(left)

    def tile_step(j, unused):
        tile = order[j]
        n = counts[tile]
        rows = cells[pl.ds(pl.multiple_of(tile * 8, 8), 8), :]
        quarters = quarter_of(rows)
        columns = (rows - QUARTER * quarters).T
        spots = quarters.T
        image = held[pl.ds(pl.multiple_of(j * QUARTER, QUARTER), QUARTER), :]
        for g in range(8 // group):

            @pl.when(n > g * group)
            def _():
                picks = [columns[:, g * group + i : g * group + i + 1] for i in range(group)]
                selector = jnp.concatenate(
                    [hot(pick, (128, QUARTER), 1) for pick in picks], axis=0
                )
                got = jnp.dot(selector, image, preferred_element_type=jnp.float32)
                for i, pick in enumerate(picks):
                    start = blocks[tile * 8 + g * group + i] * 128
                    here = pl.ds(pl.multiple_of(start, 128), 128)
                    spot = spots[:, g * group + i : g * group + i + 1]
                    part = got[i * 128 : (i + 1) * 128]
                    value = jnp.where(spot >= 2, part[:, 128:], part[:, :128])
                    stay = (spot & 1) == half
                    value = jnp.where(stay, value, swap_lanes(value))
                    sent = jnp.where(pick >= 0, mine[here, :].astype(jnp.float32), 0.0)
                    total[here, :] += jnp.where(inside, sent - value, 0.0)

        return 0

    lax.fori_loop(0, tiles, tile_step, 0)
    if not last:
        out[...] = total[...]
        return
    surveys = matrices.shape[0]
    rows = total.shape[0] // surveys
    sends = []
    for survey in range(surveys):
        here = slice(survey * rows, (survey + 1) * rows)
        total[here] = lax.dot_general(
            total[here].astype(jnp.bfloat16),
            matrices[survey],
            (((1,), (1,)), ((), ())),
            preferred_element_type=jnp.float32,
        )
        sends.append(
            pltpu.make_async_copy(
                total.at[pl.ds(survey * rows, rows)],
                out.at[pl.ds(survey * rows, rows)],
                sems.at[len(sizes) + 1 + survey],
            )
        )
        sends[-1].start()
    for send in sends:
        send.wait()


def read_call(half, order, slots, own, pieces, before, matrices=None):
    first, last = before is None, matrices is not None
    sizes = tuple(piece.shape[0] for piece in pieces)
    extra = ([matrices] if last else []) + ([] if first else [before])
    surveys = matrices.shape[0] if last else 0
    tiles = sum(sizes) // QUARTER
    return pl.pallas_call(
        functools.partial(read_kernel, (sizes, half, first, last)),
        out_shape=jax.ShapeDtypeStruct(own.shape, jnp.float32),
        in_specs=[IN_SMEM] * 3
        + [IN_VMEM]
        + [IN_ANY] * (1 + len(pieces))
        + [IN_VMEM] * len(extra),
        out_specs=IN_ANY if last else IN_VMEM,
        scratch_shapes=[
            pltpu.VMEM((sum(sizes), 256), jnp.bfloat16),
            pltpu.VMEM(own.shape, jnp.bfloat16),
            pltpu.VMEM(own.shape, jnp.float32),
            pltpu.SemaphoreType.DMA((len(sizes) + 1 + surveys,)),
        ],
        compiler_params=pltpu.CompilerParams(vmem_limit_bytes=32 * MIB),
        cost_estimate=pl.CostEstimate(
            flops=tiles * 4 * 2 * QUARTER * 128 * 256,
            bytes_accessed=8 * MIB,
            transcendentals=0,
        ),
        name="read",
    )(order, *slots, own, *pieces, *extra)


def with_halo(block, sides, width):
    for axis, count, dim in sides:
        forward = [(i, i + 1) for i in range(count - 1)]
        backward = [(target, source) for source, target in forward]
        low = lax.ppermute(
            lax.slice_in_dim(block, block.shape[dim] - width, None, axis=dim), axis, forward
        )
        high = lax.ppermute(lax.slice_in_dim(block, 0, width, axis=dim), axis, backward)
        block = jnp.concatenate([low, block, high], axis=dim)
    return block


def cycle_box(values, rows_out, cols_out):
    box_total = jnp.zeros((rows_out, cols_out, values.shape[2]), jnp.float32)
    for row_shift in range(3):
        for col_shift in range(3):
            box_total = (
                box_total
                + values[row_shift : row_shift + rows_out, col_shift : col_shift + cols_out]
            )
    return box_total / 9.0


def tensor(tile_image, il, xl):
    axis_il, count_il, at_il = il
    axis_xl, count_xl, at_xl = xl
    padded = with_halo(tile_image, ((axis_il, count_il, 0), (axis_xl, count_xl, 1)), 2)
    padded_time = jnp.pad(padded, ((0, 0), (0, 0), (1, 1)))
    grad_il = (padded[2:, 1:-1] - padded[:-2, 1:-1]) * 0.5
    grad_xl = (padded[1:-1, 2:] - padded[1:-1, :-2]) * 0.5
    grad_time = (padded_time[1:-1, 1:-1, 2:] - padded_time[1:-1, 1:-1, :-2]) * 0.5
    rows_il = at_il * CIL + jnp.arange(CIL + 2, dtype=jnp.int32) - 1
    rows_xl = at_xl * CXL + jnp.arange(CXL + 2, dtype=jnp.int32) - 1
    inside_il = ((rows_il >= 0) & (rows_il < CIL * count_il)).astype(jnp.float32)
    inside_xl = ((rows_xl >= 0) & (rows_xl < CXL * count_xl)).astype(jnp.float32)
    cycle_mask = inside_il[:, None, None] * inside_xl[None, :, None]
    factor_pairs = (
        (grad_il, grad_il),
        (grad_xl, grad_xl),
        (grad_time, grad_time),
        (grad_il, grad_xl),
        (grad_il, grad_time),
        (grad_xl, grad_time),
    )
    return jnp.stack(
        [
            cycle_box(left_part * right_part * cycle_mask, CIL, CXL)
            for left_part, right_part in factor_pairs
        ]
    )


SWAP = [(0, 1), (1, 0)]


def over(axis, value):
    return lax.ppermute(value, axis, SWAP)


def along_z(value, step):
    return lax.ppermute(value, "z", [(i, (i + step) % 4) for i in range(4)])


def local_planes(traces, filter_taps, slot_block, slot_cells, pair_count):
    row_block = slot_cells.shape[3]
    capacity = slot_block.shape[2]
    samples = traces.shape[1]
    surveys, tap_count = filter_taps.shape
    x, core, z, y = (lax.axis_index(name) for name in ("x", "c", "z", "y"))
    other = 1 - core

    slot_live = jnp.arange(capacity, dtype=jnp.int32)[None, :] < pair_count[0][:, None]
    out_cells = jnp.where(slot_live[:, :, None], slot_cells[0], -1)
    numbers = jnp.concatenate([slot_block[0], pair_count[0][:, None]], axis=1)
    numbers = jnp.pad(numbers, ((0, 0), (0, row_block - 8)))
    slots = jnp.concatenate([out_cells, numbers[:, None, :]], axis=1)
    by_column = slots.reshape(2, 2, 4, 2, 8, row_block).transpose(0, 1, 3, 2, 4, 5)
    arrived = lax.all_to_all(
        by_column.reshape(8, 4, 8, row_block), ("x", "c", "y"), 0, 0, tiled=True
    )
    in_numbers = arrived[:, :, 7, :8].reshape(32, 8)
    in_slots = (in_numbers[:, 7], in_numbers.reshape(256), arrived.reshape(256, row_block))
    own_cells = jnp.pad(out_cells, ((0, 0), (0, 1), (0, 0)), constant_values=-1)
    own_slots = (pair_count[0], numbers[:, :8].reshape(256), own_cells.reshape(256, row_block))

    taps = jnp.pad(filter_taps, ((0, 0), (0, samples - tap_count))).reshape(surveys, 1, samples)
    rows_half = traces.shape[0] // 2
    first_half, matrices = filter_call(0, traces, taps)
    second_half, filtered = filter_call(1, traces, taps)
    filtered = filtered.reshape(traces.shape)

    def column(*sources):
        return jnp.stack([(at_x * 2 + at_core) * 2 + at_y for at_x, at_core, at_y in sources])

    def tile_at(at_x, at_core, step, at_y):
        return ((at_x * 2 + at_core) * 4 + lax.rem(z + 4 - step, 4)) * 2 + at_y

    tile_order = jnp.stack([lax.rem(z + step, 4) for step in range(4)])
    near = column(
        (x, core, y),
        (x, other, y),
        (1 - x, core, y),
        (1 - x, other, y),
        (x, core, 1 - y),
        (x, other, 1 - y),
    )
    far = column((1 - x, core, 1 - y), (1 - x, other, 1 - y))

    def spread(value):
        middle = value.shape[0] // 2
        from_x, from_y = over("x", value), over("y", value)
        return from_x, from_y, over("y", from_x[:middle]), over("x", from_y[middle:])

    residual = None
    ready = None
    stacked = None
    gathered = []
    for half, packed in enumerate((first_half, second_half)):
        packed = packed.reshape(rows_half, samples)
        if half == 1:
            packed = tie(packed, ready)
        from_x, from_y, part0, part1 = spread(packed)
        pieces = []
        for piece in (packed, from_x, from_y):
            pieces += [piece, over("c", piece)]
        (ready,) = stack_call((tile_order, near), in_slots, pieces, 6, None, 4, half == 0, False)
        part0, part1 = tie(part0, ready), tie(part1, ready)
        pieces = [part0, part1, over("c", part0), over("c", part1)]
        partial = stack_call((tile_order, far), in_slots, pieces, 2, ready, 4, half == 0, True)
        totals = [partial[0]] + [along_z(partial[step], step) for step in (2, 1, 3)]
        if half == 0:
            packed_image, stacked, fold = image_call(0, totals, [])
        else:
            packed_image, image = image_call(1, totals, [fold, stacked])
        layers = [packed_image] + [along_z(packed_image, step) for step in (1, 2, 3)]
        layers = jnp.concatenate(layers, axis=0)
        gathered.append((layers,) + spread(layers))

    structure_tensor = tensor(
        image.reshape(CIL, CXL, samples),
        (("x", "c"), 4, x * 2 + core),
        (("z", "y"), 8, z * 2 + y),
    )

    spots = (
        (x, y, (0, 1, 2, 3)),
        (1 - x, y, (0, 1, 2, 3)),
        (x, 1 - y, (0, 1, 2, 3)),
        (1 - x, 1 - y, (0, 1)),
        (1 - x, 1 - y, (2, 3)),
    )

    def read(half, parts, before, last=None):
        pieces, order = [], []
        for part in parts:
            at_x, at_y, steps = spots[part]
            piece = gathered[half][part]
            if half == 1 and part >= 3:
                piece = tie(piece, before)
            pieces += [piece, over("c", piece)]
            order += [tile_at(at_x, core, step, at_y) for step in steps]
            order += [tile_at(at_x, other, step, at_y) for step in steps]
        return read_call(
            half, jnp.stack(order), own_slots, filtered, pieces, before, last
        )

    residual = read(0, (0, 1, 2, 3, 4), None)
    residual = read(1, (0,), residual)
    residual = read(1, (1, 2), residual)
    adjoint_traces = read(1, (3, 4), residual, matrices)
    return (structure_tensor, adjoint_traces)


def filter_matrices(filter_taps, samples):
    lag_table = (
        jnp.arange(samples, dtype=jnp.int32)[None, :]
        - jnp.arange(samples, dtype=jnp.int32)[:, None]
    )
    tap_count = filter_taps.shape[1]
    inside = (lag_table >= 0) & (lag_table < tap_count)
    picked = filter_taps[:, jnp.clip(lag_table, 0, tap_count - 1)]
    return jnp.where(inside[None], picked, 0.0).astype(jnp.bfloat16)


def local(traces, filter_taps, slot_block, slot_cells, pair_count):
    count_il = lax.axis_size("il")
    count_xl = lax.axis_size("xl")
    devices = count_il * count_xl
    samples = traces.shape[1]
    row_block = slot_cells.shape[3]
    capacity = slot_block.shape[2]
    surveys = filter_taps.shape[0]
    blocks_here = traces.shape[0] // row_block
    cell_count = CIL * CXL
    group_size = 16
    slot_total = devices * capacity
    group_count = slot_total // group_size
    matrices = filter_matrices(filter_taps, samples)
    by_survey = traces.reshape(surveys, blocks_here // surveys * row_block, samples)
    filtered = jnp.einsum("sru,sut->srt", by_survey, matrices, preferred_element_type=jnp.float32)
    filtered = filtered.astype(jnp.bfloat16).reshape(blocks_here, row_block, samples)
    block_ids = slot_block[0].reshape(-1)
    outgoing = jnp.take(filtered, block_ids, axis=0).reshape(devices, capacity, row_block, samples)
    slot_live = jnp.arange(capacity, dtype=jnp.int32)[None, :] < pair_count[0][:, None]
    out_cells = jnp.where(slot_live[:, :, None], slot_cells[0], -1)
    incoming, in_cells = (
        lax.all_to_all(outgoing, ("il", "xl"), split_axis=0, concat_axis=0, tiled=True),
        lax.all_to_all(out_cells, ("il", "xl"), split_axis=0, concat_axis=0, tiled=True),
    )
    incoming = incoming.reshape(slot_total, row_block, samples)
    in_cells = in_cells.reshape(slot_total, row_block)
    cell_line = jnp.arange(cell_count, dtype=jnp.int32)

    def one_hot(group_cells):
        return (cell_line[:, None] == group_cells.reshape(1, -1)).astype(jnp.bfloat16)

    def add_group(running, group_blocks, group_cells):
        stacked, fold_counts = running
        selector = one_hot(group_cells)
        stacked = stacked + jnp.dot(
            selector, group_blocks.reshape(-1, samples), preferred_element_type=jnp.float32
        )
        fold_counts = fold_counts + jnp.sum(selector, axis=1, dtype=jnp.float32)
        return (stacked, fold_counts)

    initial = (jnp.zeros((cell_count, samples), jnp.float32), jnp.zeros((cell_count,), jnp.float32))

    def scan_step(running, scan_item):
        return (add_group(running, scan_item[0], scan_item[1]), None)

    (stacked, fold_counts), unused = lax.scan(
        scan_step,
        initial,
        (
            incoming.reshape(group_count, group_size, row_block, samples),
            in_cells.reshape(group_count, group_size, row_block),
        ),
    )
    stack_image = stacked / jnp.maximum(fold_counts, 1.0)[:, None]
    image_half = stack_image.astype(jnp.bfloat16)

    def read_group(group_cells):
        selector = one_hot(group_cells)
        picked = lax.dot_general(
            selector, image_half, (((0,), (0,)), ((), ())), preferred_element_type=jnp.float32
        )
        return picked.astype(jnp.bfloat16).reshape(group_size, row_block, samples)

    answer = lax.map(read_group, in_cells.reshape(group_count, group_size, row_block)).reshape(
        slot_total, row_block, samples
    )
    returned = lax.all_to_all(
        answer.reshape(devices, capacity, row_block, samples),
        ("il", "xl"),
        split_axis=0,
        concat_axis=0,
        tiled=True,
    )
    returned = returned.reshape(slot_total, row_block, samples)
    out_valid = (out_cells >= 0).reshape(slot_total, row_block, 1)
    zero_half = jnp.zeros((), jnp.bfloat16)
    sent_part = jnp.where(out_valid, outgoing.reshape(slot_total, row_block, samples), zero_half)
    back_part = jnp.where(out_valid, returned, zero_half)
    selector_rows = (
        block_ids[:, None] == jnp.arange(blocks_here, dtype=jnp.int32)[None, :]
    ).astype(jnp.bfloat16)
    residual = jnp.einsum(
        "sb,sit->bit", selector_rows, sent_part, preferred_element_type=jnp.float32
    )
    residual = residual - jnp.einsum(
        "sb,sit->bit", selector_rows, back_part, preferred_element_type=jnp.float32
    )
    residual_half = residual.astype(jnp.bfloat16).reshape(surveys, -1, samples)
    adjoint_traces = jnp.einsum(
        "srt,sut->sru", residual_half, matrices, preferred_element_type=jnp.float32
    ).reshape(traces.shape)
    structure_tensor = tensor(
        stack_image.reshape(CIL, CXL, samples),
        ("il", count_il, lax.axis_index("il")),
        ("xl", count_xl, lax.axis_index("xl")),
    )
    return (structure_tensor, adjoint_traces)


def solution(mesh):
    inner, names, body = mesh, (("il",), ("xl",)), local
    if mesh.devices.shape == (4, 8):
        inner = Mesh(mesh.devices.reshape(2, 2, 4, 2), ("x", "c", "z", "y"))
        names, body = (("x", "c"), ("z", "y")), local_planes
    il, xl = names
    both = il + xl
    return jax.shard_map(
        body,
        mesh=inner,
        in_specs=(
            P(both, None),
            P(),
            P(both, None, None),
            P(both, None, None, None),
            P(both, None),
        ),
        out_specs=(P(None, il, xl, None), P(both, None)),
        check_vma=False,
    )
```

time: 340 us -> 361 us (1.062)
  waiting for transfers between devices: 169 us -> 105 us
  Pallas kernels: 77.5 us -> 116 us
  starting transfers between devices: 47 us -> 83.6 us
  local copies, waits for them, and re-layouts: 15.7 us -> 35.4 us
  between operations: 14.6 us -> 1.46 us
  other arithmetic: 12.1 us -> 17.5 us
    reduce_scatter x1 -> x0, waiting for transfers between devices: 70.1 us -> none  [local_planes(): total = lax.psum_scatter(stack, 'z', scatter_dimension=0, tiled=True)[0]]
    pallas_call x10 -> x19, Pallas kernels: 77.5 us -> 116 us  [the longest x4 63.1 us: read_call(): pl.pallas_call(functools.partial(read_kernel, (sizes, half, first, last))...]
    ppermute x42 -> x36, waiting for transfers between devices: 71.4 us -> 38.7 us  [over(): return lax.ppermute(value, axis, SWAP)]
    ppermute x3 -> x12, waiting for transfers between devices: 23.9 us -> 56.4 us  [along_z(): return lax.ppermute(value, 'z', [(i, (i + step) % 4) for i in range(4)])]
    ppermute x3 -> x12, starting transfers between devices: 6.98 us -> 38.5 us  [along_z(): return lax.ppermute(value, 'z', [(i, (i + step) % 4) for i in range(4)])]
    unnamed x37 -> x75, local copies, waits for them, and re-layouts: 12.6 us -> 22.5 us
    slice x1 -> x9, local copies, waits for them, and re-layouts: 0.18 us -> 8.37 us  [the longest x4 4.5 us: spread(): from_y[middle:]]
    unnamed x6, other arithmetic: 3.03 us -> 8.39 us
  transfers between devices with their start and end apart: 51 -> 53, of which waited for: 16 -> 14; matrix products, arithmetic and copies ran while one was open for 5% -> 9% of each run, Pallas kernels for 13% -> 28%
where the time goes in v2:
time: 361 us; the launch traced here: 359 us
  Pallas kernels  116 us (32%)
  waiting for transfers between devices  105 us (29%)
  starting transfers between devices  83.6 us (23%)
  local copies, waits for them, and re-layouts  35.4 us (10%)
  other arithmetic  17.5 us (5%)
    pallas_call x4, Pallas kernels, read_call(): pl.pallas_call(functools.partial(read_kernel, (sizes, half, first, last))...  63.1 us
    ppermute x12, waiting for transfers between devices, along_z(): return lax.ppermute(value, 'z', [(i, (i + step) % 4) for i in range(4)])  56.4 us
    ppermute x36, waiting for transfers between devices, over(): return lax.ppermute(value, axis, SWAP)  38.7 us
    ppermute x12, starting transfers between devices, along_z(): return lax.ppermute(value, 'z', [(i, (i + step) % 4) for i in range(4)])  38.5 us
    pallas_call x4, Pallas kernels, stack_call(): pl.pallas_call(functools.partial(stack_kernel, (sizes, sources, tiles, wi...  38 us
    ppermute x36, starting transfers between devices, over(): return lax.ppermute(value, axis, SWAP)  30.9 us
    unnamed x75, local copies, waits for them, and re-layouts  22.5 us
    pallas_call x2, Pallas kernels, filter_call(): pl.pallas_call(functools.partial(filter_kernel, half), grid=(surveys // e...  8.85 us
  transfers between devices with their start and end apart: 53, of which 14 were waited for; matrix products, arithmetic and copies ran while one was open for 9% of the time, Pallas kernels for 28%

profile of v2, /device:TPU:0, one launch (start us, length us, event | category | flops | bytes accessed | tf_op | source)
XLA Modules:
  0.0 359.1 jit_solution(17111214255640714710)
XLA Ops:
  1.9 4.3 %filter_0.1 = (bf16[12,320,128]{2,1,0:T(8,128)(2,1)}, bf16[12,128,128]{2,1,0:T(8,128)(2,1)}) custom-call(f32[12,1,128]{2,1,0:T(1,128)} %reshape.127.taps, bf16[12,640,128]{2,1,0:T(8,128)(2,1)} %bitcast.116), custom_call_target="tpu_custom_call" | custom-call | tf_op jit(solution)/shard_map/filter_0/pallas_call | solution.py:82
  6.2 3.0 collective-permute-start.3
  9.2 1.5 collective-permute-start.1
  10.7 20.5 %collective-permute-done.3.refs_4_ = bf16[3840,128]{1,0:T(8,128)(2,1)S(1)} collective-permute-done((bf16[3840,128]{1,0:T(8,128)(2,1)}, bf16[3840,128]{1,0:T(8,128)(2,1)S(1)}, u32[]{:S(2)}, u32[]{:S(2)}) %collective-permute-start.3) | collective-permute-done | bytes 983072 | tf_op jit(solution)/shard_map/ppermute | solution.py:443
  31.2 1.5 collective-permute-done.1.refs_2_
  33.8 1.3 reduce.5
  38.6 1.5 collective-permute-start.18
  42.4 3.4 all-to-all-start
  45.8 4.5 %filter_1.1 = (bf16[12,320,128]{2,1,0:T(8,128)(2,1)}, bf16[12,640,128]{2,1,0:T(8,128)(2,1)}) custom-call(f32[12,1,128]{2,1,0:T(1,128)} %reshape.127.taps, bf16[12,640,128]{2,1,0:T(8,128)(2,1)} %bitcast.117), custom_call_target="tpu_custom_call" | custom-call | tf_op jit(solution)/shard_map/filter_1/pallas_call | solution.py:82
  50.5 5.2 %all-to-all-done = s32[8,4,8,128]{3,1,2,0:T(4,128)S(1)} async-done(((s32[8,4,8,128]{3,1,2,0:T(4,128)}), s32[8,4,8,128]{3,1,2,0:T(4,128)S(1)}, u32[]{:S(2)}, u32[]{:S(2)}) %all-to-all-start) | async-done | bytes 131104 | tf_op jit(solution)/shard_map/all_to_all | solution.py:464
  56.1 1.2 copy-done.11
  57.3 1.2 copy-done.14
  58.5 12.7 %stack.268.refs_1_.refs_4_ = f32[4,400,256]{2,1,0:T(8,128)S(1)} custom-call(s32[4]{0:T(128)S(1)} %pad_add_fusion.2.tile_order, s32[6]{0:T(128)S(1)} %stack.224.source_order, s32[32]{0:T(128)S(1)} %slice_reduce_fusion.counts, s32[256]{0:T(256)S(1)} %reshape_reshape_squeeze.3.blocks, s32[256,128]{1,0:T(8,128)S(1)} %bitcast.98, ...), custom_call_target="tpu_custom_call" | custom-call | flops 1207959552 | bytes 10092544 | tf_op jit(solution)/shard_map/stack/pallas_call | solution.py:197
  71.2 1.2 copy-done.2
  73.7 3.2 collective-permute-start.5
  77.0 5.8 %stack.271 = (f32[400,256]{1,0:T(8,128)S(1)}, f32[400,256]{1,0:T(8,128)S(1)}, f32[400,256]{1,0:T(8,128)S(1)}, f32[400,256]{1,0:T(8,128)S(1)}) custom-call(s32[4]{0:T(128)S(1)} %pad_add_fusion.2.tile_order, s32[2]{0:T(128)S(1)} %pad_add_fusion.3.source_order, s32[32]{0:T(128)S(1)} %slice_reduce_fusion.counts, s32[256]{0:T(256)S(1)} %reshape_reshape_squeeze.3.blocks, ...), custom_call_target="tpu_custom_call" | custom-call | flops 402653184 | bytes 6160384 | tf_op jit(solution)/shard_map/stack/pallas_call | solution.py:197
  83.6 3.5 collective-permute-start.21
  87.2 3.7 %collective-permute-start.23 = (f32[400,256]{1,0:T(8,128)S(1)}, f32[400,256]{1,0:T(8,128)S(1)}, u32[]{:S(2)}, u32[]{:S(2)}) collective-permute-start(f32[400,256]{1,0:T(8,128)S(1)} %get-tuple-element.28), channel_id=1, source_target_pairs={{0,6},{2,0},{4,2},{6,4},{1,7},{3,1},{5,3},{7,5},{8,14},{10,8},{12,... | collective-permute-start | bytes 1228808 | tf_op jit(solution)/shard_map/ppermute | solution.py:447
  90.9 23.8 %collective-permute-done.21.refs_1_ = f32[400,256]{1,0:T(8,128)S(1)} collective-permute-done((f32[400,256]{1,0:T(8,128)S(1)}, f32[400,256]{1,0:T(8,128)S(1)}, u32[]{:S(2)}, u32[]{:S(2)}) %collective-permute-start.21) | collective-permute-done | bytes 409632 | tf_op jit(solution)/shard_map/ppermute | solution.py:447
  116.7 2.6 image_0.1
  119.2 7.7 %collective-permute-start.37 = (bf16[384,256]{1,0:T(8,128)(2,1)}, bf16[384,256]{1,0:T(8,128)(2,1)S(1)}, u32[]{:S(2)}, u32[]{:S(2)}) collective-permute-start(bf16[384,256]{1,0:T(8,128)(2,1)} %get-tuple-element.34), channel_id=1, source_target_pairs={{0,2},{2,4},{4,6},{6,0},{1,3},{3,5},{5,7},{7,1},{8,10},{10,12},{12... | collective-permute-start | bytes 589832 | tf_op jit(solution)/shard_map/ppermute | solution.py:447
  127.0 5.6 %collective-permute-done.37 = bf16[384,256]{1,0:T(8,128)(2,1)S(1)} collective-permute-done((bf16[384,256]{1,0:T(8,128)(2,1)}, bf16[384,256]{1,0:T(8,128)(2,1)S(1)}, u32[]{:S(2)}, u32[]{:S(2)}) %collective-permute-start.37) | collective-permute-done | bytes 196640 | tf_op jit(solution)/shard_map/ppermute | solution.py:447
  132.6 10.1 %collective-permute-start.38 = (bf16[384,256]{1,0:T(8,128)(2,1)}, bf16[384,256]{1,0:T(8,128)(2,1)S(1)}, u32[]{:S(2)}, u32[]{:S(2)}) collective-permute-start(bf16[384,256]{1,0:T(8,128)(2,1)} %get-tuple-element.34), channel_id=1, source_target_pairs={{0,4},{2,6},{4,0},{6,2},{1,5},{3,7},{5,1},{7,3},{8,12},{10,14},{12... | collective-permute-start | bytes 589832 | tf_op jit(solution)/shard_map/ppermute | solution.py:447
  142.7 1.6 constant_dynamic-update-slice_fusion.7
  144.3 1.8 slice.310
  146.1 1.1 slice.309
  147.9 1.7 collective-permute-start.11
  152.1 1.9 collective-permute-start.43
  154.7 1.2 copy-done.16
  155.9 12.8 %stack.269.refs_1_.refs_4_ = f32[4,384,256]{2,1,0:T(8,128)S(1)} custom-call(s32[4]{0:T(128)S(1)} %pad_add_fusion.2.tile_order, s32[6]{0:T(128)S(1)} %stack.224.source_order, s32[32]{0:T(128)S(1)} %slice_reduce_fusion.counts, s32[256]{0:T(256)S(1)} %reshape_reshape_squeeze.3.blocks, s32[256,128]{1,0:T(8,128)S(1)} %bitcast.100, ...), custom_call_target="tpu_custom_call" | custom-call | flops 1207959552 | bytes 10092544 | tf_op jit(solution)/shard_map/stack/pallas_call | solution.py:197
  168.7 1.1 copy-done.5
  170.4 1.7 collective-permute-done.43.refs_4_
  172.1 1.8 slice.371
  173.9 3.6 collective-permute-start.47
  177.5 1.8 slice.370
  179.2 1.7 collective-permute-start.45
  182.6 6.7 %stack.270 = (f32[384,256]{1,0:T(8,128)S(1)}, f32[384,256]{1,0:T(8,128)}, f32[384,256]{1,0:T(8,128)}, f32[384,256]{1,0:T(8,128)}) custom-call(s32[4]{0:T(128)S(1)} %pad_add_fusion.2.tile_order, s32[2]{0:T(128)S(1)} %copy-done.22, s32[32]{0:T(128)S(1)} %slice_reduce_fusion.counts, s32[256]{0:T(256)S(1)} %reshape_reshape_squeeze.3.blocks, ...), custom_call_target="tpu_custom_call" | custom-call | flops 402653184 | bytes 6160384 | tf_op jit(solution)/shard_map/stack/pallas_call | solution.py:197
  190.1 5.8 %collective-permute-start.15 = (f32[384,256]{1,0:T(8,128)}, f32[384,256]{1,0:T(8,128)}, u32[]{:S(2)}, u32[]{:S(2)}) collective-permute-start(f32[384,256]{1,0:T(8,128)} %get-tuple-element.23), channel_id=1, source_target_pairs={{0,2},{2,4},{4,6},{6,0},{1,3},{3,5},{5,7},{7,1},{8,10},{10,12},{12... | collective-permute-start | bytes 1179656 | tf_op jit(solution)/shard_map/ppermute | solution.py:447
  197.0 22.8 %collective-permute-done.14.refs_1_ = f32[384,256]{1,0:T(8,128)S(1)} collective-permute-done((f32[384,256]{1,0:T(8,128)}, f32[384,256]{1,0:T(8,128)S(1)}, u32[]{:S(2)}, u32[]{:S(2)}) %collective-permute-start.14) | collective-permute-done | bytes 393248 | tf_op jit(solution)/shard_map/ppermute | solution.py:447
  219.8 1.1 bitcast_select_fusion
  223.5 3.7 %image_1.1 = (bf16[384,256]{1,0:T(8,128)(2,1)}, f32[1536,128]{1,0:T(8,128)}) custom-call(f32[384,256]{1,0:T(8,128)} %copy-done.19, f32[384,256]{1,0:T(8,128)} %copy-done.28, f32[384,256]{1,0:T(8,128)} %collective-permute-done.15.refs_2_, f32[384,256]{1,0:T(8,128)} %collective-permute-done.16.refs_3_, f32[16,256]{1,0:T(8,128)} %get-tuple-element.29.refs_4_, ...), custom_call_target="tpu_custom_call" | custom-call | tf_op jit(solution)/shard_map/image_1/pallas_call | solution.py:265
  228.1 1.3 collective-permute-start.25
  229.4 3.0 collective-permute-start.24
  232.5 29.6 %read.4.refs_2_ = f32[7680,128]{1,0:T(8,128)S(1)} custom-call(s32[32]{0:T(128)S(1)} %stack.267.order, s32[32]{0:T(128)S(1)} %bitcast.108, s32[256]{0:T(256)S(1)} %reshape.132.blocks, s32[256,128]{1,0:T(8,128)S(1)} %pad_bitcast_fusion.cells, bf16[7680,128]{1,0:T(8,128)(2,1)S(1)} %bitcast.93, bf16[1536,256]{1,0:T(8,128)(2,1)} %constant_dynamic-update-slice_fusion.4.refs_0_, ...), custom_call_target="tpu_custom_call" | custom-call | flops 3221225472 | bytes 8388608 | tf_op jit(solution)/shard_map/read/pallas_call | solution.py:363
  262.1 1.1 collective-permute-start.30
  263.2 4.4 %collective-permute-start.29 = (bf16[384,256]{1,0:T(8,128)(2,1)S(1)}, bf16[384,256]{1,0:T(8,128)(2,1)S(1)}, u32[]{:S(2)}, u32[]{:S(2)}) collective-permute-start(bf16[384,256]{1,0:T(8,128)(2,1)S(1)} %copy-done.29), channel_id=1, source_target_pairs={{0,4},{2,6},{4,0},{6,2},{1,5},{3,7},{5,1},{7,3},{8,12},{10,14},{12... | collective-permute-start | bytes 589832 | tf_op jit(solution)/shard_map/ppermute | solution.py:447
  267.6 1.6 collective-permute-start.28
  269.2 5.2 %collective-permute-start.26 = (f32[36,2,128]{2,1,0:T(2,128)S(1)}, f32[36,2,128]{2,1,0:T(2,128)S(1)}, u32[]{:S(2)}, u32[]{:S(2)}) collective-permute-start(f32[36,2,128]{2,1,0:T(2,128)S(1)} %get-tuple-element.42), channel_id=1, source_target_pairs={{0,1},{1,2},{2,3},{3,4},{4,5},{5,6},{6,7},{8,9},{9,10},{10,11},{11... | collective-permute-start | bytes 110600 | tf_op jit(solution)/shard_map/ppermute | solution.py:391
  274.5 1.3 collective-permute-start.27
  276.1 4.2 %collective-permute-done.27 = f32[36,2,128]{2,1,0:T(2,128)S(1)} collective-permute-done((f32[36,2,128]{2,1,0:T(2,128)S(1)}, f32[36,2,128]{2,1,0:T(2,128)S(1)}, u32[]{:S(2)}, u32[]{:S(2)}) %collective-permute-start.27) | collective-permute-done | bytes 36896 | tf_op jit(solution)/shard_map/ppermute | solution.py:394
  280.9 3.1 collective-permute-done.29
  284.0 4.0 %collective-permute-start.34 = (bf16[1536,256]{1,0:T(8,128)(2,1)S(1)}, bf16[1536,256]{1,0:T(8,128)(2,1)S(1)}, u32[]{:S(2)}, u32[]{:S(2)}) collective-permute-start(bf16[1536,256]{1,0:T(8,128)(2,1)S(1)} %constant_dynamic-update-slice_fusion.refs_0_), channel_id=1, source_target_pairs={{0,1},{1,0},{2,3},{3,2},{4,5},{5,4},{6,7},{7,6},{8,9},{9,8},{10,11... | collective-permute-start | bytes 2359304 | tf_op jit(solution)/shard_map/ppermute | solution.py:443
  288.8 3.0 multiply_multiply_fusion
  292.7 13.6 %collective-permute-done.34.refs_2_ = bf16[1536,256]{1,0:T(8,128)(2,1)S(1)} collective-permute-done((bf16[1536,256]{1,0:T(8,128)(2,1)S(1)}, bf16[1536,256]{1,0:T(8,128)(2,1)S(1)}, u32[]{:S(2)}, u32[]{:S(2)}) %collective-permute-start.34) | collective-permute-done | bytes 786464 | tf_op jit(solution)/shard_map/ppermute | solution.py:443
  306.5 1.5 collective-permute-done.31.refs_0_
  310.1 2.2 copy-done.32
  312.2 7.7 %read.5.refs_4_ = f32[7680,128]{1,0:T(8,128)S(1)} custom-call(s32[8]{0:T(128)S(1)} %stack.266.order, s32[32]{0:T(128)S(1)} %bitcast.109, s32[256]{0:T(256)S(1)} %reshape.132.blocks, s32[256,128]{1,0:T(8,128)S(1)} %pad_bitcast_fusion.cells, bf16[7680,128]{1,0:T(8,128)(2,1)S(1)} %bitcast.94, bf16[1536,256]{1,0:T(8,128)(2,1)S(1)} %constant_dynamic-update-slice_fusion.refs_0_, ...), custom_call_target="tpu_custom_call" | custom-call | flops 805306368 | bytes 8388608 | tf_op jit(solution)/shard_map/read/pallas_call | solution.py:363
  320.0 15.1 %read.6.refs_1_.refs_5_ = f32[7680,128]{1,0:T(8,128)S(1)} custom-call(s32[16]{0:T(128)S(1)} %stack.257.order, s32[32]{0:T(128)S(1)} %bitcast.110, s32[256]{0:T(256)S(1)} %reshape.132.blocks, s32[256,128]{1,0:T(8,128)S(1)} %pad_bitcast_fusion.cells, bf16[7680,128]{1,0:T(8,128)(2,1)S(1)} %bitcast.95, bf16[1536,256]{1,0:T(8,128)(2,1)S(1)} %collective-permute-done.31.refs_0_, ...), custom_call_target="tpu_custom_call" | custom-call | flops 1610612736 | bytes 8388608 | tf_op jit(solution)/shard_map/read/pallas_call | solution.py:363
  335.1 1.9 copy-done
  337.8 2.0 collective-permute-start.49
  339.9 5.7 %fusion.10 = f32[6,32,48,128]{3,2,1,0:T(8,128)} fusion(f32[6,32,48,128]{3,2,1,0:T(8,128)} %copy-done.32, f32[34,50,128]{2,1,0:T(8,128)} %get-tuple-element.38), kind=kLoop, calls=%fused_computation.35 | loop fusion | flops 1769472 | bytes 7864320
  345.7 1.2 fusion.7
  346.9 1.1 copy-done.1
  348.2 10.7 %read.7 = f32[7680,128]{1,0:T(8,128)} custom-call(s32[8]{0:T(128)S(1)} %stack.240.order, s32[32]{0:T(128)S(1)} %bitcast.111, s32[256]{0:T(256)S(1)} %reshape.132.blocks, s32[256,128]{1,0:T(8,128)S(1)} %pad_bitcast_fusion.cells, bf16[7680,128]{1,0:T(8,128)(2,1)S(1)} %bitcast.96, bf16[768,256]{1,0:T(8,128)(2,1)S(1)} %copy-done.13, ...), custom_call_target="tpu_custom_call" | custom-call | flops 805306368 | bytes 8388608 | tf_op jit(solution)/shard_map/read/pallas_call | solution.py:363
  (187 shorter events, 30.2 us)
Async XLA Ops:
  6.2 24.9 %collective-permute-start.3 = (bf16[3840,128]{1,0:T(8,128)(2,1)}, bf16[3840,128]{1,0:T(8,128)(2,1)S(1)}, u32[]{:S(2)}, u32[]{:S(2)}) collective-permute-start(bf16[3840,128]{1,0:T(8,128)(2,1)} %bitcast.102), channel_id=1, source_target_pairs={{0,1},{1,0},{2,3},{3,2},{4,5},{5,4},{6,7},{7,6},{8,9},{9,8},{10,11... | collective-permute-start | bytes 2949128 | tf_op jit(solution)/shard_map/ppermute | solution.py:443
  9.2 23.4 %collective-permute-start.1 = (bf16[3840,128]{1,0:T(8,128)(2,1)}, bf16[3840,128]{1,0:T(8,128)(2,1)S(1)}, u32[]{:S(2)}, u32[]{:S(2)}) collective-permute-start(bf16[3840,128]{1,0:T(8,128)(2,1)} %bitcast.103), channel_id=1, source_target_pairs={{0,16},{16,0},{1,17},{17,1},{2,18},{18,2},{3,19},{19,3},{4,20},{20... | collective-permute-start | bytes 2949128 | tf_op jit(solution)/shard_map/ppermute | solution.py:443
  10.7 45.3 %collective-permute-start = (bf16[3840,128]{1,0:T(8,128)(2,1)}, bf16[3840,128]{1,0:T(8,128)(2,1)}, u32[]{:S(2)}, u32[]{:S(2)}) collective-permute-start(bf16[3840,128]{1,0:T(8,128)(2,1)} %bitcast.104), channel_id=1, source_target_pairs={{0,8},{8,0},{1,9},{9,1},{2,10},{10,2},{3,11},{11,3},{4,12},{12,4},... | collective-permute-start | bytes 2949128 | tf_op jit(solution)/shard_map/ppermute | solution.py:443
  31.2 24.8 %collective-permute-start.4 = (bf16[3840,128]{1,0:T(8,128)(2,1)S(1)}, bf16[3840,128]{1,0:T(8,128)(2,1)}, u32[]{:S(2)}, u32[]{:S(2)}) collective-permute-start(bf16[3840,128]{1,0:T(8,128)(2,1)S(1)} %collective-permute-done.3.refs_4_), channel_id=1, source_target_pairs={{0,8},{8,0},{1,9},{9,1},{2,10},{10,2},{3,11},{11,3},{4,12},{12,4},... | collective-permute-start | bytes 2949128 | tf_op jit(solution)/shard_map/ppermute | solution.py:443
  32.6 23.4 %copy-start.10 = (bf16[3840,128]{1,0:T(8,128)(2,1)}, bf16[3840,128]{1,0:T(8,128)(2,1)S(1)}, u32[]{:S(2)}) copy-start(bf16[3840,128]{1,0:T(8,128)(2,1)S(1)} %collective-permute-done.1.refs_2_) | copy-start | bytes 2949124
  32.6 23.4 %collective-permute-start.2 = (bf16[3840,128]{1,0:T(8,128)(2,1)S(1)}, bf16[3840,128]{1,0:T(8,128)(2,1)}, u32[]{:S(2)}, u32[]{:S(2)}) collective-permute-start(bf16[3840,128]{1,0:T(8,128)(2,1)S(1)} %collective-permute-done.1.refs_2_), channel_id=1, source_target_pairs={{0,8},{8,0},{1,9},{9,1},{2,10},{10,2},{3,11},{11,3},{4,12},{12,4},... | collective-permute-start | bytes 2949128 | tf_op jit(solution)/shard_map/ppermute | solution.py:443
  38.6 33.9 %collective-permute-start.18 = (bf16[1920,128]{1,0:T(8,128)(2,1)}, bf16[1920,128]{1,0:T(8,128)(2,1)}, u32[]{:S(2)}, u32[]{:S(2)}) collective-permute-start(bf16[1920,128]{1,0:T(8,128)(2,1)} %slice.312), channel_id=1, source_target_pairs={{0,16},{16,0},{1,17},{17,1},{2,18},{18,2},{3,19},{19,3},{4,20},{20... | collective-permute-start | bytes 1474568 | tf_op jit(solution)/shard_map/ppermute | solution.py:443
  40.9 31.6 %collective-permute-start.17 = (bf16[1920,128]{1,0:T(8,128)(2,1)}, bf16[1920,128]{1,0:T(8,128)(2,1)}, u32[]{:S(2)}, u32[]{:S(2)}) collective-permute-start(bf16[1920,128]{1,0:T(8,128)(2,1)} %slice.311), channel_id=1, source_target_pairs={{0,1},{1,0},{2,3},{3,2},{4,5},{5,4},{6,7},{7,6},{8,9},{9,8},{10,11... | collective-permute-start | bytes 1474568 | tf_op jit(solution)/shard_map/ppermute | solution.py:443
  42.4 13.3 %all-to-all-start = ((s32[8,4,8,128]{3,1,2,0:T(4,128)}), s32[8,4,8,128]{3,1,2,0:T(4,128)S(1)}, u32[]{:S(2)}, u32[]{:S(2)}) async-start(s32[8,4,8,128]{3,1,2,0:T(4,128)} %bitcast.10), calls=%async_computation | async-start | bytes 262144 | tf_op jit(solution)/shard_map/all_to_all | solution.py:464
  55.8 98.9 %copy-start.8 = (s32[8,4,8,128]{3,2,1,0:T(8,128)}, s32[8,4,8,128]{3,2,1,0:T(8,128)S(1)}, u32[]{:S(2)}) copy-start(s32[8,4,8,128]{3,2,1,0:T(8,128)S(1)} %copy.32) | copy-start | bytes 393220
  72.3 4.7 %copy-start.3 = (f32[4,400,256]{2,1,0:T(8,128)S(1)}, f32[4,400,256]{2,1,0:T(8,128)}, u32[]{:S(2)}) copy-start(f32[4,400,256]{2,1,0:T(8,128)} %copy-done.2) | copy-start | bytes 4915204
  72.3 42.3 %collective-permute-start.9 = (bf16[3840,128]{1,0:T(8,128)(2,1)}, bf16[3840,128]{1,0:T(8,128)(2,1)}, u32[]{:S(2)}, u32[]{:S(2)}) collective-permute-start(bf16[3840,128]{1,0:T(8,128)(2,1)} %tie.7.refs_0_), channel_id=1, source_target_pairs={{0,1},{1,0},{2,3},{3,2},{4,5},{5,4},{6,7},{7,6},{8,9},{9,8},{10,11... | collective-permute-start | bytes 2949128 | tf_op jit(solution)/shard_map/ppermute | solution.py:443
  72.5 4.5 %collective-permute-start.19 = (bf16[1920,128]{1,0:T(8,128)(2,1)}, bf16[1920,128]{1,0:T(8,128)(2,1)S(1)}, u32[]{:S(2)}, u32[]{:S(2)}) collective-permute-start(bf16[1920,128]{1,0:T(8,128)(2,1)} %tie.10.refs_0_), channel_id=1, source_target_pairs={{0,8},{8,0},{1,9},{9,1},{2,10},{10,2},{3,11},{11,3},{4,12},{12,4},... | collective-permute-start | bytes 1474568 | tf_op jit(solution)/shard_map/ppermute | solution.py:443
  72.5 4.5 %collective-permute-start.20 = (bf16[1920,128]{1,0:T(8,128)(2,1)}, bf16[1920,128]{1,0:T(8,128)(2,1)}, u32[]{:S(2)}, u32[]{:S(2)}) collective-permute-start(bf16[1920,128]{1,0:T(8,128)(2,1)} %tie.11.refs_1_), channel_id=1, source_target_pairs={{0,8},{8,0},{1,9},{9,1},{2,10},{10,2},{3,11},{11,3},{4,12},{12,4},... | collective-permute-start | bytes 1474568 | tf_op jit(solution)/shard_map/ppermute | solution.py:443
  73.7 41.5 %collective-permute-start.5 = (bf16[3840,128]{1,0:T(8,128)(2,1)S(1)}, bf16[3840,128]{1,0:T(8,128)(2,1)}, u32[]{:S(2)}, u32[]{:S(2)}) collective-permute-start(bf16[3840,128]{1,0:T(8,128)(2,1)S(1)} %copy-done.7), channel_id=1, source_target_pairs={{0,16},{16,0},{1,17},{17,1},{2,18},{18,2},{3,19},{19,3},{4,20},{20... | collective-permute-start | bytes 2949128 | tf_op jit(solution)/shard_map/ppermute | solution.py:443
  77.0 91.7 %copy-start.21 = (s32[2]{0:T(128)}, s32[2]{0:T(128)S(1)}, u32[]{:S(2)}) copy-start(s32[2]{0:T(128)S(1)} %pad_add_fusion.3.source_order) | copy-start | bytes 28
  83.6 31.1 %collective-permute-start.21 = (f32[400,256]{1,0:T(8,128)S(1)}, f32[400,256]{1,0:T(8,128)S(1)}, u32[]{:S(2)}, u32[]{:S(2)}) collective-permute-start(f32[400,256]{1,0:T(8,128)S(1)} %get-tuple-element.26), channel_id=1, source_target_pairs={{0,4},{2,6},{4,0},{6,2},{1,5},{3,7},{5,1},{7,3},{8,12},{10,14},{12... | collective-permute-start | bytes 1228808 | tf_op jit(solution)/shard_map/ppermute | solution.py:447
  87.0 28.2 %collective-permute-start.22 = (f32[400,256]{1,0:T(8,128)S(1)}, f32[400,256]{1,0:T(8,128)S(1)}, u32[]{:S(2)}, u32[]{:S(2)}) collective-permute-start(f32[400,256]{1,0:T(8,128)S(1)} %get-tuple-element.27), channel_id=1, source_target_pairs={{0,2},{2,4},{4,6},{6,0},{1,3},{3,5},{5,7},{7,1},{8,10},{10,12},{12... | collective-permute-start | bytes 1228808 | tf_op jit(solution)/shard_map/ppermute | solution.py:447
  87.2 28.7 %collective-permute-start.23 = (f32[400,256]{1,0:T(8,128)S(1)}, f32[400,256]{1,0:T(8,128)S(1)}, u32[]{:S(2)}, u32[]{:S(2)}) collective-permute-start(f32[400,256]{1,0:T(8,128)S(1)} %get-tuple-element.28), channel_id=1, source_target_pairs={{0,6},{2,0},{4,2},{6,4},{1,7},{3,1},{5,3},{7,5},{8,14},{10,8},{12,... | collective-permute-start | bytes 1228808 | tf_op jit(solution)/shard_map/ppermute | solution.py:447
  114.7 36.5 %collective-permute-start.7 = (bf16[3840,128]{1,0:T(8,128)(2,1)S(1)}, bf16[3840,128]{1,0:T(8,128)(2,1)S(1)}, u32[]{:S(2)}, u32[]{:S(2)}) collective-permute-start(bf16[3840,128]{1,0:T(8,128)(2,1)S(1)} %copy-done.7), channel_id=1, source_target_pairs={{0,8},{8,0},{1,9},{9,1},{2,10},{10,2},{3,11},{11,3},{4,12},{12,4},... | collective-permute-start | bytes 2949128 | tf_op jit(solution)/shard_map/ppermute | solution.py:443
  114.7 39.3 %collective-permute-start.10 = (bf16[3840,128]{1,0:T(8,128)(2,1)}, bf16[3840,128]{1,0:T(8,128)(2,1)}, u32[]{:S(2)}, u32[]{:S(2)}) collective-permute-start(bf16[3840,128]{1,0:T(8,128)(2,1)} %collective-permute-done.9.refs_4_), channel_id=1, source_target_pairs={{0,8},{8,0},{1,9},{9,1},{2,10},{10,2},{3,11},{11,3},{4,12},{12,4},... | collective-permute-start | bytes 2949128 | tf_op jit(solution)/shard_map/ppermute | solution.py:443
  115.2 39.5 %collective-permute-start.8 = (bf16[3840,128]{1,0:T(8,128)(2,1)}, bf16[3840,128]{1,0:T(8,128)(2,1)}, u32[]{:S(2)}, u32[]{:S(2)}) collective-permute-start(bf16[3840,128]{1,0:T(8,128)(2,1)} %collective-permute-done.5.refs_2_), channel_id=1, source_target_pairs={{0,8},{8,0},{1,9},{9,1},{2,10},{10,2},{3,11},{11,3},{4,12},{12,4},... | collective-permute-start | bytes 2949128 | tf_op jit(solution)/shard_map/ppermute | solution.py:443
  119.2 13.4 %collective-permute-start.37 = (bf16[384,256]{1,0:T(8,128)(2,1)}, bf16[384,256]{1,0:T(8,128)(2,1)S(1)}, u32[]{:S(2)}, u32[]{:S(2)}) collective-permute-start(bf16[384,256]{1,0:T(8,128)(2,1)} %get-tuple-element.34), channel_id=1, source_target_pairs={{0,2},{2,4},{4,6},{6,0},{1,3},{3,5},{5,7},{7,1},{8,10},{10,12},{12... | collective-permute-start | bytes 589832 | tf_op jit(solution)/shard_map/ppermute | solution.py:447
  127.0 20.9 %collective-permute-start.39 = (bf16[384,256]{1,0:T(8,128)(2,1)}, bf16[384,256]{1,0:T(8,128)(2,1)S(1)}, u32[]{:S(2)}, u32[]{:S(2)}) collective-permute-start(bf16[384,256]{1,0:T(8,128)(2,1)} %get-tuple-element.34), channel_id=1, source_target_pairs={{0,6},{2,0},{4,2},{6,4},{1,7},{3,1},{5,3},{7,5},{8,14},{10,8},{12,... | collective-permute-start | bytes 589832 | tf_op jit(solution)/shard_map/ppermute | solution.py:447
  132.6 17.0 %collective-permute-start.38 = (bf16[384,256]{1,0:T(8,128)(2,1)}, bf16[384,256]{1,0:T(8,128)(2,1)S(1)}, u32[]{:S(2)}, u32[]{:S(2)}) collective-permute-start(bf16[384,256]{1,0:T(8,128)(2,1)} %get-tuple-element.34), channel_id=1, source_target_pairs={{0,4},{2,6},{4,0},{6,2},{1,5},{3,7},{5,1},{7,3},{8,12},{10,14},{12... | collective-permute-start | bytes 589832 | tf_op jit(solution)/shard_map/ppermute | solution.py:447
  147.9 22.0 %collective-permute-start.11 = (bf16[1920,128]{1,0:T(8,128)(2,1)}, bf16[1920,128]{1,0:T(8,128)(2,1)}, u32[]{:S(2)}, u32[]{:S(2)}) collective-permute-start(bf16[1920,128]{1,0:T(8,128)(2,1)} %slice.310), channel_id=1, source_target_pairs={{0,16},{16,0},{1,17},{17,1},{2,18},{18,2},{3,19},{19,3},{4,20},{20... | collective-permute-start | bytes 1474568 | tf_op jit(solution)/shard_map/ppermute | solution.py:443
  149.6 20.2 %collective-permute-start.6 = (bf16[1920,128]{1,0:T(8,128)(2,1)S(1)}, bf16[1920,128]{1,0:T(8,128)(2,1)}, u32[]{:S(2)}, u32[]{:S(2)}) collective-permute-start(bf16[1920,128]{1,0:T(8,128)(2,1)S(1)} %slice.309), channel_id=1, source_target_pairs={{0,1},{1,0},{2,3},{3,2},{4,5},{5,4},{6,7},{7,6},{8,9},{9,8},{10,11... | collective-permute-start | bytes 1474568 | tf_op jit(solution)/shard_map/ppermute | solution.py:443
  152.1 20.0 %collective-permute-start.43 = (bf16[1536,256]{1,0:T(8,128)(2,1)}, bf16[1536,256]{1,0:T(8,128)(2,1)}, u32[]{:S(2)}, u32[]{:S(2)}) collective-permute-start(bf16[1536,256]{1,0:T(8,128)(2,1)} %constant_dynamic-update-slice_fusion.4.refs_0_), channel_id=1, source_target_pairs={{0,1},{1,0},{2,3},{3,2},{4,5},{5,4},{6,7},{7,6},{8,9},{9,8},{10,11... | collective-permute-start | bytes 2359304 | tf_op jit(solution)/shard_map/ppermute | solution.py:443
  154.0 23.5 %collective-permute-start.41 = (bf16[1536,256]{1,0:T(8,128)(2,1)}, bf16[1536,256]{1,0:T(8,128)(2,1)}, u32[]{:S(2)}, u32[]{:S(2)}) collective-permute-start(bf16[1536,256]{1,0:T(8,128)(2,1)} %constant_dynamic-update-slice_fusion.4.refs_0_), channel_id=1, source_target_pairs={{0,16},{16,0},{1,17},{17,1},{2,18},{18,2},{3,19},{19,3},{4,20},{20... | collective-permute-start | bytes 2359304 | tf_op jit(solution)/shard_map/ppermute | solution.py:443
  169.8 20.2 %copy-start.20 = (s32[1,32]{1,0:T(1,128)S(1)}, s32[1,32]{1,0:T(1,128)}, u32[]{:S(2)}) copy-start(s32[1,32]{1,0:T(1,128)} %param.9) | copy-start | bytes 388
  169.8 11.2 %copy-start.6 = (f32[4,384,256]{2,1,0:T(8,128)S(1)}, f32[4,384,256]{2,1,0:T(8,128)}, u32[]{:S(2)}) copy-start(f32[4,384,256]{2,1,0:T(8,128)} %copy-done.5) | copy-start | bytes 4718596
  169.8 11.1 %collective-permute-start.12 = (bf16[1920,128]{1,0:T(8,128)(2,1)}, bf16[1920,128]{1,0:T(8,128)(2,1)}, u32[]{:S(2)}, u32[]{:S(2)}) collective-permute-start(bf16[1920,128]{1,0:T(8,128)(2,1)} %tie.8.refs_0_), channel_id=1, source_target_pairs={{0,8},{8,0},{1,9},{9,1},{2,10},{10,2},{3,11},{11,3},{4,12},{12,4},... | collective-permute-start | bytes 1474568 | tf_op jit(solution)/shard_map/ppermute | solution.py:443
  169.9 62.5 %copy-start.4 = (bf16[12,640,128]{2,1,0:T(8,128)(2,1)S(1)}, bf16[12,640,128]{2,1,0:T(8,128)(2,1)}, u32[]{:S(2)}) copy-start(bf16[12,640,128]{2,1,0:T(8,128)(2,1)} %get-tuple-element.32) | copy-start | bytes 5898244
  170.0 11.0 %collective-permute-start.13 = (bf16[1920,128]{1,0:T(8,128)(2,1)}, bf16[1920,128]{1,0:T(8,128)(2,1)}, u32[]{:S(2)}, u32[]{:S(2)}) collective-permute-start(bf16[1920,128]{1,0:T(8,128)(2,1)} %tie.9.refs_1_), channel_id=1, source_target_pairs={{0,8},{8,0},{1,9},{9,1},{2,10},{10,2},{3,11},{11,3},{4,12},{12,4},... | collective-permute-start | bytes 1474568 | tf_op jit(solution)/shard_map/ppermute | solution.py:443
  173.9 22.5 %collective-permute-start.47 = (bf16[768,256]{1,0:T(8,128)(2,1)}, bf16[768,256]{1,0:T(8,128)(2,1)}, u32[]{:S(2)}, u32[]{:S(2)}) collective-permute-start(bf16[768,256]{1,0:T(8,128)(2,1)} %slice.371), channel_id=1, source_target_pairs={{0,16},{16,0},{1,17},{17,1},{2,18},{18,2},{3,19},{19,3},{4,20},{20... | collective-permute-start | bytes 1179656 | tf_op jit(solution)/shard_map/ppermute | solution.py:443
  179.2 17.3 %collective-permute-start.45 = (bf16[768,256]{1,0:T(8,128)(2,1)}, bf16[768,256]{1,0:T(8,128)(2,1)}, u32[]{:S(2)}, u32[]{:S(2)}) collective-permute-start(bf16[768,256]{1,0:T(8,128)(2,1)} %slice.370), channel_id=1, source_target_pairs={{0,1},{1,0},{2,3},{3,2},{4,5},{5,4},{6,7},{7,6},{8,9},{9,8},{10,11... | collective-permute-start | bytes 1179656 | tf_op jit(solution)/shard_map/ppermute | solution.py:443
  190.1 29.8 %collective-permute-start.14 = (f32[384,256]{1,0:T(8,128)}, f32[384,256]{1,0:T(8,128)S(1)}, u32[]{:S(2)}, u32[]{:S(2)}) collective-permute-start(f32[384,256]{1,0:T(8,128)} %get-tuple-element.22), channel_id=1, source_target_pairs={{0,4},{2,6},{4,0},{6,2},{1,5},{3,7},{5,1},{7,3},{8,12},{10,14},{12... | collective-permute-start | bytes 1179656 | tf_op jit(solution)/shard_map/ppermute | solution.py:447
  190.1 30.9 %collective-permute-start.15 = (f32[384,256]{1,0:T(8,128)}, f32[384,256]{1,0:T(8,128)}, u32[]{:S(2)}, u32[]{:S(2)}) collective-permute-start(f32[384,256]{1,0:T(8,128)} %get-tuple-element.23), channel_id=1, source_target_pairs={{0,2},{2,4},{4,6},{6,0},{1,3},{3,5},{5,7},{7,1},{8,10},{10,12},{12... | collective-permute-start | bytes 1179656 | tf_op jit(solution)/shard_map/ppermute | solution.py:447
  195.8 25.6 %collective-permute-start.16 = (f32[384,256]{1,0:T(8,128)}, f32[384,256]{1,0:T(8,128)}, u32[]{:S(2)}, u32[]{:S(2)}) collective-permute-start(f32[384,256]{1,0:T(8,128)} %get-tuple-element.24), channel_id=1, source_target_pairs={{0,6},{2,0},{4,2},{6,4},{1,7},{3,1},{5,3},{7,5},{8,14},{10,8},{12,... | collective-permute-start | bytes 1179656 | tf_op jit(solution)/shard_map/ppermute | solution.py:447
  196.4 31.7 %collective-permute-start.40 = (bf16[1536,256]{1,0:T(8,128)(2,1)}, bf16[1536,256]{1,0:T(8,128)(2,1)S(1)}, u32[]{:S(2)}, u32[]{:S(2)}) collective-permute-start(bf16[1536,256]{1,0:T(8,128)(2,1)} %constant_dynamic-update-slice_fusion.4.refs_0_), channel_id=1, source_target_pairs={{0,8},{8,0},{1,9},{9,1},{2,10},{10,2},{3,11},{11,3},{4,12},{12,4},... | collective-permute-start | bytes 2359304 | tf_op jit(solution)/shard_map/ppermute | solution.py:443
  196.5 32.9 %collective-permute-start.44 = (bf16[1536,256]{1,0:T(8,128)(2,1)}, bf16[1536,256]{1,0:T(8,128)(2,1)}, u32[]{:S(2)}, u32[]{:S(2)}) collective-permute-start(bf16[1536,256]{1,0:T(8,128)(2,1)} %collective-permute-done.43.refs_4_), channel_id=1, source_target_pairs={{0,8},{8,0},{1,9},{9,1},{2,10},{10,2},{3,11},{11,3},{4,12},{12,4},... | collective-permute-start | bytes 2359304 | tf_op jit(solution)/shard_map/ppermute | solution.py:443
  219.8 12.6 %collective-permute-start.42 = (bf16[1536,256]{1,0:T(8,128)(2,1)}, bf16[1536,256]{1,0:T(8,128)(2,1)}, u32[]{:S(2)}, u32[]{:S(2)}) collective-permute-start(bf16[1536,256]{1,0:T(8,128)(2,1)} %collective-permute-done.41.refs_2_), channel_id=1, source_target_pairs={{0,8},{8,0},{1,9},{9,1},{2,10},{10,2},{3,11},{11,3},{4,12},{12,4},... | collective-permute-start | bytes 2359304 | tf_op jit(solution)/shard_map/ppermute | solution.py:443
  221.0 11.5 %collective-permute-start.48 = (bf16[768,256]{1,0:T(8,128)(2,1)}, bf16[768,256]{1,0:T(8,128)(2,1)S(1)}, u32[]{:S(2)}, u32[]{:S(2)}) collective-permute-start(bf16[768,256]{1,0:T(8,128)(2,1)} %collective-permute-done.47.refs_8_), channel_id=1, source_target_pairs={{0,8},{8,0},{1,9},{9,1},{2,10},{10,2},{3,11},{11,3},{4,12},{12,4},... | collective-permute-start | bytes 1179656 | tf_op jit(solution)/shard_map/ppermute | solution.py:443
  221.4 11.0 %collective-permute-start.46 = (bf16[768,256]{1,0:T(8,128)(2,1)}, bf16[768,256]{1,0:T(8,128)(2,1)}, u32[]{:S(2)}, u32[]{:S(2)}) collective-permute-start(bf16[768,256]{1,0:T(8,128)(2,1)} %collective-permute-done.45.refs_6_), channel_id=1, source_target_pairs={{0,8},{8,0},{1,9},{9,1},{2,10},{10,2},{3,11},{11,3},{4,12},{12,4},... | collective-permute-start | bytes 1179656 | tf_op jit(solution)/shard_map/ppermute | solution.py:443
  228.1 41.1 %collective-permute-start.25 = (f32[2,48,128]{2,1,0:T(8,128)S(1)}, f32[2,48,128]{2,1,0:T(8,128)S(1)}, u32[]{:S(2)}, u32[]{:S(2)}) collective-permute-start(f32[2,48,128]{2,1,0:T(8,128)S(1)} %bitcast.122), channel_id=1, source_target_pairs={{8,0},{16,8},{24,16},{9,1},{17,9},{25,17},{10,2},{18,10},{26,18},{... | collective-permute-start | bytes 147464 | tf_op jit(solution)/shard_map/ppermute | solution.py:394
  229.4 39.8 %collective-permute-start.24 = (f32[2,48,128]{2,1,0:T(8,128)S(1)}, f32[2,48,128]{2,1,0:T(8,128)S(1)}, u32[]{:S(2)}, u32[]{:S(2)}) collective-permute-start(f32[2,48,128]{2,1,0:T(8,128)S(1)} %bitcast.121), channel_id=1, source_target_pairs={{0,8},{8,16},{16,24},{1,9},{9,17},{17,25},{2,10},{10,18},{18,26},{... | collective-permute-start | bytes 147464 | tf_op jit(solution)/shard_map/ppermute | solution.py:391
  232.5 29.6 %copy-start.29 = (bf16[384,256]{1,0:T(8,128)(2,1)S(1)}, bf16[384,256]{1,0:T(8,128)(2,1)}, u32[]{:S(2)}) copy-start(bf16[384,256]{1,0:T(8,128)(2,1)} %get-tuple-element.33) | copy-start | bytes 589828
  232.5 36.7 %copy-start.24 = (f32[1536,128]{1,0:T(8,128)S(1)}, f32[1536,128]{1,0:T(8,128)}, u32[]{:S(2)}) copy-start(f32[1536,128]{1,0:T(8,128)} %get-tuple-element.31) | copy-start | bytes 2359300
  232.5 56.3 %copy-start.30 = (f32[34,50]{1,0:T(8,128)S(1)}, f32[34,50]{1,0:T(8,128)}, u32[]{:S(2)}) copy-start(f32[34,50]{1,0:T(8,128)} %broadcast_multiply_fusion) | copy-start | bytes 20404
  262.1 21.9 %collective-permute-start.30 = (bf16[384,256]{1,0:T(8,128)(2,1)S(1)}, bf16[384,256]{1,0:T(8,128)(2,1)S(1)}, u32[]{:S(2)}, u32[]{:S(2)}) collective-permute-start(bf16[384,256]{1,0:T(8,128)(2,1)S(1)} %copy-done.29), channel_id=1, source_target_pairs={{0,6},{2,0},{4,2},{6,4},{1,7},{3,1},{5,3},{7,5},{8,14},{10,8},{12,... | collective-permute-start | bytes 589832 | tf_op jit(solution)/shard_map/ppermute | solution.py:447
  263.2 20.8 %collective-permute-start.29 = (bf16[384,256]{1,0:T(8,128)(2,1)S(1)}, bf16[384,256]{1,0:T(8,128)(2,1)S(1)}, u32[]{:S(2)}, u32[]{:S(2)}) collective-permute-start(bf16[384,256]{1,0:T(8,128)(2,1)S(1)} %copy-done.29), channel_id=1, source_target_pairs={{0,4},{2,6},{4,0},{6,2},{1,5},{3,7},{5,1},{7,3},{8,12},{10,14},{12... | collective-permute-start | bytes 589832 | tf_op jit(solution)/shard_map/ppermute | solution.py:447
  267.6 13.3 %collective-permute-start.28 = (bf16[384,256]{1,0:T(8,128)(2,1)S(1)}, bf16[384,256]{1,0:T(8,128)(2,1)S(1)}, u32[]{:S(2)}, u32[]{:S(2)}) collective-permute-start(bf16[384,256]{1,0:T(8,128)(2,1)S(1)} %copy-done.29), channel_id=1, source_target_pairs={{0,2},{2,4},{4,6},{6,0},{1,3},{3,5},{5,7},{7,1},{8,10},{10,12},{12... | collective-permute-start | bytes 589832 | tf_op jit(solution)/shard_map/ppermute | solution.py:447
  269.2 6.9 %collective-permute-start.26 = (f32[36,2,128]{2,1,0:T(2,128)S(1)}, f32[36,2,128]{2,1,0:T(2,128)S(1)}, u32[]{:S(2)}, u32[]{:S(2)}) collective-permute-start(f32[36,2,128]{2,1,0:T(2,128)S(1)} %get-tuple-element.42), channel_id=1, source_target_pairs={{0,1},{1,2},{2,3},{3,4},{4,5},{5,6},{6,7},{8,9},{9,10},{10,11},{11... | collective-permute-start | bytes 110600 | tf_op jit(solution)/shard_map/ppermute | solution.py:391
  274.5 5.9 %collective-permute-start.27 = (f32[36,2,128]{2,1,0:T(2,128)S(1)}, f32[36,2,128]{2,1,0:T(2,128)S(1)}, u32[]{:S(2)}, u32[]{:S(2)}) collective-permute-start(f32[36,2,128]{2,1,0:T(2,128)S(1)} %get-tuple-element.43), channel_id=1, source_target_pairs={{1,0},{2,1},{3,2},{4,3},{5,4},{6,5},{7,6},{9,8},{10,9},{11,10},{12... | collective-permute-start | bytes 110600 | tf_op jit(solution)/shard_map/ppermute | solution.py:394
  284.0 22.2 %collective-permute-start.34 = (bf16[1536,256]{1,0:T(8,128)(2,1)S(1)}, bf16[1536,256]{1,0:T(8,128)(2,1)S(1)}, u32[]{:S(2)}, u32[]{:S(2)}) collective-permute-start(bf16[1536,256]{1,0:T(8,128)(2,1)S(1)} %constant_dynamic-update-slice_fusion.refs_0_), channel_id=1, source_target_pairs={{0,1},{1,0},{2,3},{3,2},{4,5},{5,4},{6,7},{7,6},{8,9},{9,8},{10,11... | collective-permute-start | bytes 2359304 | tf_op jit(solution)/shard_map/ppermute | solution.py:443
  288.0 20.0 %collective-permute-start.31 = (bf16[1536,256]{1,0:T(8,128)(2,1)S(1)}, bf16[1536,256]{1,0:T(8,128)(2,1)S(1)}, u32[]{:S(2)}, u32[]{:S(2)}) collective-permute-start(bf16[1536,256]{1,0:T(8,128)(2,1)S(1)} %constant_dynamic-update-slice_fusion.refs_0_), channel_id=1, source_target_pairs={{0,16},{16,0},{1,17},{17,1},{2,18},{18,2},{3,19},{19,3},{4,20},{20... | collective-permute-start | bytes 2359304 | tf_op jit(solution)/shard_map/ppermute | solution.py:443
  292.6 19.6 %collective-permute-start.36 = (bf16[1536,256]{1,0:T(8,128)(2,1)S(1)}, bf16[1536,256]{1,0:T(8,128)(2,1)S(1)}, u32[]{:S(2)}, u32[]{:S(2)}) collective-permute-start(bf16[1536,256]{1,0:T(8,128)(2,1)S(1)} %constant_dynamic-update-slice_fusion.refs_0_), channel_id=1, source_target_pairs={{0,8},{8,0},{1,9},{9,1},{2,10},{10,2},{3,11},{11,3},{4,12},{12,4},... | collective-permute-start | bytes 2359304 | tf_op jit(solution)/shard_map/ppermute | solution.py:443
  306.2 13.7 %collective-permute-start.35 = (bf16[1536,256]{1,0:T(8,128)(2,1)S(1)}, bf16[1536,256]{1,0:T(8,128)(2,1)S(1)}, u32[]{:S(2)}, u32[]{:S(2)}) collective-permute-start(bf16[1536,256]{1,0:T(8,128)(2,1)S(1)} %collective-permute-done.34.refs_2_), channel_id=1, source_target_pairs={{0,8},{8,0},{1,9},{9,1},{2,10},{10,2},{3,11},{11,3},{4,12},{12,4},... | collective-permute-start | bytes 2359304 | tf_op jit(solution)/shard_map/ppermute | solution.py:443
  308.0 12.0 %collective-permute-start.33 = (bf16[1536,256]{1,0:T(8,128)(2,1)S(1)}, bf16[1536,256]{1,0:T(8,128)(2,1)S(1)}, u32[]{:S(2)}, u32[]{:S(2)}) collective-permute-start(bf16[1536,256]{1,0:T(8,128)(2,1)S(1)} %collective-permute-done.31.refs_0_), channel_id=1, source_target_pairs={{0,8},{8,0},{1,9},{9,1},{2,10},{10,2},{3,11},{11,3},{4,12},{12,4},... | collective-permute-start | bytes 2359304 | tf_op jit(solution)/shard_map/ppermute | solution.py:443
  308.7 31.1 %collective-permute-start.50 = (bf16[768,256]{1,0:T(8,128)(2,1)S(1)}, bf16[768,256]{1,0:T(8,128)(2,1)}, u32[]{:S(2)}, u32[]{:S(2)}) collective-permute-start(bf16[768,256]{1,0:T(8,128)(2,1)S(1)} %slice.372), channel_id=1, source_target_pairs={{0,16},{16,0},{1,17},{17,1},{2,18},{18,2},{3,19},{19,3},{4,20},{20... | collective-permute-start | bytes 1179656 | tf_op jit(solution)/shard_map/ppermute | solution.py:443
  309.1 27.9 %collective-permute-start.32 = (bf16[768,256]{1,0:T(8,128)(2,1)S(1)}, bf16[768,256]{1,0:T(8,128)(2,1)S(1)}, u32[]{:S(2)}, u32[]{:S(2)}) collective-permute-start(bf16[768,256]{1,0:T(8,128)(2,1)S(1)} %slice.369), channel_id=1, source_target_pairs={{0,1},{1,0},{2,3},{3,2},{4,5},{5,4},{6,7},{7,6},{8,9},{9,8},{10,11... | collective-permute-start | bytes 1179656 | tf_op jit(solution)/shard_map/ppermute | solution.py:443
  337.8 9.1 %collective-permute-start.49 = (bf16[768,256]{1,0:T(8,128)(2,1)}, bf16[768,256]{1,0:T(8,128)(2,1)S(1)}, u32[]{:S(2)}, u32[]{:S(2)}) collective-permute-start(bf16[768,256]{1,0:T(8,128)(2,1)} %tie.12.refs_0_), channel_id=1, source_target_pairs={{0,8},{8,0},{1,9},{9,1},{2,10},{10,2},{3,11},{11,3},{4,12},{12,4},... | collective-permute-start | bytes 1179656 | tf_op jit(solution)/shard_map/ppermute | solution.py:443
  339.9 5.8 %copy-start.23 = (f32[34,50,128]{2,1,0:T(8,128)S(1)}, f32[34,50,128]{2,1,0:T(8,128)}, u32[]{:S(2)}) copy-start(f32[34,50,128]{2,1,0:T(8,128)} %get-tuple-element.36) | copy-start | bytes 2611204
  339.9 7.0 %collective-permute-start.51 = (bf16[768,256]{1,0:T(8,128)(2,1)}, bf16[768,256]{1,0:T(8,128)(2,1)S(1)}, u32[]{:S(2)}, u32[]{:S(2)}) collective-permute-start(bf16[768,256]{1,0:T(8,128)(2,1)} %tie.13.refs_2_), channel_id=1, source_target_pairs={{0,8},{8,0},{1,9},{9,1},{2,10},{10,2},{3,11},{11,3},{4,12},{12,4},... | collective-permute-start | bytes 1179656 | tf_op jit(solution)/shard_map/ppermute | solution.py:443
  (22 other events, 29.5 us)

commit v3 on v2

v3 whole, which is shorter than its diff:
```python
import functools

import jax
import jax.numpy as jnp
from jax import lax
from jax.experimental import pallas as pl
from jax.experimental.pallas import tpu as pltpu
from jax.sharding import Mesh
from jax.sharding import PartitionSpec as P

CIL = 32
CXL = 48
CELLS = CIL * CXL
QUARTER = CELLS // 4
FOLD = CXL // 3
MIB = 1 << 20
VMEM_LIMIT = 56 * MIB
IN_SMEM = pl.BlockSpec(memory_space=pltpu.SMEM)
IN_VMEM = pl.BlockSpec(memory_space=pltpu.VMEM)
IN_ANY = pl.BlockSpec(memory_space=pl.ANY)
IN_HBM = pl.BlockSpec(memory_space=pltpu.HBM)

WEIGHT = pl.CostEstimate(flops=1 << 35, bytes_accessed=1 << 20, transcendentals=0)
LIGHT = pl.CostEstimate(flops=1, bytes_accessed=1, transcendentals=0)


def hot(cells, shape, axis):
    line = lax.broadcasted_iota(jnp.int32, shape, axis)
    return jnp.where(line == cells, 1.0, 0.0).astype(jnp.bfloat16)


def quarter_of(cells):
    return sum((cells >= q * QUARTER).astype(jnp.int32) for q in (1, 2, 3))


def low_lanes(shape):
    return lax.broadcasted_iota(jnp.int32, shape, len(shape) - 1) < 64


def swap_lanes(value):
    return pltpu.roll(value, 64, 1)


def tie(values, *tokens):
    count = len(values)

    def kernel(*refs):
        pass

    return pl.pallas_call(
        kernel,
        out_shape=[jax.ShapeDtypeStruct(value.shape, value.dtype) for value in values],
        in_specs=[IN_ANY] * (count + len(tokens)),
        out_specs=[IN_ANY] * count,
        input_output_aliases={i: i for i in range(count)},
        cost_estimate=LIGHT,
        name="tie",
    )(*values, *tokens)


def gate_kernel(skip, from_x, from_y, *refs):
    turn_x, turn_y, held, sems = refs[skip + 2 :]
    middle = turn_x.shape[0]
    copies = [
        pltpu.make_async_copy(from_x.at[pl.ds(0, middle)], held.at[0], sems.at[0]),
        pltpu.make_async_copy(from_y.at[pl.ds(middle, middle)], held.at[1], sems.at[1]),
    ]
    sends = [
        pltpu.make_async_copy(held.at[0], turn_x, sems.at[2]),
        pltpu.make_async_copy(held.at[1], turn_y, sems.at[3]),
    ]
    for copy in copies:
        copy.start()
    for copy, send in zip(copies, sends, strict=True):
        copy.wait()
        send.start()
    for send in sends:
        send.wait()


def gate(from_x, from_y, *tokens):
    full = jax.ShapeDtypeStruct(from_x.shape, from_x.dtype)
    part = jax.ShapeDtypeStruct((from_x.shape[0] // 2, from_x.shape[1]), from_x.dtype)
    return pl.pallas_call(
        functools.partial(gate_kernel, len(tokens)),
        out_shape=[full, full, part, part],
        in_specs=[IN_HBM] * 2 + [IN_ANY] * len(tokens),
        out_specs=[IN_HBM] * 4,
        input_output_aliases={0: 0, 1: 1},
        scratch_shapes=[
            pltpu.VMEM((2,) + part.shape, part.dtype),
            pltpu.SemaphoreType.DMA((4,)),
        ],
        name="gate",
    )(from_x, from_y, *tokens)


def filter_kernel(half, skip, taps, source, *refs):
    out, *matrices = refs[skip:]
    each, rows, samples = source.shape
    row = lax.broadcasted_iota(jnp.int32, (samples, samples), 0)
    col = lax.broadcasted_iota(jnp.int32, (samples, samples), 1)
    for i in range(each):
        line = jnp.broadcast_to(taps[i], (samples, samples))
        band = pltpu.roll(line, 0, 1, stride=1, stride_axis=0)
        matrix = jnp.where(col >= row, band, 0.0)
        if matrices:
            matrices[0][i] = matrix.astype(jnp.bfloat16)
        turned = matrix.T[64 * half : 64 * half + 64].astype(jnp.bfloat16)
        value = lax.dot_general(
            turned, source[i], (((1,), (1,)), ((), ())), preferred_element_type=jnp.float32
        ).astype(jnp.bfloat16)
        for block in range(rows // 128):
            out[i, 64 * block : 64 * block + 64] = value[:, 128 * block : 128 * block + 128]


def filter_call(half, traces, taps, tokens=()):
    surveys, unused, samples = taps.shape
    rows = traces.shape[0] // surveys
    each = 3
    out_specs = [pl.BlockSpec((each, rows // 2, samples), lambda i: (i, 0, 0))]
    out_shape = [jax.ShapeDtypeStruct((surveys, rows // 2, samples), jnp.bfloat16)]
    if half == 1:
        out_specs.append(pl.BlockSpec((each, samples, samples), lambda i: (i, 0, 0)))
        out_shape.append(jax.ShapeDtypeStruct((surveys, samples, samples), jnp.bfloat16))
    return pl.pallas_call(
        functools.partial(filter_kernel, half, len(tokens)),
        grid=(surveys // each,),
        in_specs=[
            pl.BlockSpec((each, 1, samples), lambda i: (i, 0, 0)),
            pl.BlockSpec((each, rows, samples), lambda i: (i, 0, 0)),
        ]
        + [IN_ANY] * len(tokens),
        out_specs=out_specs,
        out_shape=out_shape,
        name=f"filter_{half}",
    )(taps, traces.reshape(surveys, rows, samples), *tokens)


def stack_kernel(spec, order, cells, *refs):
    sizes, sources, tiles, with_fold, first, last, skip, base = spec
    per_slot = cells.shape[1]
    group = 16
    pieces = refs[: len(sizes)]
    refs = refs[len(sizes) :]
    if not first:
        before, refs = refs[0], refs[1:]
    refs = refs[skip:]
    outs = refs[: tiles if last else 1]
    held, total, live, numbers, sems = refs[len(outs) :]
    copies = []
    start = 0
    for i, rows in enumerate(sizes):
        copies.append(
            pltpu.make_async_copy(pieces[i], held.at[pl.ds(start, rows)], sems.at[i])
        )
        start += rows
    per_source = start // sources
    if not first:
        copies.append(pltpu.make_async_copy(before, total, sems.at[len(sizes)]))
    origins = cells.shape[0]
    for i in range(origins):
        copies.append(
            pltpu.make_async_copy(
                cells.at[i, pl.ds(per_slot - 8, 8)],
                numbers.at[pl.ds(8 * i, 8)],
                sems.at[len(sizes) + 1 + tiles + i],
            )
        )
    for copy in copies:
        copy.start()
    if first:
        total[...] = jnp.zeros_like(total)
    for copy in copies:
        copy.wait()

    def tile_step(tile, unused):
        def add_source(source, n):
            origin = order[base + source]
            wanted = order[tile]

            def add_slot(c, n):
                live[n] = wanted * 8 + c
                live[n + 128] = numbers[origin * 8 + wanted, c] * 64 + source * per_source
                live[n + 256] = origin
                return n + 1

            return lax.fori_loop(0, numbers[origin * 8 + wanted, 7], add_slot, n)

        n = lax.fori_loop(0, sources, add_source, 0)

        def one_group(g, unused):
            picked, data, selector = [], [], []
            for i in range(group):
                at = g * group + i
                place = jnp.minimum(at, n - 1)
                row = jnp.where(at < n, cells[live[256 + place], pl.ds(live[place], 1), :], -1)
                quarter = quarter_of(row)
                block = held[pl.ds(pl.multiple_of(live[128 + place], 64), 64), :]
                block = block.astype(jnp.float32)
                data.append(
                    jnp.concatenate(
                        [jnp.where(quarter == q, block, 0.0) for q in range(4)], axis=0
                    ).astype(jnp.bfloat16)
                )
                selector.append(hot(row - QUARTER * quarter, (QUARTER, 128), 0))
                picked.append(row)
            total[tile, :QUARTER] += lax.dot_general(
                jnp.concatenate(selector, axis=1),
                jnp.concatenate(data, axis=1),
                (((1,), (1,)), ((), ())),
                preferred_element_type=jnp.float32,
            )
            line = jnp.concatenate(picked, axis=1)
            width = line.shape[1]
            if with_fold:
                inline = ((line >> 4) * 171) >> 9
                cross = line - CXL * inline
                row = jnp.where(line >= 0, cross & 15, -1)
                lane = inline + 32 * (cross >> 4)
                total[tile, QUARTER:, :128] += lax.dot_general(
                    hot(row, (FOLD, width), 0),
                    hot(lane, (128, width), 0),
                    (((1,), (1,)), ((), ())),
                    preferred_element_type=jnp.float32,
                )
            return 0

        lax.fori_loop(0, (n + group - 1) // group, one_group, 0)
        return 0

    lax.fori_loop(0, tiles, tile_step, 0)
    targets = [total.at[tile] for tile in range(tiles)] if last else [total]
    sends = [
        pltpu.make_async_copy(target, out, sems.at[len(sizes) + 1 + i])
        for i, (target, out) in enumerate(zip(targets, outs, strict=True))
    ]
    for send in sends:
        send.start()
    for send in sends:
        send.wait()


def stack_call(order, base, cells, pieces, sources, before, tiles, with_fold, last, tokens=()):
    first = before is None
    sizes = tuple(piece.shape[0] for piece in pieces)
    rows = QUARTER + (FOLD if with_fold else 0)
    extra = [] if first else [before]
    every = jax.ShapeDtypeStruct((tiles, rows, 256), jnp.float32)
    single = [jax.ShapeDtypeStruct((rows, 256), jnp.float32)] * tiles
    origins = cells.shape[0]
    spec = (sizes, sources, tiles, with_fold, first, last, len(tokens), base)
    return pl.pallas_call(
        functools.partial(stack_kernel, spec),
        out_shape=single if last else [every],
        in_specs=[IN_SMEM, IN_VMEM]
        + [IN_HBM] * (len(pieces) + len(extra))
        + [IN_ANY] * len(tokens),
        out_specs=[IN_HBM] * (tiles if last else 1),
        scratch_shapes=[
            pltpu.VMEM((sum(sizes), 128), jnp.bfloat16),
            pltpu.VMEM(every.shape, jnp.float32),
            pltpu.SMEM((384,), jnp.int32),
            pltpu.SMEM((8 * origins, 128), jnp.int32),
            pltpu.SemaphoreType.DMA((len(pieces) + 1 + tiles + origins,)),
        ],
        compiler_params=pltpu.CompilerParams(vmem_limit_bytes=VMEM_LIMIT),
        cost_estimate=LIGHT if last else WEIGHT,
        name="stack",
    )(order, cells, *pieces, *extra, *tokens)


def image_kernel(half, skip, *refs):
    parts, refs = refs[:4], refs[4:]
    if half == 0:
        packed, value_out, fold_out, turned = refs[skip:]
        fold = sum(parts[i][QUARTER:] for i in range(4))
        fold_out[...] = fold
    else:
        fold_in, before, packed, image, turned = refs[:2] + refs[2 + skip :]
        fold = fold_in[...]
    fold = jnp.maximum(fold, 1.0)
    left = low_lanes((CXL, 128))
    for a in range(CIL // 4):
        here = slice(a * CXL, (a + 1) * CXL)
        columns = []
        for q in range(4):
            lane = q * (CIL // 4) + a
            columns.append(
                jnp.concatenate(
                    [fold[:, 32 * j + lane : 32 * j + lane + 1] for j in range(3)], axis=0
                )
            )
        for side in range(2):
            lanes = slice(128 * side, 128 * side + 128)
            total = (parts[0][here, lanes] + parts[1][here, lanes]) + (
                parts[2][here, lanes] + parts[3][here, lanes]
            )
            value = total / jnp.where(left, columns[2 * side], columns[2 * side + 1])
            turned[here, lanes] = value
            if half == 0:
                value_out[here, lanes] = value
            else:
                earlier = before[here, lanes]
                even, odd = 2 * side * QUARTER + a * CXL, (2 * side + 1) * QUARTER + a * CXL
                image[even : even + CXL] = jnp.where(left, earlier, swap_lanes(value))
                image[odd : odd + CXL] = jnp.where(left, swap_lanes(earlier), value)
    copy = turned[...].T.astype(jnp.bfloat16)
    for i in range(4):
        packed[256 * i : 256 * i + 256] = copy


def image_call(half, parts, extra, tokens):
    packed = jax.ShapeDtypeStruct((4 * 256, QUARTER), jnp.bfloat16)
    if half == 0:
        out_shape = [
            packed,
            jax.ShapeDtypeStruct((QUARTER, 256), jnp.float32),
            jax.ShapeDtypeStruct((FOLD, 256), jnp.float32),
        ]
    else:
        out_shape = [packed, jax.ShapeDtypeStruct((CELLS, 128), jnp.float32)]
    return pl.pallas_call(
        functools.partial(image_kernel, half, len(tokens)),
        out_shape=out_shape,
        in_specs=[IN_VMEM] * (4 + len(extra)) + [IN_ANY] * len(tokens),
        out_specs=[IN_VMEM] * len(out_shape),
        scratch_shapes=[pltpu.VMEM((QUARTER, 256), jnp.float32)],
        cost_estimate=LIGHT,
        name=f"image_{half}",
    )(*parts, *extra, *tokens)


def read_kernel(spec, order, counts, blocks, cells, own, *refs):
    sizes, first, last, skip, base = spec
    group = 4
    tiles = sum(sizes) // 256
    pieces = refs[: len(sizes)]
    refs = refs[len(sizes) :]
    if last:
        matrices, earlier, refs = refs[0], refs[1], refs[2:]
    if not first:
        before, refs = refs[0], refs[1:]
    refs = refs[skip:]
    out, held, mine, total, live, sems = refs[:6]
    copies = [pltpu.make_async_copy(own, mine, sems.at[0])]
    if not first:
        copies.append(pltpu.make_async_copy(before, total, sems.at[len(sizes) + 1]))
    if last:
        whole_out, earlier_in, band = refs[6:]
        copies.append(pltpu.make_async_copy(earlier, earlier_in, sems.at[len(sizes) + 2]))
        copies.append(pltpu.make_async_copy(matrices, band, sems.at[len(sizes) + 3]))
    start = 0
    for i, rows in enumerate(sizes):
        copies.append(
            pltpu.make_async_copy(pieces[i], held.at[pl.ds(start, rows)], sems.at[i + 1])
        )
        start += rows
    for copy in copies:
        copy.start()
    if first:
        total[...] = jnp.zeros_like(total)

    def add_tile(j, n):
        for g in range(8 // group):
            live[n] = order[base + j] * 8 + g * group
            live[n + 128] = j
            n = n + (counts[order[base + j]] > g * group).astype(jnp.int32)
        return n

    n = lax.fori_loop(0, tiles, add_tile, 0)
    for copy in copies:
        copy.wait()

    def one_step(step, unused):
        waiting = []
        for k in range(2):
            at = step * 2 + k
            place = jnp.minimum(at, n - 1)
            entry = live[place]
            rows = [
                jnp.where(at < n, cells[pl.ds(entry + i, 1), :], -1) for i in range(group)
            ]
            quarters = [quarter_of(row) for row in rows]
            selector = jnp.concatenate(
                [
                    hot(row - QUARTER * quarter, (QUARTER, 128), 0)
                    for row, quarter in zip(rows, quarters, strict=True)
                ],
                axis=1,
            )
            image = held[pl.ds(pl.multiple_of(live[128 + place] * 256, 256), 256), :]
            got = jnp.dot(image, selector, preferred_element_type=jnp.float32)
            waiting.append((entry, rows, quarters, got))
        for entry, rows, quarters, got in waiting:
            for i in range(group):
                here = pl.ds(pl.multiple_of(blocks[entry + i] * 64, 64), 64)
                part = got[:, 128 * i : 128 * i + 128]
                value = part[:64]
                for q in (1, 2, 3):
                    value = jnp.where(quarters[i] == q, part[64 * q : 64 * q + 64], value)
                sent = jnp.where(rows[i] >= 0, mine[here, :].astype(jnp.float32), 0.0)
                total[here, :] += sent - value
        return 0

    lax.fori_loop(0, (n + 1) // 2, one_step, 0)
    if not last:
        send = pltpu.make_async_copy(total, out, sems.at[len(sizes) + 4])
        send.start()
        send.wait()
        return
    surveys = matrices.shape[0]
    rows = whole_out.shape[0] // surveys
    sends = []
    for survey in range(surveys):
        for block in range(rows // 128):
            at = survey * (rows // 2) + block * 64
            residual = jnp.concatenate(
                [earlier_in[at : at + 64], total[at : at + 64]], axis=0
            ).T.astype(jnp.bfloat16)
            whole_out[survey * rows + 128 * block : survey * rows + 128 * block + 128] = (
                lax.dot_general(
                    residual,
                    band[survey],
                    (((1,), (1,)), ((), ())),
                    preferred_element_type=jnp.float32,
                )
            )
        sends.append(
            pltpu.make_async_copy(
                whole_out.at[pl.ds(survey * rows, rows)],
                out.at[pl.ds(survey * rows, rows)],
                sems.at[len(sizes) + 4 + survey],
            )
        )
        sends[-1].start()
    for send in sends:
        send.wait()


def read_call(
    order, base, slots, own, pieces, before, matrices=None, earlier=None, tokens=(), cost=None
):
    first, last = before is None, matrices is not None
    sizes = tuple(piece.shape[0] for piece in pieces)
    extra = ([matrices, earlier] if last else []) + ([] if first else [before])
    surveys = matrices.shape[0] if last else 0
    full = (2 * own.shape[0], own.shape[1])
    return pl.pallas_call(
        functools.partial(read_kernel, (sizes, first, last, len(tokens), base)),
        out_shape=jax.ShapeDtypeStruct(full if last else own.shape, jnp.float32),
        in_specs=[IN_SMEM] * 3
        + [IN_VMEM]
        + [IN_HBM] * (1 + len(pieces))
        + [IN_HBM] * len(extra)
        + [IN_ANY] * len(tokens),
        out_specs=IN_HBM,
        scratch_shapes=[
            pltpu.VMEM((sum(sizes), QUARTER), jnp.bfloat16),
            pltpu.VMEM(own.shape, jnp.bfloat16),
            pltpu.VMEM(own.shape, jnp.float32),
            pltpu.SMEM((256,), jnp.int32),
            pltpu.SemaphoreType.DMA((len(sizes) + 5 + surveys,)),
        ]
        + (
            [
                pltpu.VMEM(full, jnp.float32),
                pltpu.VMEM(own.shape, jnp.float32),
                pltpu.VMEM(matrices.shape, jnp.bfloat16),
            ]
            if last
            else []
        ),
        compiler_params=pltpu.CompilerParams(vmem_limit_bytes=VMEM_LIMIT),
        cost_estimate=cost or LIGHT,
        name="read",
    )(order, *slots, own, *pieces, *extra, *tokens)


def with_halo(block, sides, width):
    for axis, count, dim in sides:
        forward = [(i, i + 1) for i in range(count - 1)]
        backward = [(target, source) for source, target in forward]
        low = lax.ppermute(
            lax.slice_in_dim(block, block.shape[dim] - width, None, axis=dim), axis, forward
        )
        high = lax.ppermute(lax.slice_in_dim(block, 0, width, axis=dim), axis, backward)
        block = jnp.concatenate([low, block, high], axis=dim)
    return block


def cycle_box(values, rows_out, cols_out):
    box_total = jnp.zeros((rows_out, cols_out, values.shape[2]), jnp.float32)
    for row_shift in range(3):
        for col_shift in range(3):
            box_total = (
                box_total
                + values[row_shift : row_shift + rows_out, col_shift : col_shift + cols_out]
            )
    return box_total / 9.0


def tensor(padded, il, xl):
    count_il, at_il = il
    count_xl, at_xl = xl
    padded_time = jnp.pad(padded, ((0, 0), (0, 0), (1, 1)))
    grad_il = (padded[2:, 1:-1] - padded[:-2, 1:-1]) * 0.5
    grad_xl = (padded[1:-1, 2:] - padded[1:-1, :-2]) * 0.5
    grad_time = (padded_time[1:-1, 1:-1, 2:] - padded_time[1:-1, 1:-1, :-2]) * 0.5
    rows_il = at_il * CIL + jnp.arange(CIL + 2, dtype=jnp.int32) - 1
    rows_xl = at_xl * CXL + jnp.arange(CXL + 2, dtype=jnp.int32) - 1
    inside_il = ((rows_il >= 0) & (rows_il < CIL * count_il)).astype(jnp.float32)
    inside_xl = ((rows_xl >= 0) & (rows_xl < CXL * count_xl)).astype(jnp.float32)
    cycle_mask = inside_il[:, None, None] * inside_xl[None, :, None]
    factor_pairs = (
        (grad_il, grad_il),
        (grad_xl, grad_xl),
        (grad_time, grad_time),
        (grad_il, grad_xl),
        (grad_il, grad_time),
        (grad_xl, grad_time),
    )
    return jnp.stack(
        [
            cycle_box(left_part * right_part * cycle_mask, CIL, CXL)
            for left_part, right_part in factor_pairs
        ]
    )


def tensor_kernel(place, image, low_il, high_il, low_xl, high_xl, out, padded, boxed):
    padded[:2, 2 : CXL + 2] = low_il[...]
    padded[2 : CIL + 2, 2 : CXL + 2] = image[...]
    padded[CIL + 2 :, 2 : CXL + 2] = high_il[...]
    padded[:, :2] = low_xl[...]
    padded[:, CXL + 2 : CXL + 4] = high_xl[...]
    shape = (CXL + 2, 128)
    col = lax.broadcasted_iota(jnp.int32, shape, 0) + (place[2] * CXL - 1)
    lane = lax.broadcasted_iota(jnp.int32, shape, 1)
    inside = (col >= 0) & (col < CXL * place[3])

    def one_row(r, unused):
        row = place[0] * CIL + r - 1
        here = inside & (row >= 0) & (row < CIL * place[1])
        middle = padded[r + 1, 1 : CXL + 3]
        later = jnp.where(lane < 127, pltpu.roll(middle, 127, 1), 0.0)
        earlier = jnp.where(lane > 0, pltpu.roll(middle, 1, 1), 0.0)
        along = [
            (padded[r + 2, 1 : CXL + 3] - padded[r, 1 : CXL + 3]) * 0.5,
            (padded[r + 1, 2 : CXL + 4] - padded[r + 1, 0 : CXL + 2]) * 0.5,
            (later - earlier) * 0.5,
        ]
        along = [jnp.where(here, part, 0.0) for part in along]
        for k, (i, j) in enumerate(((0, 0), (1, 1), (2, 2), (0, 1), (0, 2), (1, 2))):
            product = along[i] * along[j]
            boxed[k, r] = (product[:CXL] + product[1 : CXL + 1]) + product[2:]
        return 0

    lax.fori_loop(0, CIL + 2, one_row, 0)

    def one_out(r, unused):
        for k in range(6):
            out[k, r] = ((boxed[k, r] + boxed[k, r + 1]) + boxed[k, r + 2]) / 9.0
        return 0

    lax.fori_loop(0, CIL, one_out, 0)


def tensor_call(place, image, halo, tokens=()):
    def kernel(*refs):
        tensor_kernel(*refs[:6], *refs[6 + len(tokens) :])

    return pl.pallas_call(
        kernel,
        out_shape=jax.ShapeDtypeStruct((6, CIL, CXL, 128), jnp.float32),
        in_specs=[IN_SMEM] + [IN_VMEM] * 5 + [IN_ANY] * len(tokens),
        out_specs=IN_VMEM,
        scratch_shapes=[
            pltpu.VMEM((CIL + 4, CXL + 8, 128), jnp.float32),
            pltpu.VMEM((6, CIL + 2, CXL, 128), jnp.float32),
        ],
        compiler_params=pltpu.CompilerParams(vmem_limit_bytes=VMEM_LIMIT),
        cost_estimate=LIGHT,
        name="tensor",
    )(place, image, *halo, *tokens)


def halo_of(image, side_il, side_xl):
    axis_il, count_il = side_il
    axis_xl, count_xl = side_xl
    up_il, up_xl = ([(i, i + 1) for i in range(n - 1)] for n in (count_il, count_xl))
    down_il, down_xl = ([(j, i) for i, j in up] for up in (up_il, up_xl))
    low_il = lax.ppermute(image[-2:], axis_il, up_il)
    high_il = lax.ppermute(image[:2], axis_il, down_il)

    def edge(cols):
        return jnp.concatenate([part[:, cols] for part in (low_il, image, high_il)], axis=0)

    low_xl = lax.ppermute(edge(slice(CXL - 2, CXL)), axis_xl, up_xl)
    high_xl = lax.ppermute(edge(slice(0, 2)), axis_xl, down_xl)
    return low_il, high_il, low_xl, high_xl


SWAP = [(0, 1), (1, 0)]


def along_z(value, step):
    return lax.ppermute(value, "z", [(i, (i + step) % 4) for i in range(4)])


def over(axis, value):
    return lax.ppermute(value, axis, SWAP)


def local_planes(traces, filter_taps, slot_block, slot_cells, pair_count):
    row_block = slot_cells.shape[3]
    capacity = slot_block.shape[2]
    samples = traces.shape[1]
    surveys, tap_count = filter_taps.shape
    x, core, z, y = (lax.axis_index(name) for name in ("x", "c", "z", "y"))
    other = 1 - core

    slot_live = jnp.arange(capacity, dtype=jnp.int32)[None, :] < pair_count[0][:, None]
    out_cells = jnp.where(slot_live[:, :, None], slot_cells[0], -1)
    own_cells = jnp.pad(out_cells, ((0, 0), (0, 1), (0, 0)), constant_values=-1)
    numbers = jnp.concatenate([slot_block[0], pair_count[0][:, None]], axis=1)

    def by_column(value):
        parts = value.reshape((2, 2, 4, 2) + value.shape[1:])
        return jnp.moveaxis(parts, 2, 3).reshape((8, 4) + value.shape[1:])

    arrived = lax.all_to_all(
        jnp.concatenate(
            [
                by_column(own_cells).reshape(8, 32, row_block),
                jnp.pad(by_column(numbers), ((0, 0), (0, 4), (0, row_block - 8))),
            ],
            axis=1,
        ),
        ("x", "c", "y"),
        0,
        0,
        tiled=True,
    )
    own_slots = (pair_count[0], numbers.reshape(256), own_cells.reshape(256, row_block))

    taps = jnp.pad(filter_taps, ((0, 0), (0, samples - tap_count))).reshape(surveys, 1, samples)
    rows_half = traces.shape[0] // 2
    (first_half,) = filter_call(0, traces, taps)
    second_half, matrices = filter_call(1, traces, taps)
    halves = [part.reshape(rows_half, samples) for part in (first_half, second_half)]

    spots = ((x, y), (1 - x, y), (x, 1 - y), (1 - x, 1 - y))
    orders = [lax.rem(z + step, 4) for step in range(4)]
    for at_x, at_y in spots:
        orders += [(at_x * 2 + at_core) * 2 + at_y for at_core in (core, other)]
    wanted = [(spot, core) for spot in spots[:3]] + [(spot, other) for spot in spots[:3]]
    wanted += [(spots[3], core), (spots[3], other)]
    wanted += [(spot, at_core) for spot in spots[:3] for at_core in (core, other)]
    for (at_x, at_y), at_core in wanted:
        orders += [((at_x * 2 + at_core) * 4 + at_z) * 2 + at_y for at_z in range(4)]
    orders = jnp.stack(orders)

    def spread(value, *tokens):
        from_x, from_y, turn_x, turn_y = gate(over("x", value), over("y", value), *tokens)
        return from_x, from_y, (over("y", turn_x), over("x", turn_y))

    def pairs(*pieces):
        return [part for piece in pieces for part in (piece, over("c", piece))]

    def near_stack(half, pieces, tokens=()):
        return stack_call(orders, 4, arrived, pieces, 6, None, 4, half == 0, False, tokens)[0]

    def far_stack(half, parts, before):
        pieces = [*parts, *(over("c", part) for part in parts)]
        return stack_call(orders, 10, arrived, pieces, 2, before, 4, half == 0, True)

    def sum_z(partial):
        return [partial[0]] + [along_z(partial[step], step) for step in (2, 1, 3)]

    def over_z(value):
        return lax.all_to_all(value, "z", 0, 0, tiled=True)

    def read(half, base, pieces, *rest, **named):
        return read_call(orders, base, own_slots, halves[half], pieces, *rest, **named)


    from_x, from_y, parts = spread(halves[0], halves[1], arrived, orders, *own_slots)
    near_0 = near_stack(0, pairs(halves[0], from_x, from_y))
    (own_1,) = tie([halves[1]], near_0)
    halves[1] = own_1
    partial_0 = far_stack(0, tie(parts, near_0), near_0)
    packed_0, stacked, fold = image_call(0, sum_z(partial_0), [], [])
    columns_0 = over_z(packed_0)
    from_x, from_y, parts = spread(own_1, packed_0)
    near_1 = near_stack(1, pairs(own_1, from_x, from_y))
    partial_1 = far_stack(1, tie(parts, near_1), near_1)
    from_x, from_y, parts = spread(columns_0, partial_1[0])
    own_layers = [columns_0, from_x, from_y]
    residual_0 = read(0, 12, own_layers, None)
    packed_1, image = image_call(1, sum_z(partial_1), [fold, stacked], [residual_0, *parts])
    columns_1 = over_z(packed_1)
    image = image.reshape(CIL, CXL, samples)
    halo = halo_of(image, (("x", "c"), 4), (("z", "y"), 8))
    place = jnp.stack([x * 2 + core, jnp.int32(4), z * 2 + y, jnp.int32(8)])
    own_layers = tie([*own_layers, *parts], packed_1)
    layers = [over("c", layer) for layer in own_layers]
    layers = layers[:3] + list(own_layers[3:]) + layers[3:]
    residual_0 = read(0, 24, layers, residual_0, tokens=[columns_1, *halo])
    structure_tensor = tensor_call(place, image, halo, [residual_0])
    residual_1 = read(1, 44, pairs(columns_1), None, tokens=[structure_tensor])
    from_x, from_y, parts = spread(columns_1, residual_1)
    residual_1 = read(1, 52, pairs(from_x, from_y), residual_1)
    parts = tie(parts, residual_1)
    layers = [*parts, *(over("c", part) for part in parts)]
    adjoint_traces = read(1, 36, layers, residual_1, matrices, residual_0)
    return (structure_tensor, adjoint_traces)


def filter_matrices(filter_taps, samples):
    lag_table = (
        jnp.arange(samples, dtype=jnp.int32)[None, :]
        - jnp.arange(samples, dtype=jnp.int32)[:, None]
    )
    tap_count = filter_taps.shape[1]
    inside = (lag_table >= 0) & (lag_table < tap_count)
    picked = filter_taps[:, jnp.clip(lag_table, 0, tap_count - 1)]
    return jnp.where(inside[None], picked, 0.0).astype(jnp.bfloat16)


def local(traces, filter_taps, slot_block, slot_cells, pair_count):
    count_il = lax.axis_size("il")
    count_xl = lax.axis_size("xl")
    devices = count_il * count_xl
    samples = traces.shape[1]
    row_block = slot_cells.shape[3]
    capacity = slot_block.shape[2]
    surveys = filter_taps.shape[0]
    blocks_here = traces.shape[0] // row_block
    cell_count = CIL * CXL
    group_size = 16
    slot_total = devices * capacity
    group_count = slot_total // group_size
    matrices = filter_matrices(filter_taps, samples)
    by_survey = traces.reshape(surveys, blocks_here // surveys * row_block, samples)
    filtered = jnp.einsum("sru,sut->srt", by_survey, matrices, preferred_element_type=jnp.float32)
    filtered = filtered.astype(jnp.bfloat16).reshape(blocks_here, row_block, samples)
    block_ids = slot_block[0].reshape(-1)
    outgoing = jnp.take(filtered, block_ids, axis=0).reshape(devices, capacity, row_block, samples)
    slot_live = jnp.arange(capacity, dtype=jnp.int32)[None, :] < pair_count[0][:, None]
    out_cells = jnp.where(slot_live[:, :, None], slot_cells[0], -1)
    incoming, in_cells = (
        lax.all_to_all(outgoing, ("il", "xl"), split_axis=0, concat_axis=0, tiled=True),
        lax.all_to_all(out_cells, ("il", "xl"), split_axis=0, concat_axis=0, tiled=True),
    )
    incoming = incoming.reshape(slot_total, row_block, samples)
    in_cells = in_cells.reshape(slot_total, row_block)
    cell_line = jnp.arange(cell_count, dtype=jnp.int32)

    def one_hot(group_cells):
        return (cell_line[:, None] == group_cells.reshape(1, -1)).astype(jnp.bfloat16)

    def add_group(running, group_blocks, group_cells):
        stacked, fold_counts = running
        selector = one_hot(group_cells)
        stacked = stacked + jnp.dot(
            selector, group_blocks.reshape(-1, samples), preferred_element_type=jnp.float32
        )
        fold_counts = fold_counts + jnp.sum(selector, axis=1, dtype=jnp.float32)
        return (stacked, fold_counts)

    initial = (jnp.zeros((cell_count, samples), jnp.float32), jnp.zeros((cell_count,), jnp.float32))

    def scan_step(running, scan_item):
        return (add_group(running, scan_item[0], scan_item[1]), None)

    (stacked, fold_counts), unused = lax.scan(
        scan_step,
        initial,
        (
            incoming.reshape(group_count, group_size, row_block, samples),
            in_cells.reshape(group_count, group_size, row_block),
        ),
    )
    stack_image = stacked / jnp.maximum(fold_counts, 1.0)[:, None]
    image_half = stack_image.astype(jnp.bfloat16)

    def read_group(group_cells):
        selector = one_hot(group_cells)
        picked = lax.dot_general(
            selector, image_half, (((0,), (0,)), ((), ())), preferred_element_type=jnp.float32
        )
        return picked.astype(jnp.bfloat16).reshape(group_size, row_block, samples)

    answer = lax.map(read_group, in_cells.reshape(group_count, group_size, row_block)).reshape(
        slot_total, row_block, samples
    )
    returned = lax.all_to_all(
        answer.reshape(devices, capacity, row_block, samples),
        ("il", "xl"),
        split_axis=0,
        concat_axis=0,
        tiled=True,
    )
    returned = returned.reshape(slot_total, row_block, samples)
    out_valid = (out_cells >= 0).reshape(slot_total, row_block, 1)
    zero_half = jnp.zeros((), jnp.bfloat16)
    sent_part = jnp.where(out_valid, outgoing.reshape(slot_total, row_block, samples), zero_half)
    back_part = jnp.where(out_valid, returned, zero_half)
    selector_rows = (
        block_ids[:, None] == jnp.arange(blocks_here, dtype=jnp.int32)[None, :]
    ).astype(jnp.bfloat16)
    residual = jnp.einsum(
        "sb,sit->bit", selector_rows, sent_part, preferred_element_type=jnp.float32
    )
    residual = residual - jnp.einsum(
        "sb,sit->bit", selector_rows, back_part, preferred_element_type=jnp.float32
    )
    residual_half = residual.astype(jnp.bfloat16).reshape(surveys, -1, samples)
    adjoint_traces = jnp.einsum(
        "srt,sut->sru", residual_half, matrices, preferred_element_type=jnp.float32
    ).reshape(traces.shape)
    padded = with_halo(
        stack_image.reshape(CIL, CXL, samples), (("il", count_il, 0), ("xl", count_xl, 1)), 2
    )
    structure_tensor = tensor(
        padded, (count_il, lax.axis_index("il")), (count_xl, lax.axis_index("xl"))
    )
    return (structure_tensor, adjoint_traces)


def solution(mesh):
    inner, names, body = mesh, (("il",), ("xl",)), local
    if mesh.devices.shape == (4, 8):
        inner = Mesh(mesh.devices.reshape(2, 2, 4, 2), ("x", "c", "z", "y"))
        names, body = (("x", "c"), ("z", "y")), local_planes
    il, xl = names
    both = il + xl
    return jax.shard_map(
        body,
        mesh=inner,
        in_specs=(
            P(both, None),
            P(),
            P(both, None, None),
            P(both, None, None, None),
            P(both, None),
        ),
        out_specs=(P(None, il, xl, None), P(both, None)),
        check_vma=False,
    )
```

time: 361 us -> 291 us (0.81)
  waiting for transfers between devices: 105 us -> 76.8 us
  other arithmetic: 17.5 us -> 2.32 us
  local copies, waits for them, and re-layouts: 35.4 us -> 22.3 us
  starting transfers between devices: 83.6 us -> 72.1 us
    ppermute x36, waiting for transfers between devices: 38.7 us -> 6.09 us  [over(): return lax.ppermute(value, axis, SWAP)]
    ppermute x12 -> x6, starting transfers between devices: 38.5 us -> 12.3 us  [along_z(): return lax.ppermute(value, 'z', [(i, (i + step) % 4) for i in range(4)])]
    all_to_all x1 -> x3, waiting for transfers between devices: 5.21 us -> 27.4 us  [the longest x2 16.4 us: over_z(): return lax.all_to_all(value, 'z', 0, 0, tiled=True)]
    all_to_all x1 -> x3, starting transfers between devices: 3.37 us -> 23 us  [the longest x2 19.7 us: over_z(): return lax.all_to_all(value, 'z', 0, 0, tiled=True)]
    ppermute x12 -> x6, waiting for transfers between devices: 56.4 us -> 39.9 us  [along_z(): return lax.ppermute(value, 'z', [(i, (i + step) % 4) for i in range(4)])]
    unnamed x6 -> x1, other arithmetic: 8.39 us -> 0.66 us
    slice x11 -> x4, local copies, waits for them, and re-layouts: 9.2 us -> 1.83 us  [the longest x3 1 us: edge(): part[:, cols]]
    unnamed x75 -> x89, local copies, waits for them, and re-layouts: 22.5 us -> 16.8 us
  transfers between devices with their start and end apart: 53 -> 49, of which waited for: 14 -> 17; matrix products, arithmetic and copies ran while one was open for 9% -> 2% of each run, Pallas kernels for 28% -> 33%
where the time goes in v3:
time: 291 us; the launch traced here: 289 us
  Pallas kernels  114 us (39%)
  waiting for transfers between devices  76.8 us (26%)
  starting transfers between devices  72.1 us (25%)
  local copies, waits for them, and re-layouts  22.3 us (8%)
    pallas_call x5, Pallas kernels, read_call(): pl.pallas_call(functools.partial(read_kernel, (sizes, first, last, len(to...  45.1 us
    ppermute x6, waiting for transfers between devices, along_z(): return lax.ppermute(value, 'z', [(i, (i + step) % 4) for i in range(4)])  39.9 us
    pallas_call x4, Pallas kernels, stack_call(): pl.pallas_call(functools.partial(stack_kernel, spec), out_shape=single if...  37.5 us
    ppermute x36, starting transfers between devices, over(): return lax.ppermute(value, axis, SWAP)  29.4 us
    all_to_all x2, starting transfers between devices, over_z(): return lax.all_to_all(value, 'z', 0, 0, tiled=True)  19.7 us
    unnamed x89, local copies, waits for them, and re-layouts  16.8 us
    all_to_all x2, waiting for transfers between devices, over_z(): return lax.all_to_all(value, 'z', 0, 0, tiled=True)  16.4 us
    ppermute x6, starting transfers between devices, along_z(): return lax.ppermute(value, 'z', [(i, (i + step) % 4) for i in range(4)])  12.3 us
  transfers between devices with their start and end apart: 49, of which 17 were waited for; matrix products, arithmetic and copies ran while one was open for 2% of the time, Pallas kernels for 33%

profile of v3, /device:TPU:0, one launch (start us, length us, event | category | flops | bytes accessed | tf_op | source)
XLA Modules:
  0.0 289.0 jit_solution(3786870204197400444)
XLA Ops:
  2.0 4.4 %filter_0.1 = bf16[12,320,128]{2,1,0:T(8,128)(2,1)} custom-call(f32[12,1,128]{2,1,0:T(1,128)} %reshape.69.taps, bf16[12,640,128]{2,1,0:T(8,128)(2,1)} %bitcast.82), custom_call_target="tpu_custom_call" | custom-call | tf_op jit(solution)/shard_map/filter_0/pallas_call | solution.py:126
  6.4 3.0 %collective-permute-start.2 = (bf16[3840,128]{1,0:T(8,128)(2,1)}, bf16[3840,128]{1,0:T(8,128)(2,1)S(1)}, u32[]{:S(2)}, u32[]{:S(2)}) collective-permute-start(bf16[3840,128]{1,0:T(8,128)(2,1)} %bitcast.76), channel_id=1, source_target_pairs={{0,1},{1,0},{2,3},{3,2},{4,5},{5,4},{6,7},{7,6},{8,9},{9,8},{10,11... | collective-permute-start | bytes 2949128 | tf_op jit(solution)/shard_map/ppermute | solution.py:612
  9.4 1.5 collective-permute-start.1
  13.3 3.4 %all-to-all-start = ((s32[8,40,128]{2,1,0:T(8,128)}), s32[8,40,128]{2,1,0:T(8,128)S(1)}, u32[]{:S(2)}, u32[]{:S(2)}) async-start(s32[8,40,128]{2,1,0:T(8,128)} %pad_add_fusion), calls=%async_computation | async-start | bytes 327680 | tf_op jit(solution)/shard_map/all_to_all | solution.py:632
  17.8 4.4 %filter_1.1 = (bf16[12,320,128]{2,1,0:T(8,128)(2,1)}, bf16[12,128,128]{2,1,0:T(8,128)(2,1)}) custom-call(f32[12,1,128]{2,1,0:T(1,128)} %reshape.69.taps, bf16[12,640,128]{2,1,0:T(8,128)(2,1)} %bitcast.83), custom_call_target="tpu_custom_call" | custom-call | tf_op jit(solution)/shard_map/filter_1/pallas_call | solution.py:126
  23.6 10.9 %all-to-all-done.refs_1_.cells = s32[8,40,128]{2,1,0:T(8,128)S(1)} async-done(((s32[8,40,128]{2,1,0:T(8,128)}), s32[8,40,128]{2,1,0:T(8,128)S(1)}, u32[]{:S(2)}, u32[]{:S(2)}) %all-to-all-start) | async-done | bytes 163872 | tf_op jit(solution)/shard_map/all_to_all | solution.py:632
  35.9 2.1 gate.4
  38.6 1.2 collective-permute-start.7
  39.8 1.5 collective-permute-start.8
  41.3 0.9 collective-permute-done.4.refs_5_
  42.3 1.0 copy-done.42
  43.3 11.6 %stack.220.refs_1_.refs_2_.refs_4_ = f32[4,400,256]{2,1,0:T(8,128)} custom-call(s32[68]{0:T(128)} %stack.219.refs_2_.order, s32[8,40,128]{2,1,0:T(8,128)} %copy-done.9, bf16[3840,128]{1,0:T(8,128)(2,1)} %bitcast.79, bf16[3840,128]{1,0:T(8,128)(2,1)} %collective-permute-done.refs_1_, bf16[3840,128]{1,0:T(8,128)(2,1)} %get-tuple-element.45.refs_2_, ...), custom_call_target="tpu_custom_call" | custom-call | flops 34359738368 | bytes 1048576 | tf_op jit(solution)/shard_map/stack/pallas_call | solution.py:253
  56.5 1.0 collective-permute-start.9
  57.5 1.6 collective-permute-start.6
  60.8 7.8 %stack.221 = (f32[400,256]{1,0:T(8,128)}, f32[400,256]{1,0:T(8,128)}, f32[400,256]{1,0:T(8,128)}, f32[400,256]{1,0:T(8,128)}) custom-call(s32[68]{0:T(128)} %stack.219.refs_2_.order, s32[8,40,128]{2,1,0:T(8,128)} %copy-done.9, bf16[1920,128]{1,0:T(8,128)(2,1)} %get-tuple-element.49.refs_0_, bf16[1920,128]{1,0:T(8,128)(2,1)} %get-tuple-element.50.refs_1_, ...), custom_call_target="tpu_custom_call" | custom-call | flops 1 | bytes 1 | tf_op jit(solution)/shard_map/stack/pallas_call | solution.py:253
  68.6 4.5 %collective-permute-start.11 = (f32[400,256]{1,0:T(8,128)}, f32[400,256]{1,0:T(8,128)S(1)}, u32[]{:S(2)}, u32[]{:S(2)}) collective-permute-start(f32[400,256]{1,0:T(8,128)} %get-tuple-element.52), channel_id=1, source_target_pairs={{0,4},{2,6},{4,0},{6,2},{1,5},{3,7},{5,1},{7,3},{8,12},{10,14},{12... | collective-permute-start | bytes 1228808 | tf_op jit(solution)/shard_map/ppermute | solution.py:608
  73.8 3.1 %collective-permute-start.13 = (f32[400,256]{1,0:T(8,128)}, f32[400,256]{1,0:T(8,128)}, u32[]{:S(2)}, u32[]{:S(2)}) collective-permute-start(f32[400,256]{1,0:T(8,128)} %get-tuple-element.54), channel_id=1, source_target_pairs={{0,6},{2,0},{4,2},{6,4},{1,7},{3,1},{5,3},{7,5},{8,14},{10,8},{12,... | collective-permute-start | bytes 1228808 | tf_op jit(solution)/shard_map/ppermute | solution.py:608
  76.9 24.3 %collective-permute-done.11.refs_1_ = f32[400,256]{1,0:T(8,128)S(1)} collective-permute-done((f32[400,256]{1,0:T(8,128)}, f32[400,256]{1,0:T(8,128)S(1)}, u32[]{:S(2)}, u32[]{:S(2)}) %collective-permute-start.11) | collective-permute-done | bytes 409632 | tf_op jit(solution)/shard_map/ppermute | solution.py:608
  101.2 1.4 collective-permute-done.13.refs_3_
  102.6 2.8 image_0.1
  105.4 11.0 %all-to-all-start.1 = ((bf16[4,256,384]{2,1,0:T(8,128)(2,1)}), bf16[4,256,384]{2,1,0:T(8,128)(2,1)S(1)}, u32[]{:S(2)}, u32[]{:S(2)}) async-start(bf16[4,256,384]{2,1,0:T(8,128)(2,1)} %bitcast.99), calls=%async_computation.1 | async-start | bytes 1572864 | tf_op jit(solution)/shard_map/all_to_all | solution.py:682
  116.4 0.9 copy-done.18
  117.3 2.1 gate.5
  120.1 1.7 collective-permute-start.15
  121.9 14.4 %all-to-all-done.1 = bf16[4,256,384]{2,1,0:T(8,128)(2,1)S(1)} async-done(((bf16[4,256,384]{2,1,0:T(8,128)(2,1)}), bf16[4,256,384]{2,1,0:T(8,128)(2,1)S(1)}, u32[]{:S(2)}, u32[]{:S(2)}) %all-to-all-start.1) | async-done | bytes 786464 | tf_op jit(solution)/shard_map/all_to_all | solution.py:682
  136.3 1.4 collective-permute-start.24
  137.7 10.7 %stack.222.refs_2_.refs_4_ = f32[4,384,256]{2,1,0:T(8,128)} custom-call(s32[68]{0:T(128)} %stack.219.refs_2_.order, s32[8,40,128]{2,1,0:T(8,128)} %copy-done.9, bf16[3840,128]{1,0:T(8,128)(2,1)} %tie.5.refs_0_.own, bf16[3840,128]{1,0:T(8,128)(2,1)} %collective-permute-done.16.refs_1_, bf16[3840,128]{1,0:T(8,128)(2,1)} %get-tuple-element.58.refs_2_, ...), custom_call_target="tpu_custom_call" | custom-call | flops 34359738368 | bytes 1048576 | tf_op jit(solution)/shard_map/stack/pallas_call | solution.py:253
  150.5 1.6 collective-permute-done.19.refs_2_
  152.9 0.8 copy-done.25
  153.7 7.3 %stack.223 = (f32[384,256]{1,0:T(8,128)}, f32[384,256]{1,0:T(8,128)}, f32[384,256]{1,0:T(8,128)}, f32[384,256]{1,0:T(8,128)}) custom-call(s32[68]{0:T(128)} %stack.219.refs_2_.order, s32[8,40,128]{2,1,0:T(8,128)} %copy-done.9, bf16[1920,128]{1,0:T(8,128)(2,1)} %get-tuple-element.60.refs_0_, bf16[1920,128]{1,0:T(8,128)(2,1)} %get-tuple-element.61.refs_1_, ...), custom_call_target="tpu_custom_call" | custom-call | flops 1 | bytes 1 | tf_op jit(solution)/shard_map/stack/pallas_call | solution.py:253
  161.2 3.2 %collective-permute-start.22 = (f32[384,256]{1,0:T(8,128)}, f32[384,256]{1,0:T(8,128)S(1)}, u32[]{:S(2)}, u32[]{:S(2)}) collective-permute-start(f32[384,256]{1,0:T(8,128)} %get-tuple-element.64), channel_id=1, source_target_pairs={{0,2},{2,4},{4,6},{6,0},{1,3},{3,5},{5,7},{7,1},{8,10},{10,12},{12... | collective-permute-start | bytes 1179656 | tf_op jit(solution)/shard_map/ppermute | solution.py:608
  165.0 0.9 copy-done.3
  166.1 1.9 gate.6
  168.0 1.6 collective-permute-start.26
  169.9 7.9 %read.5.refs_6_.refs_7_ = f32[3840,128]{1,0:T(8,128)} custom-call(s32[68]{0:T(128)} %stack.219.refs_2_.order, s32[32]{0:T(128)} %bitcast.110, s32[256]{0:T(256)} %reshape.73.refs_4_.blocks, s32[256,128]{1,0:T(8,128)} %bitcast.94, bf16[3840,128]{1,0:T(8,128)(2,1)} %bitcast.80, bf16[1024,384]{1,0:T(8,128)(2,1)} %bitcast.91, ...), custom_call_target="tpu_custom_call" | custom-call | flops 1 | bytes 1 | tf_op jit(solution)/shard_map/read/pallas_call | solution.py:449
  177.8 12.8 %collective-permute-done.21.refs_1_ = f32[384,256]{1,0:T(8,128)S(1)} collective-permute-done((f32[384,256]{1,0:T(8,128)}, f32[384,256]{1,0:T(8,128)S(1)}, u32[]{:S(2)}, u32[]{:S(2)}) %collective-permute-start.21) | collective-permute-done | bytes 393248 | tf_op jit(solution)/shard_map/ppermute | solution.py:608
  190.6 1.4 collective-permute-done.23.refs_3_
  193.1 4.1 %image_1.1 = (bf16[1024,384]{1,0:T(8,128)(2,1)}, f32[1536,128]{1,0:T(8,128)}) custom-call(f32[384,256]{1,0:T(8,128)} %get-tuple-element.62.refs_0_, f32[384,256]{1,0:T(8,128)} %copy-done.31, f32[384,256]{1,0:T(8,128)} %copy-done.32, f32[384,256]{1,0:T(8,128)} %copy-done.33, f32[16,256]{1,0:T(8,128)} %get-tuple-element.66.refs_4_, ...), custom_call_target="tpu_custom_call" | custom-call | flops 1 | bytes 1 | tf_op jit(solution)/shard_map/image_1/pallas_call | solution.py:323
  197.1 8.7 %all-to-all-start.2 = ((bf16[4,256,384]{2,1,0:T(8,128)(2,1)}), bf16[4,256,384]{2,1,0:T(8,128)(2,1)S(1)}, u32[]{:S(2)}, u32[]{:S(2)}) async-start(bf16[4,256,384]{2,1,0:T(8,128)(2,1)} %bitcast.100), calls=%async_computation.2 | async-start | bytes 1572864 | tf_op jit(solution)/shard_map/all_to_all | solution.py:682
  205.8 0.8 fusion.1
  206.6 1.6 collective-permute-start.28
  208.4 1.0 fusion
  209.4 1.3 collective-permute-start.29
  210.7 1.2 collective-permute-start.35
  212.6 3.3 %collective-permute-start.30 = (f32[36,2,128]{2,1,0:T(2,128)S(1)}, f32[36,2,128]{2,1,0:T(2,128)S(1)}, u32[]{:S(2)}, u32[]{:S(2)}) collective-permute-start(f32[36,2,128]{2,1,0:T(2,128)S(1)} %pad_maximum_fusion), channel_id=1, source_target_pairs={{0,1},{1,2},{2,3},{3,4},{4,5},{5,6},{6,7},{8,9},{9,10},{10,11},{11... | collective-permute-start | bytes 110600 | tf_op jit(solution)/shard_map/ppermute | solution.py:599
  215.9 1.3 collective-permute-start.31
  217.5 2.1 collective-permute-start.33
  219.6 2.6 collective-permute-done.31.refs_12_.refs_5_
  222.2 2.2 collective-permute-start.34
  224.4 2.0 all-to-all-done.2
  226.5 2.4 collective-permute-start.38
  229.7 11.4 %read.6.refs_6_.refs_5_ = f32[3840,128]{1,0:T(8,128)} custom-call(s32[68]{0:T(128)} %stack.219.refs_2_.order, s32[32]{0:T(128)} %bitcast.111, s32[256]{0:T(256)} %reshape.73.refs_4_.blocks, s32[256,128]{1,0:T(8,128)} %bitcast.95, bf16[3840,128]{1,0:T(8,128)(2,1)} %bitcast.81, bf16[1024,384]{1,0:T(8,128)(2,1)} %copy-done.19, ...), custom_call_target="tpu_custom_call" | custom-call | flops 1 | bytes 1 | tf_op jit(solution)/shard_map/read/pallas_call | solution.py:449
  241.1 7.7 %tensor.1.refs_2_ = f32[6,32,48,128]{3,2,1,0:T(8,128)} custom-call(s32[4]{0:T(128)} %pad_add_fusion.2.refs_0_, f32[32,48,128]{2,1,0:T(8,128)} %bitcast.103, f32[2,48,128]{2,1,0:T(8,128)} %copy-done.34, f32[2,48,128]{2,1,0:T(8,128)} %copy-done.35, f32[36,2,128]{2,1,0:T(2,128)} %copy-done.36, f32[36,2,128]{2,1,0:T(2,128)} %copy-done.37, ...), custom_call_target="tpu_custom_call" | custom-call | flops 1 | bytes 1 | tf_op jit(solution)/shard_map/tensor/pallas_call | solution.py:573
  248.8 6.4 %read.7.refs_0_.refs_4_ = f32[3840,128]{1,0:T(8,128)} custom-call(s32[68]{0:T(128)} %stack.219.refs_2_.order, s32[32]{0:T(128)} %bitcast.112, s32[256]{0:T(256)} %reshape.73.refs_4_.blocks, s32[256,128]{1,0:T(8,128)} %bitcast.96, bf16[3840,128]{1,0:T(8,128)(2,1)} %tie.5.refs_0_.own, bf16[1024,384]{1,0:T(8,128)(2,1)} %bitcast.88, ...), custom_call_target="tpu_custom_call" | custom-call | flops 1 | bytes 1 | tf_op jit(solution)/shard_map/read/pallas_call | solution.py:449
  255.3 0.9 copy-done.7
  256.2 0.9 copy-done.8
  257.1 1.9 gate.7
  259.6 1.2 collective-permute-start.40
  260.8 2.0 collective-permute-start.41
  262.8 1.0 copy-done.20
  263.8 0.9 copy-done.21
  264.7 10.2 %read.8.refs_2_.refs_6_ = f32[3840,128]{1,0:T(8,128)} custom-call(s32[68]{0:T(128)} %stack.219.refs_2_.order, s32[32]{0:T(128)} %bitcast.113, s32[256]{0:T(256)} %reshape.73.refs_4_.blocks, s32[256,128]{1,0:T(8,128)} %bitcast.97, bf16[3840,128]{1,0:T(8,128)(2,1)} %tie.5.refs_0_.own, bf16[1024,384]{1,0:T(8,128)(2,1)} %get-tuple-element.81.refs_0_, ...), custom_call_target="tpu_custom_call" | custom-call | flops 1 | bytes 1 | tf_op jit(solution)/shard_map/read/pallas_call | solution.py:449
  277.0 1.4 collective-permute-done.44.refs_2_
  279.7 9.1 %read.9 = f32[7680,128]{1,0:T(8,128)} custom-call(s32[68]{0:T(128)} %stack.219.refs_2_.order, s32[32]{0:T(128)} %bitcast.114, s32[256]{0:T(256)} %reshape.73.refs_4_.blocks, s32[256,128]{1,0:T(8,128)} %bitcast.98, bf16[3840,128]{1,0:T(8,128)(2,1)} %tie.5.refs_0_.own, bf16[512,384]{1,0:T(8,128)(2,1)} %get-tuple-element.83.refs_0_, ...), custom_call_target="tpu_custom_call" | custom-call | flops 1 | bytes 1 | tf_op jit(solution)/shard_map/read/pallas_call | solution.py:449
  (169 shorter events, 23.9 us)
Async XLA Ops:
  0.6 10.8 %copy-start.39 = (s32[1,32]{1,0:T(1,128)S(1)}, s32[1,32]{1,0:T(1,128)}, u32[]{:S(2)}) copy-start(s32[1,32]{1,0:T(1,128)} %param.9) | copy-start | bytes 388
  0.6 11.5 %copy-start.40 = (s32[1,32,7]{1,0,2:T(1,128)S(1)}, s32[1,32,7]{1,0,2:T(1,128)}, u32[]{:S(2)}) copy-start(s32[1,32,7]{1,0,2:T(1,128)} %param.7) | copy-start | bytes 2692
  0.7 11.7 %copy-start.38 = (s32[1,32,7,128]{3,1,2,0:T(8,128)S(1)}, s32[1,32,7,128]{3,1,2,0:T(8,128)}, u32[]{:S(2)}) copy-start(s32[1,32,7,128]{3,1,2,0:T(8,128)} %param.8) | copy-start | bytes 344068
  6.4 28.2 %collective-permute-start.2 = (bf16[3840,128]{1,0:T(8,128)(2,1)}, bf16[3840,128]{1,0:T(8,128)(2,1)S(1)}, u32[]{:S(2)}, u32[]{:S(2)}) collective-permute-start(bf16[3840,128]{1,0:T(8,128)(2,1)} %bitcast.76), channel_id=1, source_target_pairs={{0,1},{1,0},{2,3},{3,2},{4,5},{5,4},{6,7},{7,6},{8,9},{9,8},{10,11... | collective-permute-start | bytes 2949128 | tf_op jit(solution)/shard_map/ppermute | solution.py:612
  9.4 25.2 %collective-permute-start.1 = (bf16[3840,128]{1,0:T(8,128)(2,1)}, bf16[3840,128]{1,0:T(8,128)(2,1)S(1)}, u32[]{:S(2)}, u32[]{:S(2)}) collective-permute-start(bf16[3840,128]{1,0:T(8,128)(2,1)} %bitcast.77), channel_id=1, source_target_pairs={{0,16},{16,0},{1,17},{17,1},{2,18},{18,2},{3,19},{19,3},{4,20},{20... | collective-permute-start | bytes 2949128 | tf_op jit(solution)/shard_map/ppermute | solution.py:612
  13.3 21.3 %all-to-all-start = ((s32[8,40,128]{2,1,0:T(8,128)}), s32[8,40,128]{2,1,0:T(8,128)S(1)}, u32[]{:S(2)}, u32[]{:S(2)}) async-start(s32[8,40,128]{2,1,0:T(8,128)} %pad_add_fusion), calls=%async_computation | async-start | bytes 327680 | tf_op jit(solution)/shard_map/all_to_all | solution.py:632
  16.7 24.6 %collective-permute-start = (bf16[3840,128]{1,0:T(8,128)(2,1)}, bf16[3840,128]{1,0:T(8,128)(2,1)}, u32[]{:S(2)}, u32[]{:S(2)}) collective-permute-start(bf16[3840,128]{1,0:T(8,128)(2,1)} %bitcast.78), channel_id=1, source_target_pairs={{0,8},{8,0},{1,9},{9,1},{2,10},{10,2},{3,11},{11,3},{4,12},{12,4},... | collective-permute-start | bytes 2949128 | tf_op jit(solution)/shard_map/ppermute | solution.py:612
  38.0 3.3 %collective-permute-start.3 = (bf16[3840,128]{1,0:T(8,128)(2,1)}, bf16[3840,128]{1,0:T(8,128)(2,1)S(1)}, u32[]{:S(2)}, u32[]{:S(2)}) collective-permute-start(bf16[3840,128]{1,0:T(8,128)(2,1)} %get-tuple-element.45.refs_2_), channel_id=1, source_target_pairs={{0,8},{8,0},{1,9},{9,1},{2,10},{10,2},{3,11},{11,3},{4,12},{12,4},... | collective-permute-start | bytes 2949128 | tf_op jit(solution)/shard_map/ppermute | solution.py:612
  38.1 4.2 %collective-permute-start.4 = (bf16[3840,128]{1,0:T(8,128)(2,1)}, bf16[3840,128]{1,0:T(8,128)(2,1)S(1)}, u32[]{:S(2)}, u32[]{:S(2)}) collective-permute-start(bf16[3840,128]{1,0:T(8,128)(2,1)} %get-tuple-element.46.refs_4_), channel_id=1, source_target_pairs={{0,8},{8,0},{1,9},{9,1},{2,10},{10,2},{3,11},{11,3},{4,12},{12,4},... | collective-permute-start | bytes 2949128 | tf_op jit(solution)/shard_map/ppermute | solution.py:612
  38.6 16.3 %collective-permute-start.7 = (bf16[1920,128]{1,0:T(8,128)(2,1)}, bf16[1920,128]{1,0:T(8,128)(2,1)S(1)}, u32[]{:S(2)}, u32[]{:S(2)}) collective-permute-start(bf16[1920,128]{1,0:T(8,128)(2,1)} %get-tuple-element.47), channel_id=1, source_target_pairs={{0,1},{1,0},{2,3},{3,2},{4,5},{5,4},{6,7},{7,6},{8,9},{9,8},{10,11... | collective-permute-start | bytes 1474568 | tf_op jit(solution)/shard_map/ppermute | solution.py:612
  39.8 15.1 %collective-permute-start.8 = (bf16[1920,128]{1,0:T(8,128)(2,1)}, bf16[1920,128]{1,0:T(8,128)(2,1)S(1)}, u32[]{:S(2)}, u32[]{:S(2)}) collective-permute-start(bf16[1920,128]{1,0:T(8,128)(2,1)} %get-tuple-element.48), channel_id=1, source_target_pairs={{0,16},{16,0},{1,17},{17,1},{2,18},{18,2},{3,19},{19,3},{4,20},{20... | collective-permute-start | bytes 1474568 | tf_op jit(solution)/shard_map/ppermute | solution.py:612
  56.5 2.7 collective-permute-start.9
  57.5 2.4 collective-permute-start.10
  57.5 58.9 %collective-permute-start.6 = (bf16[3840,128]{1,0:T(8,128)(2,1)}, bf16[3840,128]{1,0:T(8,128)(2,1)S(1)}, u32[]{:S(2)}, u32[]{:S(2)}) collective-permute-start(bf16[3840,128]{1,0:T(8,128)(2,1)} %tie.5.refs_0_.own), channel_id=1, source_target_pairs={{0,1},{1,0},{2,3},{3,2},{4,5},{5,4},{6,7},{7,6},{8,9},{9,8},{10,11... | collective-permute-start | bytes 2949128 | tf_op jit(solution)/shard_map/ppermute | solution.py:612
  59.0 57.4 %collective-permute-start.5 = (bf16[3840,128]{1,0:T(8,128)(2,1)}, bf16[3840,128]{1,0:T(8,128)(2,1)}, u32[]{:S(2)}, u32[]{:S(2)}) collective-permute-start(bf16[3840,128]{1,0:T(8,128)(2,1)} %tie.5.refs_0_.own), channel_id=1, source_target_pairs={{0,16},{16,0},{1,17},{17,1},{2,18},{18,2},{3,19},{19,3},{4,20},{20... | collective-permute-start | bytes 2949128 | tf_op jit(solution)/shard_map/ppermute | solution.py:612
  68.6 47.8 %copy-start = (bf16[3840,128]{1,0:T(8,128)(2,1)S(1)}, bf16[3840,128]{1,0:T(8,128)(2,1)}, u32[]{:S(2)}) copy-start(bf16[3840,128]{1,0:T(8,128)(2,1)} %tie.5.refs_0_.own) | copy-start | bytes 2949124
  68.6 32.6 %collective-permute-start.11 = (f32[400,256]{1,0:T(8,128)}, f32[400,256]{1,0:T(8,128)S(1)}, u32[]{:S(2)}, u32[]{:S(2)}) collective-permute-start(f32[400,256]{1,0:T(8,128)} %get-tuple-element.52), channel_id=1, source_target_pairs={{0,4},{2,6},{4,0},{6,2},{1,5},{3,7},{5,1},{7,3},{8,12},{10,14},{12... | collective-permute-start | bytes 1228808 | tf_op jit(solution)/shard_map/ppermute | solution.py:608
  73.1 28.1 %collective-permute-start.12 = (f32[400,256]{1,0:T(8,128)}, f32[400,256]{1,0:T(8,128)S(1)}, u32[]{:S(2)}, u32[]{:S(2)}) collective-permute-start(f32[400,256]{1,0:T(8,128)} %get-tuple-element.53), channel_id=1, source_target_pairs={{0,2},{2,4},{4,6},{6,0},{1,3},{3,5},{5,7},{7,1},{8,10},{10,12},{12... | collective-permute-start | bytes 1228808 | tf_op jit(solution)/shard_map/ppermute | solution.py:608
  73.8 28.8 %collective-permute-start.13 = (f32[400,256]{1,0:T(8,128)}, f32[400,256]{1,0:T(8,128)}, u32[]{:S(2)}, u32[]{:S(2)}) collective-permute-start(f32[400,256]{1,0:T(8,128)} %get-tuple-element.54), channel_id=1, source_target_pairs={{0,6},{2,0},{4,2},{6,4},{1,7},{3,1},{5,3},{7,5},{8,14},{10,8},{12,... | collective-permute-start | bytes 1228808 | tf_op jit(solution)/shard_map/ppermute | solution.py:608
  101.2 1.4 copy-start.26
  101.2 1.4 copy-start.27
  105.4 30.9 %all-to-all-start.1 = ((bf16[4,256,384]{2,1,0:T(8,128)(2,1)}), bf16[4,256,384]{2,1,0:T(8,128)(2,1)S(1)}, u32[]{:S(2)}, u32[]{:S(2)}) async-start(bf16[4,256,384]{2,1,0:T(8,128)(2,1)} %bitcast.99), calls=%async_computation.1 | async-start | bytes 1572864 | tf_op jit(solution)/shard_map/all_to_all | solution.py:682
  116.4 5.5 %collective-permute-start.16 = (bf16[3840,128]{1,0:T(8,128)(2,1)S(1)}, bf16[3840,128]{1,0:T(8,128)(2,1)}, u32[]{:S(2)}, u32[]{:S(2)}) collective-permute-start(bf16[3840,128]{1,0:T(8,128)(2,1)S(1)} %copy-done), channel_id=1, source_target_pairs={{0,8},{8,0},{1,9},{9,1},{2,10},{10,2},{3,11},{11,3},{4,12},{12,4},... | collective-permute-start | bytes 2949128 | tf_op jit(solution)/shard_map/ppermute | solution.py:612
  119.4 16.9 %collective-permute-start.17 = (bf16[3840,128]{1,0:T(8,128)(2,1)}, bf16[3840,128]{1,0:T(8,128)(2,1)}, u32[]{:S(2)}, u32[]{:S(2)}) collective-permute-start(bf16[3840,128]{1,0:T(8,128)(2,1)} %get-tuple-element.58.refs_2_), channel_id=1, source_target_pairs={{0,8},{8,0},{1,9},{9,1},{2,10},{10,2},{3,11},{11,3},{4,12},{12,4},... | collective-permute-start | bytes 2949128 | tf_op jit(solution)/shard_map/ppermute | solution.py:612
  120.0 17.7 %collective-permute-start.18 = (bf16[3840,128]{1,0:T(8,128)(2,1)}, bf16[3840,128]{1,0:T(8,128)(2,1)}, u32[]{:S(2)}, u32[]{:S(2)}) collective-permute-start(bf16[3840,128]{1,0:T(8,128)(2,1)} %get-tuple-element.59.refs_4_), channel_id=1, source_target_pairs={{0,8},{8,0},{1,9},{9,1},{2,10},{10,2},{3,11},{11,3},{4,12},{12,4},... | collective-permute-start | bytes 2949128 | tf_op jit(solution)/shard_map/ppermute | solution.py:612
  120.0 28.4 %collective-permute-start.14 = (bf16[1920,128]{1,0:T(8,128)(2,1)}, bf16[1920,128]{1,0:T(8,128)(2,1)S(1)}, u32[]{:S(2)}, u32[]{:S(2)}) collective-permute-start(bf16[1920,128]{1,0:T(8,128)(2,1)} %get-tuple-element.56), channel_id=1, source_target_pairs={{0,1},{1,0},{2,3},{3,2},{4,5},{5,4},{6,7},{7,6},{8,9},{9,8},{10,11... | collective-permute-start | bytes 1474568 | tf_op jit(solution)/shard_map/ppermute | solution.py:612
  120.1 28.3 %collective-permute-start.15 = (bf16[1920,128]{1,0:T(8,128)(2,1)}, bf16[1920,128]{1,0:T(8,128)(2,1)S(1)}, u32[]{:S(2)}, u32[]{:S(2)}) collective-permute-start(bf16[1920,128]{1,0:T(8,128)(2,1)} %get-tuple-element.57), channel_id=1, source_target_pairs={{0,16},{16,0},{1,17},{17,1},{2,18},{18,2},{3,19},{19,3},{4,20},{20... | collective-permute-start | bytes 1474568 | tf_op jit(solution)/shard_map/ppermute | solution.py:612
  136.3 12.2 %copy-start.2 = (bf16[4,256,384]{2,1,0:T(8,128)(2,1)}, bf16[4,256,384]{2,1,0:T(8,128)(2,1)S(1)}, u32[]{:S(2)}) copy-start(bf16[4,256,384]{2,1,0:T(8,128)(2,1)S(1)} %all-to-all-done.1) | copy-start | bytes 2359300
  136.3 28.7 %collective-permute-start.25 = (bf16[1024,384]{1,0:T(8,128)(2,1)S(1)}, bf16[1024,384]{1,0:T(8,128)(2,1)S(1)}, u32[]{:S(2)}, u32[]{:S(2)}) collective-permute-start(bf16[1024,384]{1,0:T(8,128)(2,1)S(1)} %bitcast.89), channel_id=1, source_target_pairs={{0,1},{1,0},{2,3},{3,2},{4,5},{5,4},{6,7},{7,6},{8,9},{9,8},{10,11... | collective-permute-start | bytes 2359304 | tf_op jit(solution)/shard_map/ppermute | solution.py:612
  136.3 28.7 %collective-permute-start.24 = (bf16[1024,384]{1,0:T(8,128)(2,1)S(1)}, bf16[1024,384]{1,0:T(8,128)(2,1)S(1)}, u32[]{:S(2)}, u32[]{:S(2)}) collective-permute-start(bf16[1024,384]{1,0:T(8,128)(2,1)S(1)} %bitcast.90), channel_id=1, source_target_pairs={{0,16},{16,0},{1,17},{17,1},{2,18},{18,2},{3,19},{19,3},{4,20},{20... | collective-permute-start | bytes 2359304 | tf_op jit(solution)/shard_map/ppermute | solution.py:612
  150.0 2.1 collective-permute-start.19
  150.0 2.8 collective-permute-start.20
  161.0 29.6 %collective-permute-start.21 = (f32[384,256]{1,0:T(8,128)}, f32[384,256]{1,0:T(8,128)S(1)}, u32[]{:S(2)}, u32[]{:S(2)}) collective-permute-start(f32[384,256]{1,0:T(8,128)} %get-tuple-element.63), channel_id=1, source_target_pairs={{0,4},{2,6},{4,0},{6,2},{1,5},{3,7},{5,1},{7,3},{8,12},{10,14},{12... | collective-permute-start | bytes 1179656 | tf_op jit(solution)/shard_map/ppermute | solution.py:608
  161.2 29.5 %collective-permute-start.22 = (f32[384,256]{1,0:T(8,128)}, f32[384,256]{1,0:T(8,128)S(1)}, u32[]{:S(2)}, u32[]{:S(2)}) collective-permute-start(f32[384,256]{1,0:T(8,128)} %get-tuple-element.64), channel_id=1, source_target_pairs={{0,2},{2,4},{4,6},{6,0},{1,3},{3,5},{5,7},{7,1},{8,10},{10,12},{12... | collective-permute-start | bytes 1179656 | tf_op jit(solution)/shard_map/ppermute | solution.py:608
  164.4 27.6 %collective-permute-start.23 = (f32[384,256]{1,0:T(8,128)}, f32[384,256]{1,0:T(8,128)S(1)}, u32[]{:S(2)}, u32[]{:S(2)}) collective-permute-start(f32[384,256]{1,0:T(8,128)} %get-tuple-element.65), channel_id=1, source_target_pairs={{0,6},{2,0},{4,2},{6,4},{1,7},{3,1},{5,3},{7,5},{8,14},{10,8},{12,... | collective-permute-start | bytes 1179656 | tf_op jit(solution)/shard_map/ppermute | solution.py:608
  168.0 24.0 %collective-permute-start.26 = (bf16[512,384]{1,0:T(8,128)(2,1)}, bf16[512,384]{1,0:T(8,128)(2,1)S(1)}, u32[]{:S(2)}, u32[]{:S(2)}) collective-permute-start(bf16[512,384]{1,0:T(8,128)(2,1)} %get-tuple-element.70), channel_id=1, source_target_pairs={{0,1},{1,0},{2,3},{3,2},{4,5},{5,4},{6,7},{7,6},{8,9},{9,8},{10,11... | collective-permute-start | bytes 1179656 | tf_op jit(solution)/shard_map/ppermute | solution.py:612
  169.7 22.4 %collective-permute-start.27 = (bf16[512,384]{1,0:T(8,128)(2,1)}, bf16[512,384]{1,0:T(8,128)(2,1)S(1)}, u32[]{:S(2)}, u32[]{:S(2)}) collective-permute-start(bf16[512,384]{1,0:T(8,128)(2,1)} %get-tuple-element.71), channel_id=1, source_target_pairs={{0,16},{16,0},{1,17},{17,1},{2,18},{18,2},{3,19},{19,3},{4,20},{20... | collective-permute-start | bytes 1179656 | tf_op jit(solution)/shard_map/ppermute | solution.py:612
  190.6 1.4 copy-start.31
  190.6 1.5 copy-start.32
  197.1 29.3 %all-to-all-start.2 = ((bf16[4,256,384]{2,1,0:T(8,128)(2,1)}), bf16[4,256,384]{2,1,0:T(8,128)(2,1)S(1)}, u32[]{:S(2)}, u32[]{:S(2)}) async-start(bf16[4,256,384]{2,1,0:T(8,128)(2,1)} %bitcast.100), calls=%async_computation.2 | async-start | bytes 1572864 | tf_op jit(solution)/shard_map/all_to_all | solution.py:682
  206.6 5.4 %collective-permute-start.28 = (f32[2,48,128]{2,1,0:T(8,128)S(1)}, f32[2,48,128]{2,1,0:T(8,128)S(1)}, u32[]{:S(2)}, u32[]{:S(2)}) collective-permute-start(f32[2,48,128]{2,1,0:T(8,128)S(1)} %bitcast.108), channel_id=1, source_target_pairs={{0,8},{8,16},{16,24},{1,9},{9,17},{17,25},{2,10},{10,18},{18,26},{... | collective-permute-start | bytes 147464 | tf_op jit(solution)/shard_map/ppermute | solution.py:593
  208.2 20.7 %collective-permute-start.32 = (bf16[1024,384]{1,0:T(8,128)(2,1)}, bf16[1024,384]{1,0:T(8,128)(2,1)S(1)}, u32[]{:S(2)}, u32[]{:S(2)}) collective-permute-start(bf16[1024,384]{1,0:T(8,128)(2,1)} %get-tuple-element.74), channel_id=1, source_target_pairs={{0,8},{8,0},{1,9},{9,1},{2,10},{10,2},{3,11},{11,3},{4,12},{12,4},... | collective-permute-start | bytes 2359304 | tf_op jit(solution)/shard_map/ppermute | solution.py:612
  209.4 3.1 %collective-permute-start.29 = (f32[2,48,128]{2,1,0:T(8,128)S(1)}, f32[2,48,128]{2,1,0:T(8,128)S(1)}, u32[]{:S(2)}, u32[]{:S(2)}) collective-permute-start(f32[2,48,128]{2,1,0:T(8,128)S(1)} %bitcast.107), channel_id=1, source_target_pairs={{8,0},{16,8},{24,16},{9,1},{17,9},{25,17},{10,2},{18,10},{26,18},{... | collective-permute-start | bytes 147464 | tf_op jit(solution)/shard_map/ppermute | solution.py:594
  210.7 13.7 %collective-permute-start.35 = (bf16[512,384]{1,0:T(8,128)(2,1)}, bf16[512,384]{1,0:T(8,128)(2,1)S(1)}, u32[]{:S(2)}, u32[]{:S(2)}) collective-permute-start(bf16[512,384]{1,0:T(8,128)(2,1)} %get-tuple-element.77.refs_3_), channel_id=1, source_target_pairs={{0,8},{8,0},{1,9},{9,1},{2,10},{10,2},{3,11},{11,3},{4,12},{12,4},... | collective-permute-start | bytes 1179656 | tf_op jit(solution)/shard_map/ppermute | solution.py:612
  211.9 14.6 %collective-permute-start.36 = (bf16[512,384]{1,0:T(8,128)(2,1)}, bf16[512,384]{1,0:T(8,128)(2,1)}, u32[]{:S(2)}, u32[]{:S(2)}) collective-permute-start(bf16[512,384]{1,0:T(8,128)(2,1)} %get-tuple-element.78.refs_4_), channel_id=1, source_target_pairs={{0,8},{8,0},{1,9},{9,1},{2,10},{10,2},{3,11},{11,3},{4,12},{12,4},... | collective-permute-start | bytes 1179656 | tf_op jit(solution)/shard_map/ppermute | solution.py:612
  212.0 14.5 %copy-start.34 = (f32[2,48,128]{2,1,0:T(8,128)}, f32[2,48,128]{2,1,0:T(8,128)S(1)}, u32[]{:S(2)}) copy-start(f32[2,48,128]{2,1,0:T(8,128)S(1)} %collective-permute-done.28.refs_9_.refs_2_) | copy-start | bytes 147460
  212.5 13.9 %copy-start.35 = (f32[2,48,128]{2,1,0:T(8,128)}, f32[2,48,128]{2,1,0:T(8,128)S(1)}, u32[]{:S(2)}) copy-start(f32[2,48,128]{2,1,0:T(8,128)S(1)} %collective-permute-done.29.refs_10_.refs_3_) | copy-start | bytes 147460
  212.6 4.9 %collective-permute-start.30 = (f32[36,2,128]{2,1,0:T(2,128)S(1)}, f32[36,2,128]{2,1,0:T(2,128)S(1)}, u32[]{:S(2)}, u32[]{:S(2)}) collective-permute-start(f32[36,2,128]{2,1,0:T(2,128)S(1)} %pad_maximum_fusion), channel_id=1, source_target_pairs={{0,1},{1,2},{2,3},{3,4},{4,5},{5,6},{6,7},{8,9},{9,10},{10,11},{11... | collective-permute-start | bytes 110600 | tf_op jit(solution)/shard_map/ppermute | solution.py:599
  215.9 6.3 %collective-permute-start.31 = (f32[36,2,128]{2,1,0:T(2,128)S(1)}, f32[36,2,128]{2,1,0:T(2,128)S(1)}, u32[]{:S(2)}, u32[]{:S(2)}) collective-permute-start(f32[36,2,128]{2,1,0:T(2,128)S(1)} %pad_maximum_fusion.1), channel_id=1, source_target_pairs={{1,0},{2,1},{3,2},{4,3},{5,4},{6,5},{7,6},{9,8},{10,9},{11,10},{12... | collective-permute-start | bytes 110600 | tf_op jit(solution)/shard_map/ppermute | solution.py:600
  217.5 9.0 %copy-start.36 = (f32[36,2,128]{2,1,0:T(2,128)}, f32[36,2,128]{2,1,0:T(2,128)S(1)}, u32[]{:S(2)}) copy-start(f32[36,2,128]{2,1,0:T(2,128)S(1)} %collective-permute-done.30.refs_11_.refs_4_) | copy-start | bytes 110596
  217.5 12.1 %collective-permute-start.33 = (bf16[1024,384]{1,0:T(8,128)(2,1)}, bf16[1024,384]{1,0:T(8,128)(2,1)}, u32[]{:S(2)}, u32[]{:S(2)}) collective-permute-start(bf16[1024,384]{1,0:T(8,128)(2,1)} %get-tuple-element.75), channel_id=1, source_target_pairs={{0,8},{8,0},{1,9},{9,1},{2,10},{10,2},{3,11},{11,3},{4,12},{12,4},... | collective-permute-start | bytes 2359304 | tf_op jit(solution)/shard_map/ppermute | solution.py:612
  222.2 4.3 %copy-start.37 = (f32[36,2,128]{2,1,0:T(2,128)}, f32[36,2,128]{2,1,0:T(2,128)S(1)}, u32[]{:S(2)}) copy-start(f32[36,2,128]{2,1,0:T(2,128)S(1)} %collective-permute-done.31.refs_12_.refs_5_) | copy-start | bytes 110596
  222.2 7.4 %collective-permute-start.34 = (bf16[1024,384]{1,0:T(8,128)(2,1)}, bf16[1024,384]{1,0:T(8,128)(2,1)}, u32[]{:S(2)}, u32[]{:S(2)}) collective-permute-start(bf16[1024,384]{1,0:T(8,128)(2,1)} %get-tuple-element.76), channel_id=1, source_target_pairs={{0,8},{8,0},{1,9},{9,1},{2,10},{10,2},{3,11},{11,3},{4,12},{12,4},... | collective-permute-start | bytes 2359304 | tf_op jit(solution)/shard_map/ppermute | solution.py:612
  224.4 5.2 %copy-start.28 = (bf16[512,384]{1,0:T(8,128)(2,1)}, bf16[512,384]{1,0:T(8,128)(2,1)S(1)}, u32[]{:S(2)}) copy-start(bf16[512,384]{1,0:T(8,128)(2,1)S(1)} %collective-permute-done.35.refs_5_) | copy-start | bytes 1179652
  226.4 3.2 %copy-start.1 = (bf16[4,256,384]{2,1,0:T(8,128)(2,1)}, bf16[4,256,384]{2,1,0:T(8,128)(2,1)S(1)}, u32[]{:S(2)}) copy-start(bf16[4,256,384]{2,1,0:T(8,128)(2,1)S(1)} %all-to-all-done.2) | copy-start | bytes 2359300
  226.5 22.4 %collective-permute-start.39 = (bf16[1024,384]{1,0:T(8,128)(2,1)S(1)}, bf16[1024,384]{1,0:T(8,128)(2,1)}, u32[]{:S(2)}, u32[]{:S(2)}) collective-permute-start(bf16[1024,384]{1,0:T(8,128)(2,1)S(1)} %bitcast.84), channel_id=1, source_target_pairs={{0,8},{8,0},{1,9},{9,1},{2,10},{10,2},{3,11},{11,3},{4,12},{12,4},... | collective-permute-start | bytes 2359304 | tf_op jit(solution)/shard_map/ppermute | solution.py:612
  226.5 28.8 %collective-permute-start.38 = (bf16[1024,384]{1,0:T(8,128)(2,1)S(1)}, bf16[1024,384]{1,0:T(8,128)(2,1)S(1)}, u32[]{:S(2)}, u32[]{:S(2)}) collective-permute-start(bf16[1024,384]{1,0:T(8,128)(2,1)S(1)} %bitcast.85), channel_id=1, source_target_pairs={{0,1},{1,0},{2,3},{3,2},{4,5},{5,4},{6,7},{7,6},{8,9},{9,8},{10,11... | collective-permute-start | bytes 2359304 | tf_op jit(solution)/shard_map/ppermute | solution.py:612
  228.9 26.4 %collective-permute-start.37 = (bf16[1024,384]{1,0:T(8,128)(2,1)S(1)}, bf16[1024,384]{1,0:T(8,128)(2,1)S(1)}, u32[]{:S(2)}, u32[]{:S(2)}) collective-permute-start(bf16[1024,384]{1,0:T(8,128)(2,1)S(1)} %bitcast.86), channel_id=1, source_target_pairs={{0,16},{16,0},{1,17},{17,1},{2,18},{18,2},{3,19},{19,3},{4,20},{20... | collective-permute-start | bytes 2359304 | tf_op jit(solution)/shard_map/ppermute | solution.py:612
  259.0 3.8 %collective-permute-start.42 = (bf16[1024,384]{1,0:T(8,128)(2,1)}, bf16[1024,384]{1,0:T(8,128)(2,1)S(1)}, u32[]{:S(2)}, u32[]{:S(2)}) collective-permute-start(bf16[1024,384]{1,0:T(8,128)(2,1)} %get-tuple-element.81.refs_0_), channel_id=1, source_target_pairs={{0,8},{8,0},{1,9},{9,1},{2,10},{10,2},{3,11},{11,3},{4,12},{12,4},... | collective-permute-start | bytes 2359304 | tf_op jit(solution)/shard_map/ppermute | solution.py:612
  259.4 3.4 %collective-permute-start.43 = (bf16[1024,384]{1,0:T(8,128)(2,1)}, bf16[1024,384]{1,0:T(8,128)(2,1)S(1)}, u32[]{:S(2)}, u32[]{:S(2)}) collective-permute-start(bf16[1024,384]{1,0:T(8,128)(2,1)} %get-tuple-element.82.refs_2_), channel_id=1, source_target_pairs={{0,8},{8,0},{1,9},{9,1},{2,10},{10,2},{3,11},{11,3},{4,12},{12,4},... | collective-permute-start | bytes 2359304 | tf_op jit(solution)/shard_map/ppermute | solution.py:612
  259.6 15.4 %collective-permute-start.40 = (bf16[512,384]{1,0:T(8,128)(2,1)}, bf16[512,384]{1,0:T(8,128)(2,1)S(1)}, u32[]{:S(2)}, u32[]{:S(2)}) collective-permute-start(bf16[512,384]{1,0:T(8,128)(2,1)} %get-tuple-element.79), channel_id=1, source_target_pairs={{0,1},{1,0},{2,3},{3,2},{4,5},{5,4},{6,7},{7,6},{8,9},{9,8},{10,11... | collective-permute-start | bytes 1179656 | tf_op jit(solution)/shard_map/ppermute | solution.py:612
  260.8 14.2 %collective-permute-start.41 = (bf16[512,384]{1,0:T(8,128)(2,1)}, bf16[512,384]{1,0:T(8,128)(2,1)S(1)}, u32[]{:S(2)}, u32[]{:S(2)}) collective-permute-start(bf16[512,384]{1,0:T(8,128)(2,1)} %get-tuple-element.80), channel_id=1, source_target_pairs={{0,16},{16,0},{1,17},{17,1},{2,18},{18,2},{3,19},{19,3},{4,20},{20... | collective-permute-start | bytes 1179656 | tf_op jit(solution)/shard_map/ppermute | solution.py:612
  276.5 1.9 collective-permute-start.44
  276.5 2.5 collective-permute-start.45
  (28 other events, 24.4 us)

commit v4 on v3

--- a/solution.py
+++ b/solution.py
@@ -14,7 +14,7 @@
 QUARTER = CELLS // 4
 FOLD = CXL // 3
 MIB = 1 << 20
-VMEM_LIMIT = 56 * MIB
+VMEM_LIMIT = 62 * MIB
 IN_SMEM = pl.BlockSpec(memory_space=pltpu.SMEM)
 IN_VMEM = pl.BlockSpec(memory_space=pltpu.VMEM)
 IN_ANY = pl.BlockSpec(memory_space=pl.ANY)
@@ -54,6 +54,7 @@
         out_specs=[IN_ANY] * count,
         input_output_aliases={i: i for i in range(count)},
         cost_estimate=LIGHT,
+        compiler_params=pltpu.CompilerParams(vmem_limit_bytes=VMEM_LIMIT),
         name="tie",
     )(*values, *tokens)
 
@@ -91,6 +92,7 @@
             pltpu.VMEM((2,) + part.shape, part.dtype),
             pltpu.SemaphoreType.DMA((4,)),
         ],
+        compiler_params=pltpu.CompilerParams(vmem_limit_bytes=VMEM_LIMIT),
         name="gate",
     )(from_x, from_y, *tokens)
 
@@ -100,8 +102,10 @@
     each, rows, samples = source.shape
     row = lax.broadcasted_iota(jnp.int32, (samples, samples), 0)
     col = lax.broadcasted_iota(jnp.int32, (samples, samples), 1)
+    rest = jnp.zeros((1, samples - taps.shape[1]), jnp.float32)
     for i in range(each):
-        line = jnp.broadcast_to(taps[i], (samples, samples))
+        line = taps[pl.ds(pl.program_id(0) * each + i, 1), :]
+        line = jnp.broadcast_to(jnp.concatenate([line, rest], axis=1), (samples, samples))
         band = pltpu.roll(line, 0, 1, stride=1, stride_axis=0)
         matrix = jnp.where(col >= row, band, 0.0)
         if matrices:
@@ -115,7 +119,8 @@
 
 
 def filter_call(half, traces, taps, tokens=()):
-    surveys, unused, samples = taps.shape
+    surveys = taps.shape[0]
+    samples = traces.shape[1]
     rows = traces.shape[0] // surveys
     each = 3
     out_specs = [pl.BlockSpec((each, rows // 2, samples), lambda i: (i, 0, 0))]
@@ -127,12 +132,13 @@
         functools.partial(filter_kernel, half, len(tokens)),
         grid=(surveys // each,),
         in_specs=[
-            pl.BlockSpec((each, 1, samples), lambda i: (i, 0, 0)),
+            pl.BlockSpec(taps.shape, lambda i: (0, 0)),
             pl.BlockSpec((each, rows, samples), lambda i: (i, 0, 0)),
         ]
         + [IN_ANY] * len(tokens),
         out_specs=out_specs,
         out_shape=out_shape,
+        compiler_params=pltpu.CompilerParams(vmem_limit_bytes=VMEM_LIMIT),
         name=f"filter_{half}",
     )(taps, traces.reshape(surveys, rows, samples), *tokens)
 
@@ -327,6 +333,7 @@
         out_specs=[IN_VMEM] * len(out_shape),
         scratch_shapes=[pltpu.VMEM((QUARTER, 256), jnp.float32)],
         cost_estimate=LIGHT,
+        compiler_params=pltpu.CompilerParams(vmem_limit_bytes=VMEM_LIMIT),
         name=f"image_{half}",
     )(*parts, *extra, *tokens)
 
@@ -348,8 +355,10 @@
         copies.append(pltpu.make_async_copy(before, total, sems.at[len(sizes) + 1]))
     if last:
         whole_out, earlier_in, band = refs[6:]
-        copies.append(pltpu.make_async_copy(earlier, earlier_in, sems.at[len(sizes) + 2]))
-        copies.append(pltpu.make_async_copy(matrices, band, sems.at[len(sizes) + 3]))
+        later = [
+            pltpu.make_async_copy(earlier, earlier_in, sems.at[len(sizes) + 2]),
+            pltpu.make_async_copy(matrices, band, sems.at[len(sizes) + 3]),
+        ]
     start = 0
     for i, rows in enumerate(sizes):
         copies.append(
@@ -368,6 +377,9 @@
             n = n + (counts[order[base + j]] > g * group).astype(jnp.int32)
         return n
 
+    if last:
+        for copy in later:
+            copy.start()
     n = lax.fori_loop(0, tiles, add_tile, 0)
     for copy in copies:
         copy.wait()
@@ -409,6 +421,8 @@
         send.start()
         send.wait()
         return
+    for copy in later:
+        copy.wait()
     surveys = matrices.shape[0]
     rows = whole_out.shape[0] // surveys
     sends = []
@@ -644,10 +658,9 @@
     )
     own_slots = (pair_count[0], numbers.reshape(256), own_cells.reshape(256, row_block))
 
-    taps = jnp.pad(filter_taps, ((0, 0), (0, samples - tap_count))).reshape(surveys, 1, samples)
     rows_half = traces.shape[0] // 2
-    (first_half,) = filter_call(0, traces, taps)
-    second_half, matrices = filter_call(1, traces, taps)
+    (first_half,) = filter_call(0, traces, filter_taps)
+    second_half, matrices = filter_call(1, traces, filter_taps)
     halves = [part.reshape(rows_half, samples) for part in (first_half, second_half)]
 
     spots = ((x, y), (1 - x, y), (x, 1 - y), (1 - x, 1 - y))
@@ -691,11 +704,12 @@
     halves[1] = own_1
     partial_0 = far_stack(0, tie(parts, near_0), near_0)
     packed_0, stacked, fold = image_call(0, sum_z(partial_0), [], [])
-    columns_0 = over_z(packed_0)
     from_x, from_y, parts = spread(own_1, packed_0)
+    columns_0 = over_z(tie([packed_0], from_x)[0])
     near_1 = near_stack(1, pairs(own_1, from_x, from_y))
     partial_1 = far_stack(1, tie(parts, near_1), near_1)
-    from_x, from_y, parts = spread(columns_0, partial_1[0])
+    (columns_0,) = tie([columns_0], partial_1[0])
+    from_x, from_y, parts = spread(columns_0)
     own_layers = [columns_0, from_x, from_y]
     residual_0 = read(0, 12, own_layers, None)
     packed_1, image = image_call(1, sum_z(partial_1), [fold, stacked], [residual_0, *parts])
@@ -708,9 +722,8 @@
     layers = layers[:3] + list(own_layers[3:]) + layers[3:]
     residual_0 = read(0, 24, layers, residual_0, tokens=[columns_1, *halo])
     structure_tensor = tensor_call(place, image, halo, [residual_0])
-    residual_1 = read(1, 44, pairs(columns_1), None, tokens=[structure_tensor])
-    from_x, from_y, parts = spread(columns_1, residual_1)
-    residual_1 = read(1, 52, pairs(from_x, from_y), residual_1)
+    from_x, from_y, parts = spread(columns_1, structure_tensor)
+    residual_1 = read(1, 44, pairs(columns_1, from_x, from_y), None)
     parts = tie(parts, residual_1)
     layers = [*parts, *(over("c", part) for part in parts)]
     adjoint_traces = read(1, 36, layers, residual_1, matrices, residual_0)

time: 291 us -> 270 us (0.928)
  waiting for transfers between devices: 76.8 us -> 60.4 us
  local copies, waits for them, and re-layouts: 22.3 us -> 18.3 us
  starting transfers between devices: 72.1 us -> 76.1 us
  Pallas kernels: 114 us -> 111 us
    ppermute x6, waiting for transfers between devices: 39.9 us -> 24.4 us  [along_z(): return lax.ppermute(value, 'z', [(i, (i + step) % 4) for i in range(4)])]
    ppermute x36, waiting for transfers between devices: 6.09 us -> 21.6 us  [over(): return lax.ppermute(value, axis, SWAP)]
    all_to_all x2, waiting for transfers between devices: 16.4 us -> 1.5 us  [over_z(): return lax.all_to_all(value, 'z', 0, 0, tiled=True)]
    pallas_call x5 -> x4, Pallas kernels: 45.1 us -> 39.8 us  [read_call(): pl.pallas_call(functools.partial(read_kernel, (sizes, first, last, len(to...]
    ppermute x36, starting transfers between devices: 29.4 us -> 32.7 us  [over(): return lax.ppermute(value, axis, SWAP)]
    unnamed x89 -> x69, local copies, waits for them, and re-layouts: 16.8 us -> 14 us
  transfers between devices with their start and end apart: 49 -> 49, of which waited for: 17 -> 18; matrix products, arithmetic and copies ran while one was open for 2% -> 3% of each run, Pallas kernels for 33% -> 35%
where the time goes in v4:
time: 270 us; the launch traced here: 269 us
  Pallas kernels  111 us (41%)
  starting transfers between devices  76.1 us (28%)
  waiting for transfers between devices  60.4 us (22%)
  local copies, waits for them, and re-layouts  18.3 us (7%)
    pallas_call x4, Pallas kernels, read_call(): pl.pallas_call(functools.partial(read_kernel, (sizes, first, last, len(to...  39.8 us
    pallas_call x4, Pallas kernels, stack_call(): pl.pallas_call(functools.partial(stack_kernel, spec), out_shape=single if...  39.6 us
    ppermute x36, starting transfers between devices, over(): return lax.ppermute(value, axis, SWAP)  32.7 us
    ppermute x6, waiting for transfers between devices, along_z(): return lax.ppermute(value, 'z', [(i, (i + step) % 4) for i in range(4)])  24.4 us
    ppermute x36, waiting for transfers between devices, over(): return lax.ppermute(value, axis, SWAP)  21.6 us
    all_to_all x2, starting transfers between devices, over_z(): return lax.all_to_all(value, 'z', 0, 0, tiled=True)  18.7 us
    unnamed x69, local copies, waits for them, and re-layouts  14 us
    ppermute x6, starting transfers between devices, along_z(): return lax.ppermute(value, 'z', [(i, (i + step) % 4) for i in range(4)])  13.5 us
  transfers between devices with their start and end apart: 49, of which 18 were waited for; matrix products, arithmetic and copies ran while one was open for 3% of the time, Pallas kernels for 35%

profile of v4, /device:TPU:0, one launch (start us, length us, event | category | flops | bytes accessed | tf_op | source)
XLA Modules:
  0.0 269.2 jit_solution(15145781036380350141)
XLA Ops:
  0.7 4.5 %filter_0.1 = bf16[12,320,128]{2,1,0:T(8,128)(2,1)} custom-call(f32[12,64]{1,0:T(8,128)} %taps.3, bf16[12,640,128]{2,1,0:T(8,128)(2,1)} %bitcast.83), custom_call_target="tpu_custom_call" | custom-call | tf_op jit(solution)/shard_map/filter_0/pallas_call | solution.py:131
  5.1 3.0 %collective-permute-start.2 = (bf16[3840,128]{1,0:T(8,128)(2,1)}, bf16[3840,128]{1,0:T(8,128)(2,1)S(1)}, u32[]{:S(2)}, u32[]{:S(2)}) collective-permute-start(bf16[3840,128]{1,0:T(8,128)(2,1)} %bitcast.77), channel_id=1, source_target_pairs={{0,1},{1,0},{2,3},{3,2},{4,5},{5,4},{6,7},{7,6},{8,9},{9,8},{10,11... | collective-permute-start | bytes 2949128 | tf_op jit(solution)/shard_map/ppermute | solution.py:626
  8.1 1.5 collective-permute-start.1
  12.0 3.4 %all-to-all-start = ((s32[8,40,128]{2,1,0:T(8,128)}), s32[8,40,128]{2,1,0:T(8,128)S(1)}, u32[]{:S(2)}, u32[]{:S(2)}) async-start(s32[8,40,128]{2,1,0:T(8,128)} %pad_add_fusion), calls=%async_computation | async-start | bytes 327680 | tf_op jit(solution)/shard_map/all_to_all | solution.py:646
  16.5 4.4 %filter_1.1 = (bf16[12,320,128]{2,1,0:T(8,128)(2,1)}, bf16[12,128,128]{2,1,0:T(8,128)(2,1)}) custom-call(f32[12,64]{1,0:T(8,128)} %taps.3, bf16[12,640,128]{2,1,0:T(8,128)(2,1)} %bitcast.84), custom_call_target="tpu_custom_call" | custom-call | tf_op jit(solution)/shard_map/filter_1/pallas_call | solution.py:131
  22.4 10.9 %all-to-all-done.refs_1_.cells = s32[8,40,128]{2,1,0:T(8,128)S(1)} async-done(((s32[8,40,128]{2,1,0:T(8,128)}), s32[8,40,128]{2,1,0:T(8,128)S(1)}, u32[]{:S(2)}, u32[]{:S(2)}) %all-to-all-start) | async-done | bytes 163872 | tf_op jit(solution)/shard_map/all_to_all | solution.py:646
  34.3 2.0 gate.4
  36.9 1.2 collective-permute-start.7
  38.2 1.5 collective-permute-start.8
  39.8 0.9 collective-permute-done.4.refs_5_
  40.8 12.6 %stack.220.refs_1_.refs_2_.refs_4_ = f32[4,400,256]{2,1,0:T(8,128)} custom-call(s32[68]{0:T(128)} %stack.219.refs_2_.order, s32[8,40,128]{2,1,0:T(8,128)} %copy-done.9, bf16[3840,128]{1,0:T(8,128)(2,1)} %bitcast.80, bf16[3840,128]{1,0:T(8,128)(2,1)} %collective-permute-done.refs_1_, bf16[3840,128]{1,0:T(8,128)(2,1)} %get-tuple-element.45.refs_2_, ...), custom_call_target="tpu_custom_call" | custom-call | flops 34359738368 | bytes 1048576 | tf_op jit(solution)/shard_map/stack/pallas_call | solution.py:259
  53.6 1.4 collective-permute-start.5
  55.9 0.8 copy-done.11
  57.2 1.7 collective-permute-done.9.refs_2_
  59.6 8.0 %stack.221 = (f32[400,256]{1,0:T(8,128)}, f32[400,256]{1,0:T(8,128)}, f32[400,256]{1,0:T(8,128)}, f32[400,256]{1,0:T(8,128)}) custom-call(s32[68]{0:T(128)} %stack.219.refs_2_.order, s32[8,40,128]{2,1,0:T(8,128)} %copy-done.9, bf16[1920,128]{1,0:T(8,128)(2,1)} %get-tuple-element.49.refs_0_, bf16[1920,128]{1,0:T(8,128)(2,1)} %get-tuple-element.50.refs_1_, ...), custom_call_target="tpu_custom_call" | custom-call | flops 1 | bytes 1 | tf_op jit(solution)/shard_map/stack/pallas_call | solution.py:259
  67.6 3.5 %collective-permute-start.11 = (f32[400,256]{1,0:T(8,128)}, f32[400,256]{1,0:T(8,128)S(1)}, u32[]{:S(2)}, u32[]{:S(2)}) collective-permute-start(f32[400,256]{1,0:T(8,128)} %get-tuple-element.52), channel_id=1, source_target_pairs={{0,4},{2,6},{4,0},{6,2},{1,5},{3,7},{5,1},{7,3},{8,12},{10,14},{12... | collective-permute-start | bytes 1228808 | tf_op jit(solution)/shard_map/ppermute | solution.py:622
  71.9 3.1 %collective-permute-start.13 = (f32[400,256]{1,0:T(8,128)}, f32[400,256]{1,0:T(8,128)S(1)}, u32[]{:S(2)}, u32[]{:S(2)}) collective-permute-start(f32[400,256]{1,0:T(8,128)} %get-tuple-element.54), channel_id=1, source_target_pairs={{0,6},{2,0},{4,2},{6,4},{1,7},{3,1},{5,3},{7,5},{8,14},{10,8},{12,... | collective-permute-start | bytes 1228808 | tf_op jit(solution)/shard_map/ppermute | solution.py:622
  75.0 24.4 %collective-permute-done.11.refs_1_ = f32[400,256]{1,0:T(8,128)S(1)} collective-permute-done((f32[400,256]{1,0:T(8,128)}, f32[400,256]{1,0:T(8,128)S(1)}, u32[]{:S(2)}, u32[]{:S(2)}) %collective-permute-start.11) | collective-permute-done | bytes 409632 | tf_op jit(solution)/shard_map/ppermute | solution.py:622
  101.6 2.8 %image_0.1 = (bf16[1024,384]{1,0:T(8,128)(2,1)}, f32[384,256]{1,0:T(8,128)}, f32[16,256]{1,0:T(8,128)}) custom-call(f32[400,256]{1,0:T(8,128)} %get-tuple-element.51.refs_0_, f32[400,256]{1,0:T(8,128)} %copy-done.18, f32[400,256]{1,0:T(8,128)} %copy-done.19, f32[400,256]{1,0:T(8,128)} %copy-done.20), custom_call_target="tpu_custom_call" | custom-call | flops 1 | bytes 1 | tf_op jit(solution)/shard_map/image_0/pallas_call | solution.py:329
  104.4 1.0 copy-done.5
  105.4 2.1 gate.5
  108.1 10.3 %all-to-all-start.1 = ((bf16[4,256,384]{2,1,0:T(8,128)(2,1)}), bf16[4,256,384]{2,1,0:T(8,128)(2,1)S(1)}, u32[]{:S(2)}, u32[]{:S(2)}) async-start(bf16[4,256,384]{2,1,0:T(8,128)(2,1)} %bitcast.90), calls=%async_computation.1 | async-start | bytes 1572864 | tf_op jit(solution)/shard_map/all_to_all | solution.py:695
  118.4 1.2 collective-permute-start.14
  119.6 1.9 collective-permute-start.15
  121.5 11.5 %stack.222.refs_2_.refs_4_ = f32[4,384,256]{2,1,0:T(8,128)} custom-call(s32[68]{0:T(128)} %stack.219.refs_2_.order, s32[8,40,128]{2,1,0:T(8,128)} %copy-done.9, bf16[3840,128]{1,0:T(8,128)(2,1)} %tie.7.refs_0_.own, bf16[3840,128]{1,0:T(8,128)(2,1)} %collective-permute-done.16.refs_1_, bf16[3840,128]{1,0:T(8,128)(2,1)} %get-tuple-element.58.refs_2_.refs_1_, ...), custom_call_target="tpu_custom_call" | custom-call | flops 34359738368 | bytes 1048576 | tf_op jit(solution)/shard_map/stack/pallas_call | solution.py:259
  133.6 1.6 collective-permute-done.19.refs_2_
  136.7 7.5 %stack.223 = (f32[384,256]{1,0:T(8,128)}, f32[384,256]{1,0:T(8,128)}, f32[384,256]{1,0:T(8,128)}, f32[384,256]{1,0:T(8,128)}) custom-call(s32[68]{0:T(128)} %stack.219.refs_2_.order, s32[8,40,128]{2,1,0:T(8,128)} %copy-done.9, bf16[1920,128]{1,0:T(8,128)(2,1)} %get-tuple-element.60.refs_0_, bf16[1920,128]{1,0:T(8,128)(2,1)} %get-tuple-element.61.refs_1_, ...), custom_call_target="tpu_custom_call" | custom-call | flops 1 | bytes 1 | tf_op jit(solution)/shard_map/stack/pallas_call | solution.py:259
  144.2 0.9 copy-done.1
  145.2 1.3 collective-permute-start.24
  146.5 2.4 collective-permute-start.21
  148.9 1.9 collective-permute-start.22
  150.9 1.9 collective-permute-start.23
  152.7 12.0 %collective-permute-done.25.from_y = bf16[1024,384]{1,0:T(8,128)(2,1)S(1)} collective-permute-done((bf16[1024,384]{1,0:T(8,128)(2,1)}, bf16[1024,384]{1,0:T(8,128)(2,1)S(1)}, u32[]{:S(2)}, u32[]{:S(2)}) %collective-permute-start.25) | collective-permute-done | bytes 786464 | tf_op jit(solution)/shard_map/ppermute | solution.py:626
  164.8 0.9 copy-done.3
  165.7 0.9 copy-done.4
  166.6 2.0 gate.6
  168.5 0.9 collective-permute-start.26
  169.5 1.3 collective-permute-start.27
  170.8 7.9 %read.4.refs_6_.refs_7_ = f32[3840,128]{1,0:T(8,128)} custom-call(s32[68]{0:T(128)} %stack.219.refs_2_.order, s32[32]{0:T(128)} %bitcast.106, s32[256]{0:T(256)} %reshape.69.refs_4_.blocks, s32[256,128]{1,0:T(8,128)} %bitcast.92, bf16[3840,128]{1,0:T(8,128)(2,1)} %bitcast.81, bf16[1024,384]{1,0:T(8,128)(2,1)} %tie.11.refs_0_, ...), custom_call_target="tpu_custom_call" | custom-call | flops 1 | bytes 1 | tf_op jit(solution)/shard_map/read/pallas_call | solution.py:463
  180.1 4.2 %image_1.1 = (bf16[1024,384]{1,0:T(8,128)(2,1)}, f32[1536,128]{1,0:T(8,128)}) custom-call(f32[384,256]{1,0:T(8,128)} %get-tuple-element.62.refs_1_.refs_0_, f32[384,256]{1,0:T(8,128)} %copy-done.24, f32[384,256]{1,0:T(8,128)} %collective-permute-done.22.refs_2_, f32[384,256]{1,0:T(8,128)} %collective-permute-done.23.refs_3_, ...), custom_call_target="tpu_custom_call" | custom-call | flops 1 | bytes 1 | tf_op jit(solution)/shard_map/image_1/pallas_call | solution.py:329
  184.3 8.4 %all-to-all-start.2 = ((bf16[4,256,384]{2,1,0:T(8,128)(2,1)}), bf16[4,256,384]{2,1,0:T(8,128)(2,1)S(1)}, u32[]{:S(2)}, u32[]{:S(2)}) async-start(bf16[4,256,384]{2,1,0:T(8,128)(2,1)} %bitcast.96), calls=%async_computation.2 | async-start | bytes 1572864 | tf_op jit(solution)/shard_map/all_to_all | solution.py:695
  192.7 0.8 fusion.1
  193.5 1.6 collective-permute-start.28
  195.2 1.0 fusion
  196.2 1.3 collective-permute-start.29
  197.5 2.0 collective-permute-start.35
  200.1 3.6 %collective-permute-start.30 = (f32[36,2,128]{2,1,0:T(2,128)S(1)}, f32[36,2,128]{2,1,0:T(2,128)S(1)}, u32[]{:S(2)}, u32[]{:S(2)}) collective-permute-start(f32[36,2,128]{2,1,0:T(2,128)S(1)} %pad_maximum_fusion), channel_id=1, source_target_pairs={{0,1},{1,2},{2,3},{3,4},{4,5},{5,6},{6,7},{8,9},{9,10},{10,11},{11... | collective-permute-start | bytes 110600 | tf_op jit(solution)/shard_map/ppermute | solution.py:613
  203.8 1.3 collective-permute-start.31
  205.1 2.9 %collective-permute-start.32 = (bf16[1024,384]{1,0:T(8,128)(2,1)}, bf16[1024,384]{1,0:T(8,128)(2,1)}, u32[]{:S(2)}, u32[]{:S(2)}) collective-permute-start(bf16[1024,384]{1,0:T(8,128)(2,1)} %get-tuple-element.74), channel_id=1, source_target_pairs={{0,8},{8,0},{1,9},{9,1},{2,10},{10,2},{3,11},{11,3},{4,12},{12,4},... | collective-permute-start | bytes 2359304 | tf_op jit(solution)/shard_map/ppermute | solution.py:626
  208.0 1.6 collective-permute-done.31.refs_12_.refs_5_
  209.6 2.0 collective-permute-start.34
  211.6 1.5 all-to-all-done.2
  213.1 2.6 collective-permute-start.38
  215.7 1.0 collective-permute-start.37
  217.4 11.4 %read.5.refs_6_.refs_5_ = f32[3840,128]{1,0:T(8,128)} custom-call(s32[68]{0:T(128)} %stack.219.refs_2_.order, s32[32]{0:T(128)} %bitcast.107, s32[256]{0:T(256)} %reshape.69.refs_4_.blocks, s32[256,128]{1,0:T(8,128)} %bitcast.93, bf16[3840,128]{1,0:T(8,128)(2,1)} %bitcast.82, bf16[1024,384]{1,0:T(8,128)(2,1)} %collective-permute-done.32.refs_0_, ...), custom_call_target="tpu_custom_call" | custom-call | flops 1 | bytes 1 | tf_op jit(solution)/shard_map/read/pallas_call | solution.py:463
  228.9 7.7 %tensor.1.refs_0_ = f32[6,32,48,128]{3,2,1,0:T(8,128)} custom-call(s32[4]{0:T(128)} %pad_add_fusion.2.refs_0_, f32[32,48,128]{2,1,0:T(8,128)} %bitcast.99, f32[2,48,128]{2,1,0:T(8,128)} %copy-done.25, f32[2,48,128]{2,1,0:T(8,128)} %copy-done.26, f32[36,2,128]{2,1,0:T(2,128)} %copy-done.27, f32[36,2,128]{2,1,0:T(2,128)} %copy-done.28, ...), custom_call_target="tpu_custom_call" | custom-call | flops 1 | bytes 1 | tf_op jit(solution)/shard_map/tensor/pallas_call | solution.py:587
  236.7 0.9 copy-done.8
  237.5 1.9 gate.7
  240.5 1.9 collective-permute-start.40
  242.5 0.9 collective-permute-done.43.refs_5_
  243.4 12.0 %read.6.refs_2_.refs_6_ = f32[3840,128]{1,0:T(8,128)} custom-call(s32[68]{0:T(128)} %stack.219.refs_2_.order, s32[32]{0:T(128)} %bitcast.108, s32[256]{0:T(256)} %reshape.69.refs_4_.blocks, s32[256,128]{1,0:T(8,128)} %bitcast.94, bf16[3840,128]{1,0:T(8,128)(2,1)} %tie.7.refs_0_.own, bf16[1024,384]{1,0:T(8,128)(2,1)} %bitcast.89, ...), custom_call_target="tpu_custom_call" | custom-call | flops 1 | bytes 1 | tf_op jit(solution)/shard_map/read/pallas_call | solution.py:463
  256.9 0.8 collective-permute-start.44
  257.8 1.6 collective-permute-done.44.refs_2_
  260.7 8.5 %read.7 = f32[7680,128]{1,0:T(8,128)} custom-call(s32[68]{0:T(128)} %stack.219.refs_2_.order, s32[32]{0:T(128)} %bitcast.109, s32[256]{0:T(256)} %reshape.69.refs_4_.blocks, s32[256,128]{1,0:T(8,128)} %bitcast.95, bf16[3840,128]{1,0:T(8,128)(2,1)} %tie.7.refs_0_.own, bf16[512,384]{1,0:T(8,128)(2,1)} %get-tuple-element.83.refs_0_, ...), custom_call_target="tpu_custom_call" | custom-call | flops 1 | bytes 1 | tf_op jit(solution)/shard_map/read/pallas_call | solution.py:463
  (148 shorter events, 21.7 us)
Async XLA Ops:
  0.6 9.5 %copy-start.30 = (s32[1,32]{1,0:T(1,128)S(1)}, s32[1,32]{1,0:T(1,128)}, u32[]{:S(2)}) copy-start(s32[1,32]{1,0:T(1,128)} %param.9) | copy-start | bytes 388
  0.6 10.2 %copy-start.31 = (s32[1,32,7]{1,0,2:T(1,128)S(1)}, s32[1,32,7]{1,0,2:T(1,128)}, u32[]{:S(2)}) copy-start(s32[1,32,7]{1,0,2:T(1,128)} %param.7) | copy-start | bytes 2692
  0.7 10.4 %copy-start.29 = (s32[1,32,7,128]{3,1,2,0:T(8,128)S(1)}, s32[1,32,7,128]{3,1,2,0:T(8,128)}, u32[]{:S(2)}) copy-start(s32[1,32,7,128]{3,1,2,0:T(8,128)} %param.8) | copy-start | bytes 344068
  5.1 28.2 %collective-permute-start.2 = (bf16[3840,128]{1,0:T(8,128)(2,1)}, bf16[3840,128]{1,0:T(8,128)(2,1)S(1)}, u32[]{:S(2)}, u32[]{:S(2)}) collective-permute-start(bf16[3840,128]{1,0:T(8,128)(2,1)} %bitcast.77), channel_id=1, source_target_pairs={{0,1},{1,0},{2,3},{3,2},{4,5},{5,4},{6,7},{7,6},{8,9},{9,8},{10,11... | collective-permute-start | bytes 2949128 | tf_op jit(solution)/shard_map/ppermute | solution.py:626
  8.1 25.2 %collective-permute-start.1 = (bf16[3840,128]{1,0:T(8,128)(2,1)}, bf16[3840,128]{1,0:T(8,128)(2,1)}, u32[]{:S(2)}, u32[]{:S(2)}) collective-permute-start(bf16[3840,128]{1,0:T(8,128)(2,1)} %bitcast.78), channel_id=1, source_target_pairs={{0,16},{16,0},{1,17},{17,1},{2,18},{18,2},{3,19},{19,3},{4,20},{20... | collective-permute-start | bytes 2949128 | tf_op jit(solution)/shard_map/ppermute | solution.py:626
  12.0 21.3 %all-to-all-start = ((s32[8,40,128]{2,1,0:T(8,128)}), s32[8,40,128]{2,1,0:T(8,128)S(1)}, u32[]{:S(2)}, u32[]{:S(2)}) async-start(s32[8,40,128]{2,1,0:T(8,128)} %pad_add_fusion), calls=%async_computation | async-start | bytes 327680 | tf_op jit(solution)/shard_map/all_to_all | solution.py:646
  15.4 24.3 %collective-permute-start = (bf16[3840,128]{1,0:T(8,128)(2,1)}, bf16[3840,128]{1,0:T(8,128)(2,1)}, u32[]{:S(2)}, u32[]{:S(2)}) collective-permute-start(bf16[3840,128]{1,0:T(8,128)(2,1)} %bitcast.79), channel_id=1, source_target_pairs={{0,8},{8,0},{1,9},{9,1},{2,10},{10,2},{3,11},{11,3},{4,12},{12,4},... | collective-permute-start | bytes 2949128 | tf_op jit(solution)/shard_map/ppermute | solution.py:626
  33.3 1.0 copy-start.14
  36.4 3.5 %collective-permute-start.3 = (bf16[3840,128]{1,0:T(8,128)(2,1)}, bf16[3840,128]{1,0:T(8,128)(2,1)S(1)}, u32[]{:S(2)}, u32[]{:S(2)}) collective-permute-start(bf16[3840,128]{1,0:T(8,128)(2,1)} %get-tuple-element.45.refs_2_), channel_id=1, source_target_pairs={{0,8},{8,0},{1,9},{9,1},{2,10},{10,2},{3,11},{11,3},{4,12},{12,4},... | collective-permute-start | bytes 2949128 | tf_op jit(solution)/shard_map/ppermute | solution.py:626
  36.4 4.3 %collective-permute-start.4 = (bf16[3840,128]{1,0:T(8,128)(2,1)}, bf16[3840,128]{1,0:T(8,128)(2,1)}, u32[]{:S(2)}, u32[]{:S(2)}) collective-permute-start(bf16[3840,128]{1,0:T(8,128)(2,1)} %get-tuple-element.46.refs_4_), channel_id=1, source_target_pairs={{0,8},{8,0},{1,9},{9,1},{2,10},{10,2},{3,11},{11,3},{4,12},{12,4},... | collective-permute-start | bytes 2949128 | tf_op jit(solution)/shard_map/ppermute | solution.py:626
  36.9 18.1 %collective-permute-start.7 = (bf16[1920,128]{1,0:T(8,128)(2,1)}, bf16[1920,128]{1,0:T(8,128)(2,1)S(1)}, u32[]{:S(2)}, u32[]{:S(2)}) collective-permute-start(bf16[1920,128]{1,0:T(8,128)(2,1)} %get-tuple-element.47), channel_id=1, source_target_pairs={{0,1},{1,0},{2,3},{3,2},{4,5},{5,4},{6,7},{7,6},{8,9},{9,8},{10,11... | collective-permute-start | bytes 1474568 | tf_op jit(solution)/shard_map/ppermute | solution.py:626
  38.2 16.9 %collective-permute-start.8 = (bf16[1920,128]{1,0:T(8,128)(2,1)}, bf16[1920,128]{1,0:T(8,128)(2,1)S(1)}, u32[]{:S(2)}, u32[]{:S(2)}) collective-permute-start(bf16[1920,128]{1,0:T(8,128)(2,1)} %get-tuple-element.48), channel_id=1, source_target_pairs={{0,16},{16,0},{1,17},{17,1},{2,18},{18,2},{3,19},{19,3},{4,20},{20... | collective-permute-start | bytes 1474568 | tf_op jit(solution)/shard_map/ppermute | solution.py:626
  39.8 1.0 copy-start.32
  53.4 51.0 %collective-permute-start.6 = (bf16[3840,128]{1,0:T(8,128)(2,1)}, bf16[3840,128]{1,0:T(8,128)(2,1)}, u32[]{:S(2)}, u32[]{:S(2)}) collective-permute-start(bf16[3840,128]{1,0:T(8,128)(2,1)} %tie.7.refs_0_.own), channel_id=1, source_target_pairs={{0,1},{1,0},{2,3},{3,2},{4,5},{5,4},{6,7},{7,6},{8,9},{9,8},{10,11... | collective-permute-start | bytes 2949128 | tf_op jit(solution)/shard_map/ppermute | solution.py:626
  53.6 50.8 %collective-permute-start.5 = (bf16[3840,128]{1,0:T(8,128)(2,1)}, bf16[3840,128]{1,0:T(8,128)(2,1)S(1)}, u32[]{:S(2)}, u32[]{:S(2)}) collective-permute-start(bf16[3840,128]{1,0:T(8,128)(2,1)} %tie.7.refs_0_.own), channel_id=1, source_target_pairs={{0,16},{16,0},{1,17},{17,1},{2,18},{18,2},{3,19},{19,3},{4,20},{20... | collective-permute-start | bytes 2949128 | tf_op jit(solution)/shard_map/ppermute | solution.py:626
  56.7 42.6 %copy-start = (bf16[3840,128]{1,0:T(8,128)(2,1)S(1)}, bf16[3840,128]{1,0:T(8,128)(2,1)}, u32[]{:S(2)}) copy-start(bf16[3840,128]{1,0:T(8,128)(2,1)} %tie.7.refs_0_.own) | copy-start | bytes 2949124
  56.7 2.2 collective-permute-start.9
  56.7 2.9 %collective-permute-start.10 = (bf16[1920,128]{1,0:T(8,128)(2,1)}, bf16[1920,128]{1,0:T(8,128)(2,1)}, u32[]{:S(2)}, u32[]{:S(2)}) collective-permute-start(bf16[1920,128]{1,0:T(8,128)(2,1)} %get-tuple-element.50.refs_1_), channel_id=1, source_target_pairs={{0,8},{8,0},{1,9},{9,1},{2,10},{10,2},{3,11},{11,3},{4,12},{12,4},... | collective-permute-start | bytes 1474568 | tf_op jit(solution)/shard_map/ppermute | solution.py:626
  67.6 31.7 %collective-permute-start.11 = (f32[400,256]{1,0:T(8,128)}, f32[400,256]{1,0:T(8,128)S(1)}, u32[]{:S(2)}, u32[]{:S(2)}) collective-permute-start(f32[400,256]{1,0:T(8,128)} %get-tuple-element.52), channel_id=1, source_target_pairs={{0,4},{2,6},{4,0},{6,2},{1,5},{3,7},{5,1},{7,3},{8,12},{10,14},{12... | collective-permute-start | bytes 1228808 | tf_op jit(solution)/shard_map/ppermute | solution.py:622
  71.1 29.0 %collective-permute-start.12 = (f32[400,256]{1,0:T(8,128)}, f32[400,256]{1,0:T(8,128)S(1)}, u32[]{:S(2)}, u32[]{:S(2)}) collective-permute-start(f32[400,256]{1,0:T(8,128)} %get-tuple-element.53), channel_id=1, source_target_pairs={{0,2},{2,4},{4,6},{6,0},{1,3},{3,5},{5,7},{7,1},{8,10},{10,12},{12... | collective-permute-start | bytes 1228808 | tf_op jit(solution)/shard_map/ppermute | solution.py:622
  71.9 29.0 %collective-permute-start.13 = (f32[400,256]{1,0:T(8,128)}, f32[400,256]{1,0:T(8,128)S(1)}, u32[]{:S(2)}, u32[]{:S(2)}) collective-permute-start(f32[400,256]{1,0:T(8,128)} %get-tuple-element.54), channel_id=1, source_target_pairs={{0,6},{2,0},{4,2},{6,4},{1,7},{3,1},{5,3},{7,5},{8,14},{10,8},{12,... | collective-permute-start | bytes 1228808 | tf_op jit(solution)/shard_map/ppermute | solution.py:622
  99.3 22.1 %collective-permute-start.16 = (bf16[3840,128]{1,0:T(8,128)(2,1)S(1)}, bf16[3840,128]{1,0:T(8,128)(2,1)}, u32[]{:S(2)}, u32[]{:S(2)}) collective-permute-start(bf16[3840,128]{1,0:T(8,128)(2,1)S(1)} %copy-done), channel_id=1, source_target_pairs={{0,8},{8,0},{1,9},{9,1},{2,10},{10,2},{3,11},{11,3},{4,12},{12,4},... | collective-permute-start | bytes 2949128 | tf_op jit(solution)/shard_map/ppermute | solution.py:626
  104.4 1.0 copy-start.5
  107.5 14.0 %collective-permute-start.18 = (bf16[3840,128]{1,0:T(8,128)(2,1)}, bf16[3840,128]{1,0:T(8,128)(2,1)}, u32[]{:S(2)}, u32[]{:S(2)}) collective-permute-start(bf16[3840,128]{1,0:T(8,128)(2,1)} %get-tuple-element.59.refs_4_), channel_id=1, source_target_pairs={{0,8},{8,0},{1,9},{9,1},{2,10},{10,2},{3,11},{11,3},{4,12},{12,4},... | collective-permute-start | bytes 2949128 | tf_op jit(solution)/shard_map/ppermute | solution.py:626
  107.6 13.9 %collective-permute-start.17 = (bf16[3840,128]{1,0:T(8,128)(2,1)}, bf16[3840,128]{1,0:T(8,128)(2,1)}, u32[]{:S(2)}, u32[]{:S(2)}) collective-permute-start(bf16[3840,128]{1,0:T(8,128)(2,1)} %get-tuple-element.58.refs_2_.refs_1_), channel_id=1, source_target_pairs={{0,8},{8,0},{1,9},{9,1},{2,10},{10,2},{3,11},{11,3},{4,12},{12,4},... | collective-permute-start | bytes 2949128 | tf_op jit(solution)/shard_map/ppermute | solution.py:626
  108.1 36.1 %all-to-all-start.1 = ((bf16[4,256,384]{2,1,0:T(8,128)(2,1)}), bf16[4,256,384]{2,1,0:T(8,128)(2,1)S(1)}, u32[]{:S(2)}, u32[]{:S(2)}) async-start(bf16[4,256,384]{2,1,0:T(8,128)(2,1)} %bitcast.90), calls=%async_computation.1 | async-start | bytes 1572864 | tf_op jit(solution)/shard_map/all_to_all | solution.py:695
  118.4 14.6 %collective-permute-start.14 = (bf16[1920,128]{1,0:T(8,128)(2,1)}, bf16[1920,128]{1,0:T(8,128)(2,1)}, u32[]{:S(2)}, u32[]{:S(2)}) collective-permute-start(bf16[1920,128]{1,0:T(8,128)(2,1)} %get-tuple-element.56), channel_id=1, source_target_pairs={{0,1},{1,0},{2,3},{3,2},{4,5},{5,4},{6,7},{7,6},{8,9},{9,8},{10,11... | collective-permute-start | bytes 1474568 | tf_op jit(solution)/shard_map/ppermute | solution.py:626
  119.6 13.4 %collective-permute-start.15 = (bf16[1920,128]{1,0:T(8,128)(2,1)}, bf16[1920,128]{1,0:T(8,128)(2,1)}, u32[]{:S(2)}, u32[]{:S(2)}) collective-permute-start(bf16[1920,128]{1,0:T(8,128)(2,1)} %get-tuple-element.57), channel_id=1, source_target_pairs={{0,16},{16,0},{1,17},{17,1},{2,18},{18,2},{3,19},{19,3},{4,20},{20... | collective-permute-start | bytes 1474568 | tf_op jit(solution)/shard_map/ppermute | solution.py:626
  133.0 2.1 collective-permute-start.19
  133.1 2.8 %collective-permute-start.20 = (bf16[1920,128]{1,0:T(8,128)(2,1)}, bf16[1920,128]{1,0:T(8,128)(2,1)S(1)}, u32[]{:S(2)}, u32[]{:S(2)}) collective-permute-start(bf16[1920,128]{1,0:T(8,128)(2,1)} %get-tuple-element.61.refs_1_), channel_id=1, source_target_pairs={{0,8},{8,0},{1,9},{9,1},{2,10},{10,2},{3,11},{11,3},{4,12},{12,4},... | collective-permute-start | bytes 1474568 | tf_op jit(solution)/shard_map/ppermute | solution.py:626
  145.1 19.6 %collective-permute-start.25 = (bf16[1024,384]{1,0:T(8,128)(2,1)}, bf16[1024,384]{1,0:T(8,128)(2,1)S(1)}, u32[]{:S(2)}, u32[]{:S(2)}) collective-permute-start(bf16[1024,384]{1,0:T(8,128)(2,1)} %tie.11.refs_0_), channel_id=1, source_target_pairs={{0,1},{1,0},{2,3},{3,2},{4,5},{5,4},{6,7},{7,6},{8,9},{9,8},{10,11... | collective-permute-start | bytes 2359304 | tf_op jit(solution)/shard_map/ppermute | solution.py:626
  145.2 19.6 %collective-permute-start.24 = (bf16[1024,384]{1,0:T(8,128)(2,1)}, bf16[1024,384]{1,0:T(8,128)(2,1)S(1)}, u32[]{:S(2)}, u32[]{:S(2)}) collective-permute-start(bf16[1024,384]{1,0:T(8,128)(2,1)} %tie.11.refs_0_), channel_id=1, source_target_pairs={{0,16},{16,0},{1,17},{17,1},{2,18},{18,2},{3,19},{19,3},{4,20},{20... | collective-permute-start | bytes 2359304 | tf_op jit(solution)/shard_map/ppermute | solution.py:626
  146.5 32.2 %collective-permute-start.21 = (f32[384,256]{1,0:T(8,128)}, f32[384,256]{1,0:T(8,128)S(1)}, u32[]{:S(2)}, u32[]{:S(2)}) collective-permute-start(f32[384,256]{1,0:T(8,128)} %get-tuple-element.63), channel_id=1, source_target_pairs={{0,4},{2,6},{4,0},{6,2},{1,5},{3,7},{5,1},{7,3},{8,12},{10,14},{12... | collective-permute-start | bytes 1179656 | tf_op jit(solution)/shard_map/ppermute | solution.py:622
  148.9 29.8 %collective-permute-start.22 = (f32[384,256]{1,0:T(8,128)}, f32[384,256]{1,0:T(8,128)}, u32[]{:S(2)}, u32[]{:S(2)}) collective-permute-start(f32[384,256]{1,0:T(8,128)} %get-tuple-element.64), channel_id=1, source_target_pairs={{0,2},{2,4},{4,6},{6,0},{1,3},{3,5},{5,7},{7,1},{8,10},{10,12},{12... | collective-permute-start | bytes 1179656 | tf_op jit(solution)/shard_map/ppermute | solution.py:622
  150.9 27.9 %collective-permute-start.23 = (f32[384,256]{1,0:T(8,128)}, f32[384,256]{1,0:T(8,128)}, u32[]{:S(2)}, u32[]{:S(2)}) collective-permute-start(f32[384,256]{1,0:T(8,128)} %get-tuple-element.65), channel_id=1, source_target_pairs={{0,6},{2,0},{4,2},{6,4},{1,7},{3,1},{5,3},{7,5},{8,14},{10,8},{12,... | collective-permute-start | bytes 1179656 | tf_op jit(solution)/shard_map/ppermute | solution.py:622
  165.7 0.9 copy-start.4
  168.5 10.5 %collective-permute-start.26 = (bf16[512,384]{1,0:T(8,128)(2,1)}, bf16[512,384]{1,0:T(8,128)(2,1)S(1)}, u32[]{:S(2)}, u32[]{:S(2)}) collective-permute-start(bf16[512,384]{1,0:T(8,128)(2,1)} %get-tuple-element.70), channel_id=1, source_target_pairs={{0,1},{1,0},{2,3},{3,2},{4,5},{5,4},{6,7},{7,6},{8,9},{9,8},{10,11... | collective-permute-start | bytes 1179656 | tf_op jit(solution)/shard_map/ppermute | solution.py:626
  169.5 9.9 %collective-permute-start.27 = (bf16[512,384]{1,0:T(8,128)(2,1)}, bf16[512,384]{1,0:T(8,128)(2,1)S(1)}, u32[]{:S(2)}, u32[]{:S(2)}) collective-permute-start(bf16[512,384]{1,0:T(8,128)(2,1)} %get-tuple-element.71), channel_id=1, source_target_pairs={{0,16},{16,0},{1,17},{17,1},{2,18},{18,2},{3,19},{19,3},{4,20},{20... | collective-permute-start | bytes 1179656 | tf_op jit(solution)/shard_map/ppermute | solution.py:626
  184.3 28.8 %all-to-all-start.2 = ((bf16[4,256,384]{2,1,0:T(8,128)(2,1)}), bf16[4,256,384]{2,1,0:T(8,128)(2,1)S(1)}, u32[]{:S(2)}, u32[]{:S(2)}) async-start(bf16[4,256,384]{2,1,0:T(8,128)(2,1)} %bitcast.96), calls=%async_computation.2 | async-start | bytes 1572864 | tf_op jit(solution)/shard_map/all_to_all | solution.py:695
  193.5 6.0 %collective-permute-start.28 = (f32[2,48,128]{2,1,0:T(8,128)S(1)}, f32[2,48,128]{2,1,0:T(8,128)S(1)}, u32[]{:S(2)}, u32[]{:S(2)}) collective-permute-start(f32[2,48,128]{2,1,0:T(8,128)S(1)} %bitcast.104), channel_id=1, source_target_pairs={{0,8},{8,16},{16,24},{1,9},{9,17},{17,25},{2,10},{10,18},{18,26},{... | collective-permute-start | bytes 147464 | tf_op jit(solution)/shard_map/ppermute | solution.py:607
  196.2 3.9 %collective-permute-start.29 = (f32[2,48,128]{2,1,0:T(8,128)S(1)}, f32[2,48,128]{2,1,0:T(8,128)S(1)}, u32[]{:S(2)}, u32[]{:S(2)}) collective-permute-start(f32[2,48,128]{2,1,0:T(8,128)S(1)} %bitcast.103), channel_id=1, source_target_pairs={{8,0},{16,8},{24,16},{9,1},{17,9},{25,17},{10,2},{18,10},{26,18},{... | collective-permute-start | bytes 147464 | tf_op jit(solution)/shard_map/ppermute | solution.py:608
  197.5 14.1 %collective-permute-start.35 = (bf16[512,384]{1,0:T(8,128)(2,1)}, bf16[512,384]{1,0:T(8,128)(2,1)S(1)}, u32[]{:S(2)}, u32[]{:S(2)}) collective-permute-start(bf16[512,384]{1,0:T(8,128)(2,1)} %get-tuple-element.77.refs_3_), channel_id=1, source_target_pairs={{0,8},{8,0},{1,9},{9,1},{2,10},{10,2},{3,11},{11,3},{4,12},{12,4},... | collective-permute-start | bytes 1179656 | tf_op jit(solution)/shard_map/ppermute | solution.py:626
  199.4 16.3 %collective-permute-start.36 = (bf16[512,384]{1,0:T(8,128)(2,1)}, bf16[512,384]{1,0:T(8,128)(2,1)}, u32[]{:S(2)}, u32[]{:S(2)}) collective-permute-start(bf16[512,384]{1,0:T(8,128)(2,1)} %get-tuple-element.78.refs_4_), channel_id=1, source_target_pairs={{0,8},{8,0},{1,9},{9,1},{2,10},{10,2},{3,11},{11,3},{4,12},{12,4},... | collective-permute-start | bytes 1179656 | tf_op jit(solution)/shard_map/ppermute | solution.py:626
  199.5 17.9 %copy-start.25 = (f32[2,48,128]{2,1,0:T(8,128)}, f32[2,48,128]{2,1,0:T(8,128)S(1)}, u32[]{:S(2)}) copy-start(f32[2,48,128]{2,1,0:T(8,128)S(1)} %collective-permute-done.28.refs_9_.refs_2_) | copy-start | bytes 147460
  200.0 13.0 %copy-start.26 = (f32[2,48,128]{2,1,0:T(8,128)}, f32[2,48,128]{2,1,0:T(8,128)S(1)}, u32[]{:S(2)}) copy-start(f32[2,48,128]{2,1,0:T(8,128)S(1)} %collective-permute-done.29.refs_10_.refs_3_) | copy-start | bytes 147460
  200.1 7.8 %collective-permute-start.30 = (f32[36,2,128]{2,1,0:T(2,128)S(1)}, f32[36,2,128]{2,1,0:T(2,128)S(1)}, u32[]{:S(2)}, u32[]{:S(2)}) collective-permute-start(f32[36,2,128]{2,1,0:T(2,128)S(1)} %pad_maximum_fusion), channel_id=1, source_target_pairs={{0,1},{1,2},{2,3},{3,4},{4,5},{5,6},{6,7},{8,9},{9,10},{10,11},{11... | collective-permute-start | bytes 110600 | tf_op jit(solution)/shard_map/ppermute | solution.py:613
  203.8 5.9 %collective-permute-start.31 = (f32[36,2,128]{2,1,0:T(2,128)S(1)}, f32[36,2,128]{2,1,0:T(2,128)S(1)}, u32[]{:S(2)}, u32[]{:S(2)}) collective-permute-start(f32[36,2,128]{2,1,0:T(2,128)S(1)} %pad_maximum_fusion.1), channel_id=1, source_target_pairs={{1,0},{2,1},{3,2},{4,3},{5,4},{6,5},{7,6},{9,8},{10,9},{11,10},{12... | collective-permute-start | bytes 110600 | tf_op jit(solution)/shard_map/ppermute | solution.py:614
  205.1 12.3 %collective-permute-start.32 = (bf16[1024,384]{1,0:T(8,128)(2,1)}, bf16[1024,384]{1,0:T(8,128)(2,1)}, u32[]{:S(2)}, u32[]{:S(2)}) collective-permute-start(bf16[1024,384]{1,0:T(8,128)(2,1)} %get-tuple-element.74), channel_id=1, source_target_pairs={{0,8},{8,0},{1,9},{9,1},{2,10},{10,2},{3,11},{11,3},{4,12},{12,4},... | collective-permute-start | bytes 2359304 | tf_op jit(solution)/shard_map/ppermute | solution.py:626
  207.9 5.1 %copy-start.27 = (f32[36,2,128]{2,1,0:T(2,128)}, f32[36,2,128]{2,1,0:T(2,128)S(1)}, u32[]{:S(2)}) copy-start(f32[36,2,128]{2,1,0:T(2,128)S(1)} %collective-permute-done.30.refs_11_.refs_4_) | copy-start | bytes 110596
  207.9 9.5 %collective-permute-start.33 = (bf16[1024,384]{1,0:T(8,128)(2,1)}, bf16[1024,384]{1,0:T(8,128)(2,1)}, u32[]{:S(2)}, u32[]{:S(2)}) collective-permute-start(bf16[1024,384]{1,0:T(8,128)(2,1)} %get-tuple-element.75), channel_id=1, source_target_pairs={{0,8},{8,0},{1,9},{9,1},{2,10},{10,2},{3,11},{11,3},{4,12},{12,4},... | collective-permute-start | bytes 2359304 | tf_op jit(solution)/shard_map/ppermute | solution.py:626
  209.6 3.5 %copy-start.28 = (f32[36,2,128]{2,1,0:T(2,128)}, f32[36,2,128]{2,1,0:T(2,128)S(1)}, u32[]{:S(2)}) copy-start(f32[36,2,128]{2,1,0:T(2,128)S(1)} %collective-permute-done.31.refs_12_.refs_5_) | copy-start | bytes 110596
  209.6 7.8 %collective-permute-start.34 = (bf16[1024,384]{1,0:T(8,128)(2,1)}, bf16[1024,384]{1,0:T(8,128)(2,1)}, u32[]{:S(2)}, u32[]{:S(2)}) collective-permute-start(bf16[1024,384]{1,0:T(8,128)(2,1)} %get-tuple-element.76), channel_id=1, source_target_pairs={{0,8},{8,0},{1,9},{9,1},{2,10},{10,2},{3,11},{11,3},{4,12},{12,4},... | collective-permute-start | bytes 2359304 | tf_op jit(solution)/shard_map/ppermute | solution.py:626
  211.6 5.8 %copy-start.21 = (bf16[512,384]{1,0:T(8,128)(2,1)}, bf16[512,384]{1,0:T(8,128)(2,1)S(1)}, u32[]{:S(2)}) copy-start(bf16[512,384]{1,0:T(8,128)(2,1)S(1)} %collective-permute-done.35.refs_5_) | copy-start | bytes 1179652
  213.1 4.3 %copy-start.2 = (bf16[4,256,384]{2,1,0:T(8,128)(2,1)}, bf16[4,256,384]{2,1,0:T(8,128)(2,1)S(1)}, u32[]{:S(2)}) copy-start(bf16[4,256,384]{2,1,0:T(8,128)(2,1)S(1)} %all-to-all-done.2) | copy-start | bytes 2359300
  213.1 23.6 %collective-permute-start.38 = (bf16[1024,384]{1,0:T(8,128)(2,1)S(1)}, bf16[1024,384]{1,0:T(8,128)(2,1)S(1)}, u32[]{:S(2)}, u32[]{:S(2)}) collective-permute-start(bf16[1024,384]{1,0:T(8,128)(2,1)S(1)} %bitcast.85), channel_id=1, source_target_pairs={{0,1},{1,0},{2,3},{3,2},{4,5},{5,4},{6,7},{7,6},{8,9},{9,8},{10,11... | collective-permute-start | bytes 2359304 | tf_op jit(solution)/shard_map/ppermute | solution.py:626
  215.7 20.9 %collective-permute-start.37 = (bf16[1024,384]{1,0:T(8,128)(2,1)S(1)}, bf16[1024,384]{1,0:T(8,128)(2,1)}, u32[]{:S(2)}, u32[]{:S(2)}) collective-permute-start(bf16[1024,384]{1,0:T(8,128)(2,1)S(1)} %bitcast.86), channel_id=1, source_target_pairs={{0,16},{16,0},{1,17},{17,1},{2,18},{18,2},{3,19},{19,3},{4,20},{20... | collective-permute-start | bytes 2359304 | tf_op jit(solution)/shard_map/ppermute | solution.py:626
  228.8 13.5 %collective-permute-start.41 = (bf16[1024,384]{1,0:T(8,128)(2,1)}, bf16[1024,384]{1,0:T(8,128)(2,1)}, u32[]{:S(2)}, u32[]{:S(2)}) collective-permute-start(bf16[1024,384]{1,0:T(8,128)(2,1)} %bitcast.88), channel_id=1, source_target_pairs={{0,8},{8,0},{1,9},{9,1},{2,10},{10,2},{3,11},{11,3},{4,12},{12,4},... | collective-permute-start | bytes 2359304 | tf_op jit(solution)/shard_map/ppermute | solution.py:626
  239.5 3.0 %collective-permute-start.42 = (bf16[1024,384]{1,0:T(8,128)(2,1)}, bf16[1024,384]{1,0:T(8,128)(2,1)S(1)}, u32[]{:S(2)}, u32[]{:S(2)}) collective-permute-start(bf16[1024,384]{1,0:T(8,128)(2,1)} %get-tuple-element.81.refs_2_), channel_id=1, source_target_pairs={{0,8},{8,0},{1,9},{9,1},{2,10},{10,2},{3,11},{11,3},{4,12},{12,4},... | collective-permute-start | bytes 2359304 | tf_op jit(solution)/shard_map/ppermute | solution.py:626
  240.0 3.4 %collective-permute-start.43 = (bf16[1024,384]{1,0:T(8,128)(2,1)}, bf16[1024,384]{1,0:T(8,128)(2,1)}, u32[]{:S(2)}, u32[]{:S(2)}) collective-permute-start(bf16[1024,384]{1,0:T(8,128)(2,1)} %get-tuple-element.82.refs_4_), channel_id=1, source_target_pairs={{0,8},{8,0},{1,9},{9,1},{2,10},{10,2},{3,11},{11,3},{4,12},{12,4},... | collective-permute-start | bytes 2359304 | tf_op jit(solution)/shard_map/ppermute | solution.py:626
  240.1 15.3 %collective-permute-start.39 = (bf16[512,384]{1,0:T(8,128)(2,1)}, bf16[512,384]{1,0:T(8,128)(2,1)S(1)}, u32[]{:S(2)}, u32[]{:S(2)}) collective-permute-start(bf16[512,384]{1,0:T(8,128)(2,1)} %get-tuple-element.79), channel_id=1, source_target_pairs={{0,1},{1,0},{2,3},{3,2},{4,5},{5,4},{6,7},{7,6},{8,9},{9,8},{10,11... | collective-permute-start | bytes 1179656 | tf_op jit(solution)/shard_map/ppermute | solution.py:626
  240.5 15.0 %collective-permute-start.40 = (bf16[512,384]{1,0:T(8,128)(2,1)}, bf16[512,384]{1,0:T(8,128)(2,1)S(1)}, u32[]{:S(2)}, u32[]{:S(2)}) collective-permute-start(bf16[512,384]{1,0:T(8,128)(2,1)} %get-tuple-element.80), channel_id=1, source_target_pairs={{0,16},{16,0},{1,17},{17,1},{2,18},{18,2},{3,19},{19,3},{4,20},{20... | collective-permute-start | bytes 1179656 | tf_op jit(solution)/shard_map/ppermute | solution.py:626
  242.5 0.9 copy-start.15
  256.9 2.4 collective-permute-start.44
  257.8 2.1 collective-permute-start.45
  (18 other events, 14.1 us)

commit v5 on v4

--- a/solution.py
+++ b/solution.py
@@ -122,7 +122,7 @@
     surveys = taps.shape[0]
     samples = traces.shape[1]
     rows = traces.shape[0] // surveys
-    each = 3
+    each = 6
     out_specs = [pl.BlockSpec((each, rows // 2, samples), lambda i: (i, 0, 0))]
     out_shape = [jax.ShapeDtypeStruct((surveys, rows // 2, samples), jnp.bfloat16)]
     if half == 1:
@@ -235,14 +235,18 @@
         lax.fori_loop(0, (n + group - 1) // group, one_group, 0)
         return 0
 
-    lax.fori_loop(0, tiles, tile_step, 0)
     targets = [total.at[tile] for tile in range(tiles)] if last else [total]
     sends = [
         pltpu.make_async_copy(target, out, sems.at[len(sizes) + 1 + i])
         for i, (target, out) in enumerate(zip(targets, outs, strict=True))
     ]
-    for send in sends:
-        send.start()
+    if last:
+        for tile, send in enumerate(sends):
+            tile_step(tile, 0)
+            send.start()
+    else:
+        lax.fori_loop(0, tiles, tile_step, 0)
+        sends[0].start()
     for send in sends:
         send.wait()
 

time: 270 us -> 268 us (level)
  Pallas kernels: 111 us -> 106 us
  waiting for transfers between devices: 60.4 us -> 64 us
    pallas_call x4, Pallas kernels: 39.6 us -> 36.6 us  [stack_call(): pl.pallas_call(functools.partial(stack_kernel, spec), out_shape=single if...]
  transfers between devices with their start and end apart: 49 -> 49, of which waited for: 18 -> 20; matrix products, arithmetic and copies ran while one was open for 3% -> 3% of each run, Pallas kernels for 35% -> 34%
where the time goes in v5:
time: 268 us; the launch traced here: 266 us
  Pallas kernels  106 us (40%)
  starting transfers between devices  75.5 us (28%)
  waiting for transfers between devices  64 us (24%)
  local copies, waits for them, and re-layouts  17.4 us (6%)
    pallas_call x4, Pallas kernels, read_call(): pl.pallas_call(functools.partial(read_kernel, (sizes, first, last, len(to...  39.8 us
    pallas_call x4, Pallas kernels, stack_call(): pl.pallas_call(functools.partial(stack_kernel, spec), out_shape=single if...  36.6 us
    ppermute x36, starting transfers between devices, over(): return lax.ppermute(value, axis, SWAP)  32.7 us
    ppermute x6, waiting for transfers between devices, along_z(): return lax.ppermute(value, 'z', [(i, (i + step) % 4) for i in range(4)])  24.3 us
    ppermute x36, waiting for transfers between devices, over(): return lax.ppermute(value, axis, SWAP)  23.7 us
    all_to_all x2, starting transfers between devices, over_z(): return lax.all_to_all(value, 'z', 0, 0, tiled=True)  18.4 us
    ppermute x6, starting transfers between devices, along_z(): return lax.ppermute(value, 'z', [(i, (i + step) % 4) for i in range(4)])  13.2 us
    unnamed x69, local copies, waits for them, and re-layouts  13.2 us
  transfers between devices with their start and end apart: 49, of which 20 were waited for; matrix products, arithmetic and copies ran while one was open for 3% of the time, Pallas kernels for 34%

profile of v5, /device:TPU:0, one launch (start us, length us, event | category | flops | bytes accessed | tf_op | source)
XLA Modules:
  0.0 266.2 jit_solution(11813631924356061487)
XLA Ops:
  0.7 3.4 %filter_0.1 = bf16[12,320,128]{2,1,0:T(8,128)(2,1)} custom-call(f32[12,64]{1,0:T(8,128)} %taps.3, bf16[12,640,128]{2,1,0:T(8,128)(2,1)} %bitcast.83), custom_call_target="tpu_custom_call" | custom-call | tf_op jit(solution)/shard_map/filter_0/pallas_call | solution.py:131
  4.1 3.0 %collective-permute-start.2 = (bf16[3840,128]{1,0:T(8,128)(2,1)}, bf16[3840,128]{1,0:T(8,128)(2,1)S(1)}, u32[]{:S(2)}, u32[]{:S(2)}) collective-permute-start(bf16[3840,128]{1,0:T(8,128)(2,1)} %bitcast.77), channel_id=1, source_target_pairs={{0,1},{1,0},{2,3},{3,2},{4,5},{5,4},{6,7},{7,6},{8,9},{9,8},{10,11... | collective-permute-start | bytes 2949128 | tf_op jit(solution)/shard_map/ppermute | solution.py:630
  7.0 1.5 collective-permute-start.1
  10.9 3.4 %all-to-all-start = ((s32[8,40,128]{2,1,0:T(8,128)}), s32[8,40,128]{2,1,0:T(8,128)S(1)}, u32[]{:S(2)}, u32[]{:S(2)}) async-start(s32[8,40,128]{2,1,0:T(8,128)} %pad_add_fusion), calls=%async_computation | async-start | bytes 327680 | tf_op jit(solution)/shard_map/all_to_all | solution.py:650
  15.5 3.4 %filter_1.1 = (bf16[12,320,128]{2,1,0:T(8,128)(2,1)}, bf16[12,128,128]{2,1,0:T(8,128)(2,1)}) custom-call(f32[12,64]{1,0:T(8,128)} %taps.3, bf16[12,640,128]{2,1,0:T(8,128)(2,1)} %bitcast.84), custom_call_target="tpu_custom_call" | custom-call | tf_op jit(solution)/shard_map/filter_1/pallas_call | solution.py:131
  20.3 11.9 %all-to-all-done.refs_1_.cells = s32[8,40,128]{2,1,0:T(8,128)S(1)} async-done(((s32[8,40,128]{2,1,0:T(8,128)}), s32[8,40,128]{2,1,0:T(8,128)S(1)}, u32[]{:S(2)}, u32[]{:S(2)}) %all-to-all-start) | async-done | bytes 163872 | tf_op jit(solution)/shard_map/all_to_all | solution.py:650
  33.2 2.0 gate.4
  35.9 1.2 collective-permute-start.7
  37.1 1.5 collective-permute-start.8
  38.8 0.9 collective-permute-done.4.refs_5_
  39.7 11.7 %stack.220.refs_1_.refs_2_.refs_4_ = f32[4,400,256]{2,1,0:T(8,128)} custom-call(s32[68]{0:T(128)} %stack.219.refs_2_.order, s32[8,40,128]{2,1,0:T(8,128)} %copy-done.9, bf16[3840,128]{1,0:T(8,128)(2,1)} %bitcast.80, bf16[3840,128]{1,0:T(8,128)(2,1)} %collective-permute-done.refs_1_, bf16[3840,128]{1,0:T(8,128)(2,1)} %get-tuple-element.45.refs_2_, ...), custom_call_target="tpu_custom_call" | custom-call | flops 34359738368 | bytes 1048576 | tf_op jit(solution)/shard_map/stack/pallas_call | solution.py:263
  51.4 1.2 collective-permute-start.6
  52.6 2.1 collective-permute-start.5
  55.5 0.8 copy-done.11
  56.8 1.7 collective-permute-done.9.refs_2_
  59.2 7.4 %stack.221 = (f32[400,256]{1,0:T(8,128)}, f32[400,256]{1,0:T(8,128)}, f32[400,256]{1,0:T(8,128)}, f32[400,256]{1,0:T(8,128)}) custom-call(s32[68]{0:T(128)} %stack.219.refs_2_.order, s32[8,40,128]{2,1,0:T(8,128)} %copy-done.9, bf16[1920,128]{1,0:T(8,128)(2,1)} %get-tuple-element.49.refs_0_, bf16[1920,128]{1,0:T(8,128)(2,1)} %get-tuple-element.50.refs_1_, ...), custom_call_target="tpu_custom_call" | custom-call | flops 1 | bytes 1 | tf_op jit(solution)/shard_map/stack/pallas_call | solution.py:263
  66.6 2.9 %collective-permute-start.11 = (f32[400,256]{1,0:T(8,128)}, f32[400,256]{1,0:T(8,128)S(1)}, u32[]{:S(2)}, u32[]{:S(2)}) collective-permute-start(f32[400,256]{1,0:T(8,128)} %get-tuple-element.52), channel_id=1, source_target_pairs={{0,4},{2,6},{4,0},{6,2},{1,5},{3,7},{5,1},{7,3},{8,12},{10,14},{12... | collective-permute-start | bytes 1228808 | tf_op jit(solution)/shard_map/ppermute | solution.py:626
  69.5 3.8 %collective-permute-start.13 = (f32[400,256]{1,0:T(8,128)}, f32[400,256]{1,0:T(8,128)S(1)}, u32[]{:S(2)}, u32[]{:S(2)}) collective-permute-start(f32[400,256]{1,0:T(8,128)} %get-tuple-element.54), channel_id=1, source_target_pairs={{0,6},{2,0},{4,2},{6,4},{1,7},{3,1},{5,3},{7,5},{8,14},{10,8},{12,... | collective-permute-start | bytes 1228808 | tf_op jit(solution)/shard_map/ppermute | solution.py:626
  73.3 24.3 %collective-permute-done.11.refs_1_ = f32[400,256]{1,0:T(8,128)S(1)} collective-permute-done((f32[400,256]{1,0:T(8,128)}, f32[400,256]{1,0:T(8,128)S(1)}, u32[]{:S(2)}, u32[]{:S(2)}) %collective-permute-start.11) | collective-permute-done | bytes 409632 | tf_op jit(solution)/shard_map/ppermute | solution.py:626
  99.9 2.8 %image_0.1 = (bf16[1024,384]{1,0:T(8,128)(2,1)}, f32[384,256]{1,0:T(8,128)}, f32[16,256]{1,0:T(8,128)}) custom-call(f32[400,256]{1,0:T(8,128)} %get-tuple-element.51.refs_0_, f32[400,256]{1,0:T(8,128)} %copy-done.18, f32[400,256]{1,0:T(8,128)} %copy-done.19, f32[400,256]{1,0:T(8,128)} %copy-done.20), custom_call_target="tpu_custom_call" | custom-call | flops 1 | bytes 1 | tf_op jit(solution)/shard_map/image_0/pallas_call | solution.py:333
  102.7 1.0 copy-done.5
  103.8 2.1 gate.5
  106.4 10.0 %all-to-all-start.1 = ((bf16[4,256,384]{2,1,0:T(8,128)(2,1)}), bf16[4,256,384]{2,1,0:T(8,128)(2,1)S(1)}, u32[]{:S(2)}, u32[]{:S(2)}) async-start(bf16[4,256,384]{2,1,0:T(8,128)(2,1)} %bitcast.90), calls=%async_computation.1 | async-start | bytes 1572864 | tf_op jit(solution)/shard_map/all_to_all | solution.py:699
  116.4 1.8 collective-permute-start.14
  118.4 10.7 %stack.222.refs_2_.refs_4_ = f32[4,384,256]{2,1,0:T(8,128)} custom-call(s32[68]{0:T(128)} %stack.219.refs_2_.order, s32[8,40,128]{2,1,0:T(8,128)} %copy-done.9, bf16[3840,128]{1,0:T(8,128)(2,1)} %tie.7.refs_0_.own, bf16[3840,128]{1,0:T(8,128)(2,1)} %collective-permute-done.16.refs_1_, bf16[3840,128]{1,0:T(8,128)(2,1)} %get-tuple-element.58.refs_2_.refs_1_, ...), custom_call_target="tpu_custom_call" | custom-call | flops 34359738368 | bytes 1048576 | tf_op jit(solution)/shard_map/stack/pallas_call | solution.py:263
  129.7 1.5 collective-permute-done.15.refs_1_
  131.6 1.6 collective-permute-done.19.refs_2_
  134.8 6.8 %stack.223 = (f32[384,256]{1,0:T(8,128)}, f32[384,256]{1,0:T(8,128)}, f32[384,256]{1,0:T(8,128)}, f32[384,256]{1,0:T(8,128)}) custom-call(s32[68]{0:T(128)} %stack.219.refs_2_.order, s32[8,40,128]{2,1,0:T(8,128)} %copy-done.9, bf16[1920,128]{1,0:T(8,128)(2,1)} %get-tuple-element.60.refs_0_, bf16[1920,128]{1,0:T(8,128)(2,1)} %get-tuple-element.61.refs_1_, ...), custom_call_target="tpu_custom_call" | custom-call | flops 1 | bytes 1 | tf_op jit(solution)/shard_map/stack/pallas_call | solution.py:263
  141.6 0.9 copy-done.1
  142.8 1.3 collective-permute-start.24
  144.1 2.7 %collective-permute-start.21 = (f32[384,256]{1,0:T(8,128)}, f32[384,256]{1,0:T(8,128)S(1)}, u32[]{:S(2)}, u32[]{:S(2)}) collective-permute-start(f32[384,256]{1,0:T(8,128)} %get-tuple-element.63), channel_id=1, source_target_pairs={{0,4},{2,6},{4,0},{6,2},{1,5},{3,7},{5,1},{7,3},{8,12},{10,14},{12... | collective-permute-start | bytes 1179656 | tf_op jit(solution)/shard_map/ppermute | solution.py:626
  146.8 1.5 collective-permute-start.22
  148.3 2.3 collective-permute-start.23
  150.6 10.5 %collective-permute-done.25.from_y = bf16[1024,384]{1,0:T(8,128)(2,1)S(1)} collective-permute-done((bf16[1024,384]{1,0:T(8,128)(2,1)}, bf16[1024,384]{1,0:T(8,128)(2,1)S(1)}, u32[]{:S(2)}, u32[]{:S(2)}) %collective-permute-start.25) | collective-permute-done | bytes 786464 | tf_op jit(solution)/shard_map/ppermute | solution.py:630
  161.1 1.3 collective-permute-done.24.from_x
  162.4 0.9 copy-done.4
  163.3 2.0 gate.6
  165.3 1.4 collective-permute-start.26
  166.6 1.7 collective-permute-start.27
  168.3 7.9 %read.4.refs_6_.refs_7_ = f32[3840,128]{1,0:T(8,128)} custom-call(s32[68]{0:T(128)} %stack.219.refs_2_.order, s32[32]{0:T(128)} %bitcast.106, s32[256]{0:T(256)} %reshape.69.refs_4_.blocks, s32[256,128]{1,0:T(8,128)} %bitcast.92, bf16[3840,128]{1,0:T(8,128)(2,1)} %bitcast.81, bf16[1024,384]{1,0:T(8,128)(2,1)} %tie.11.refs_0_, ...), custom_call_target="tpu_custom_call" | custom-call | flops 1 | bytes 1 | tf_op jit(solution)/shard_map/read/pallas_call | solution.py:467
  177.6 4.2 %image_1.1 = (bf16[1024,384]{1,0:T(8,128)(2,1)}, f32[1536,128]{1,0:T(8,128)}) custom-call(f32[384,256]{1,0:T(8,128)} %get-tuple-element.62.refs_1_.refs_0_, f32[384,256]{1,0:T(8,128)} %copy-done.24, f32[384,256]{1,0:T(8,128)} %collective-permute-done.22.refs_2_, f32[384,256]{1,0:T(8,128)} %collective-permute-done.23.refs_3_, ...), custom_call_target="tpu_custom_call" | custom-call | flops 1 | bytes 1 | tf_op jit(solution)/shard_map/image_1/pallas_call | solution.py:333
  181.8 8.4 %all-to-all-start.2 = ((bf16[4,256,384]{2,1,0:T(8,128)(2,1)}), bf16[4,256,384]{2,1,0:T(8,128)(2,1)S(1)}, u32[]{:S(2)}, u32[]{:S(2)}) async-start(bf16[4,256,384]{2,1,0:T(8,128)(2,1)} %bitcast.96), calls=%async_computation.2 | async-start | bytes 1572864 | tf_op jit(solution)/shard_map/all_to_all | solution.py:699
  190.2 0.8 fusion.1
  191.0 1.6 collective-permute-start.28
  192.7 1.0 fusion
  193.7 1.3 collective-permute-start.29
  195.0 1.8 collective-permute-start.35
  197.5 3.5 %collective-permute-start.30 = (f32[36,2,128]{2,1,0:T(2,128)S(1)}, f32[36,2,128]{2,1,0:T(2,128)S(1)}, u32[]{:S(2)}, u32[]{:S(2)}) collective-permute-start(f32[36,2,128]{2,1,0:T(2,128)S(1)} %pad_maximum_fusion), channel_id=1, source_target_pairs={{0,1},{1,2},{2,3},{3,4},{4,5},{5,6},{6,7},{8,9},{9,10},{10,11},{11... | collective-permute-start | bytes 110600 | tf_op jit(solution)/shard_map/ppermute | solution.py:617
  201.0 1.3 collective-permute-start.31
  202.3 2.6 collective-permute-start.32
  205.0 1.9 collective-permute-done.31.refs_12_.refs_5_
  206.8 2.1 collective-permute-start.34
  209.0 1.6 all-to-all-done.2
  210.6 2.6 collective-permute-start.38
  213.3 0.8 collective-permute-start.37
  214.8 11.4 %read.5.refs_6_.refs_5_ = f32[3840,128]{1,0:T(8,128)} custom-call(s32[68]{0:T(128)} %stack.219.refs_2_.order, s32[32]{0:T(128)} %bitcast.107, s32[256]{0:T(256)} %reshape.69.refs_4_.blocks, s32[256,128]{1,0:T(8,128)} %bitcast.93, bf16[3840,128]{1,0:T(8,128)(2,1)} %bitcast.82, bf16[1024,384]{1,0:T(8,128)(2,1)} %collective-permute-done.32.refs_0_, ...), custom_call_target="tpu_custom_call" | custom-call | flops 1 | bytes 1 | tf_op jit(solution)/shard_map/read/pallas_call | solution.py:467
  226.3 7.7 %tensor.1.refs_0_ = f32[6,32,48,128]{3,2,1,0:T(8,128)} custom-call(s32[4]{0:T(128)} %pad_add_fusion.2.refs_0_, f32[32,48,128]{2,1,0:T(8,128)} %bitcast.99, f32[2,48,128]{2,1,0:T(8,128)} %copy-done.25, f32[2,48,128]{2,1,0:T(8,128)} %copy-done.26, f32[36,2,128]{2,1,0:T(2,128)} %copy-done.27, f32[36,2,128]{2,1,0:T(2,128)} %copy-done.28, ...), custom_call_target="tpu_custom_call" | custom-call | flops 1 | bytes 1 | tf_op jit(solution)/shard_map/tensor/pallas_call | solution.py:591
  234.0 0.9 copy-done.8
  234.9 1.9 gate.7
  237.5 1.5 collective-permute-start.39
  239.9 0.9 collective-permute-done.43.refs_5_
  240.8 12.5 %read.6.refs_2_.refs_6_ = f32[3840,128]{1,0:T(8,128)} custom-call(s32[68]{0:T(128)} %stack.219.refs_2_.order, s32[32]{0:T(128)} %bitcast.108, s32[256]{0:T(256)} %reshape.69.refs_4_.blocks, s32[256,128]{1,0:T(8,128)} %bitcast.94, bf16[3840,128]{1,0:T(8,128)(2,1)} %tie.7.refs_0_.own, bf16[1024,384]{1,0:T(8,128)(2,1)} %bitcast.89, ...), custom_call_target="tpu_custom_call" | custom-call | flops 1 | bytes 1 | tf_op jit(solution)/shard_map/read/pallas_call | solution.py:467
  255.3 1.4 collective-permute-done.44.refs_2_
  258.1 8.0 %read.7 = f32[7680,128]{1,0:T(8,128)} custom-call(s32[68]{0:T(128)} %stack.219.refs_2_.order, s32[32]{0:T(128)} %bitcast.109, s32[256]{0:T(256)} %reshape.69.refs_4_.blocks, s32[256,128]{1,0:T(8,128)} %bitcast.95, bf16[3840,128]{1,0:T(8,128)(2,1)} %tie.7.refs_0_.own, bf16[512,384]{1,0:T(8,128)(2,1)} %get-tuple-element.83.refs_0_, ...), custom_call_target="tpu_custom_call" | custom-call | flops 1 | bytes 1 | tf_op jit(solution)/shard_map/read/pallas_call | solution.py:467
  (148 shorter events, 22.5 us)
Async XLA Ops:
  0.6 8.4 %copy-start.30 = (s32[1,32]{1,0:T(1,128)S(1)}, s32[1,32]{1,0:T(1,128)}, u32[]{:S(2)}) copy-start(s32[1,32]{1,0:T(1,128)} %param.9) | copy-start | bytes 388
  0.6 9.2 %copy-start.31 = (s32[1,32,7]{1,0,2:T(1,128)S(1)}, s32[1,32,7]{1,0,2:T(1,128)}, u32[]{:S(2)}) copy-start(s32[1,32,7]{1,0,2:T(1,128)} %param.7) | copy-start | bytes 2692
  0.7 9.4 %copy-start.29 = (s32[1,32,7,128]{3,1,2,0:T(8,128)S(1)}, s32[1,32,7,128]{3,1,2,0:T(8,128)}, u32[]{:S(2)}) copy-start(s32[1,32,7,128]{3,1,2,0:T(8,128)} %param.8) | copy-start | bytes 344068
  4.1 28.2 %collective-permute-start.2 = (bf16[3840,128]{1,0:T(8,128)(2,1)}, bf16[3840,128]{1,0:T(8,128)(2,1)S(1)}, u32[]{:S(2)}, u32[]{:S(2)}) collective-permute-start(bf16[3840,128]{1,0:T(8,128)(2,1)} %bitcast.77), channel_id=1, source_target_pairs={{0,1},{1,0},{2,3},{3,2},{4,5},{5,4},{6,7},{7,6},{8,9},{9,8},{10,11... | collective-permute-start | bytes 2949128 | tf_op jit(solution)/shard_map/ppermute | solution.py:630
  7.0 25.2 %collective-permute-start.1 = (bf16[3840,128]{1,0:T(8,128)(2,1)}, bf16[3840,128]{1,0:T(8,128)(2,1)}, u32[]{:S(2)}, u32[]{:S(2)}) collective-permute-start(bf16[3840,128]{1,0:T(8,128)(2,1)} %bitcast.78), channel_id=1, source_target_pairs={{0,16},{16,0},{1,17},{17,1},{2,18},{18,2},{3,19},{19,3},{4,20},{20... | collective-permute-start | bytes 2949128 | tf_op jit(solution)/shard_map/ppermute | solution.py:630
  10.9 21.3 %all-to-all-start = ((s32[8,40,128]{2,1,0:T(8,128)}), s32[8,40,128]{2,1,0:T(8,128)S(1)}, u32[]{:S(2)}, u32[]{:S(2)}) async-start(s32[8,40,128]{2,1,0:T(8,128)} %pad_add_fusion), calls=%async_computation | async-start | bytes 327680 | tf_op jit(solution)/shard_map/all_to_all | solution.py:650
  14.3 24.3 %collective-permute-start = (bf16[3840,128]{1,0:T(8,128)(2,1)}, bf16[3840,128]{1,0:T(8,128)(2,1)}, u32[]{:S(2)}, u32[]{:S(2)}) collective-permute-start(bf16[3840,128]{1,0:T(8,128)(2,1)} %bitcast.79), channel_id=1, source_target_pairs={{0,8},{8,0},{1,9},{9,1},{2,10},{10,2},{3,11},{11,3},{4,12},{12,4},... | collective-permute-start | bytes 2949128 | tf_op jit(solution)/shard_map/ppermute | solution.py:630
  32.2 1.0 copy-start.14
  35.3 3.5 %collective-permute-start.3 = (bf16[3840,128]{1,0:T(8,128)(2,1)}, bf16[3840,128]{1,0:T(8,128)(2,1)S(1)}, u32[]{:S(2)}, u32[]{:S(2)}) collective-permute-start(bf16[3840,128]{1,0:T(8,128)(2,1)} %get-tuple-element.45.refs_2_), channel_id=1, source_target_pairs={{0,8},{8,0},{1,9},{9,1},{2,10},{10,2},{3,11},{11,3},{4,12},{12,4},... | collective-permute-start | bytes 2949128 | tf_op jit(solution)/shard_map/ppermute | solution.py:630
  35.4 4.3 %collective-permute-start.4 = (bf16[3840,128]{1,0:T(8,128)(2,1)}, bf16[3840,128]{1,0:T(8,128)(2,1)}, u32[]{:S(2)}, u32[]{:S(2)}) collective-permute-start(bf16[3840,128]{1,0:T(8,128)(2,1)} %get-tuple-element.46.refs_4_), channel_id=1, source_target_pairs={{0,8},{8,0},{1,9},{9,1},{2,10},{10,2},{3,11},{11,3},{4,12},{12,4},... | collective-permute-start | bytes 2949128 | tf_op jit(solution)/shard_map/ppermute | solution.py:630
  35.9 18.8 %collective-permute-start.7 = (bf16[1920,128]{1,0:T(8,128)(2,1)}, bf16[1920,128]{1,0:T(8,128)(2,1)S(1)}, u32[]{:S(2)}, u32[]{:S(2)}) collective-permute-start(bf16[1920,128]{1,0:T(8,128)(2,1)} %get-tuple-element.47), channel_id=1, source_target_pairs={{0,1},{1,0},{2,3},{3,2},{4,5},{5,4},{6,7},{7,6},{8,9},{9,8},{10,11... | collective-permute-start | bytes 1474568 | tf_op jit(solution)/shard_map/ppermute | solution.py:630
  37.1 17.5 %collective-permute-start.8 = (bf16[1920,128]{1,0:T(8,128)(2,1)}, bf16[1920,128]{1,0:T(8,128)(2,1)S(1)}, u32[]{:S(2)}, u32[]{:S(2)}) collective-permute-start(bf16[1920,128]{1,0:T(8,128)(2,1)} %get-tuple-element.48), channel_id=1, source_target_pairs={{0,16},{16,0},{1,17},{17,1},{2,18},{18,2},{3,19},{19,3},{4,20},{20... | collective-permute-start | bytes 1474568 | tf_op jit(solution)/shard_map/ppermute | solution.py:630
  38.8 1.0 copy-start.32
  51.4 51.3 %collective-permute-start.6 = (bf16[3840,128]{1,0:T(8,128)(2,1)}, bf16[3840,128]{1,0:T(8,128)(2,1)}, u32[]{:S(2)}, u32[]{:S(2)}) collective-permute-start(bf16[3840,128]{1,0:T(8,128)(2,1)} %tie.7.refs_0_.own), channel_id=1, source_target_pairs={{0,1},{1,0},{2,3},{3,2},{4,5},{5,4},{6,7},{7,6},{8,9},{9,8},{10,11... | collective-permute-start | bytes 2949128 | tf_op jit(solution)/shard_map/ppermute | solution.py:630
  52.6 50.2 %collective-permute-start.5 = (bf16[3840,128]{1,0:T(8,128)(2,1)}, bf16[3840,128]{1,0:T(8,128)(2,1)S(1)}, u32[]{:S(2)}, u32[]{:S(2)}) collective-permute-start(bf16[3840,128]{1,0:T(8,128)(2,1)} %tie.7.refs_0_.own), channel_id=1, source_target_pairs={{0,16},{16,0},{1,17},{17,1},{2,18},{18,2},{3,19},{19,3},{4,20},{20... | collective-permute-start | bytes 2949128 | tf_op jit(solution)/shard_map/ppermute | solution.py:630
  56.3 41.4 %copy-start = (bf16[3840,128]{1,0:T(8,128)(2,1)S(1)}, bf16[3840,128]{1,0:T(8,128)(2,1)}, u32[]{:S(2)}) copy-start(bf16[3840,128]{1,0:T(8,128)(2,1)} %tie.7.refs_0_.own) | copy-start | bytes 2949124
  56.3 2.2 collective-permute-start.9
  56.3 2.9 %collective-permute-start.10 = (bf16[1920,128]{1,0:T(8,128)(2,1)}, bf16[1920,128]{1,0:T(8,128)(2,1)}, u32[]{:S(2)}, u32[]{:S(2)}) collective-permute-start(bf16[1920,128]{1,0:T(8,128)(2,1)} %get-tuple-element.50.refs_1_), channel_id=1, source_target_pairs={{0,8},{8,0},{1,9},{9,1},{2,10},{10,2},{3,11},{11,3},{4,12},{12,4},... | collective-permute-start | bytes 1474568 | tf_op jit(solution)/shard_map/ppermute | solution.py:630
  66.6 31.1 %collective-permute-start.11 = (f32[400,256]{1,0:T(8,128)}, f32[400,256]{1,0:T(8,128)S(1)}, u32[]{:S(2)}, u32[]{:S(2)}) collective-permute-start(f32[400,256]{1,0:T(8,128)} %get-tuple-element.52), channel_id=1, source_target_pairs={{0,4},{2,6},{4,0},{6,2},{1,5},{3,7},{5,1},{7,3},{8,12},{10,14},{12... | collective-permute-start | bytes 1228808 | tf_op jit(solution)/shard_map/ppermute | solution.py:626
  69.5 28.9 %collective-permute-start.12 = (f32[400,256]{1,0:T(8,128)}, f32[400,256]{1,0:T(8,128)S(1)}, u32[]{:S(2)}, u32[]{:S(2)}) collective-permute-start(f32[400,256]{1,0:T(8,128)} %get-tuple-element.53), channel_id=1, source_target_pairs={{0,2},{2,4},{4,6},{6,0},{1,3},{3,5},{5,7},{7,1},{8,10},{10,12},{12... | collective-permute-start | bytes 1228808 | tf_op jit(solution)/shard_map/ppermute | solution.py:626
  69.5 29.6 %collective-permute-start.13 = (f32[400,256]{1,0:T(8,128)}, f32[400,256]{1,0:T(8,128)S(1)}, u32[]{:S(2)}, u32[]{:S(2)}) collective-permute-start(f32[400,256]{1,0:T(8,128)} %get-tuple-element.54), channel_id=1, source_target_pairs={{0,6},{2,0},{4,2},{6,4},{1,7},{3,1},{5,3},{7,5},{8,14},{10,8},{12,... | collective-permute-start | bytes 1228808 | tf_op jit(solution)/shard_map/ppermute | solution.py:626
  97.7 20.7 %collective-permute-start.16 = (bf16[3840,128]{1,0:T(8,128)(2,1)S(1)}, bf16[3840,128]{1,0:T(8,128)(2,1)}, u32[]{:S(2)}, u32[]{:S(2)}) collective-permute-start(bf16[3840,128]{1,0:T(8,128)(2,1)S(1)} %copy-done), channel_id=1, source_target_pairs={{0,8},{8,0},{1,9},{9,1},{2,10},{10,2},{3,11},{11,3},{4,12},{12,4},... | collective-permute-start | bytes 2949128 | tf_op jit(solution)/shard_map/ppermute | solution.py:630
  102.7 1.0 copy-start.5
  105.8 12.6 %collective-permute-start.18 = (bf16[3840,128]{1,0:T(8,128)(2,1)}, bf16[3840,128]{1,0:T(8,128)(2,1)}, u32[]{:S(2)}, u32[]{:S(2)}) collective-permute-start(bf16[3840,128]{1,0:T(8,128)(2,1)} %get-tuple-element.59.refs_4_), channel_id=1, source_target_pairs={{0,8},{8,0},{1,9},{9,1},{2,10},{10,2},{3,11},{11,3},{4,12},{12,4},... | collective-permute-start | bytes 2949128 | tf_op jit(solution)/shard_map/ppermute | solution.py:630
  105.9 12.5 %collective-permute-start.17 = (bf16[3840,128]{1,0:T(8,128)(2,1)}, bf16[3840,128]{1,0:T(8,128)(2,1)}, u32[]{:S(2)}, u32[]{:S(2)}) collective-permute-start(bf16[3840,128]{1,0:T(8,128)(2,1)} %get-tuple-element.58.refs_2_.refs_1_), channel_id=1, source_target_pairs={{0,8},{8,0},{1,9},{9,1},{2,10},{10,2},{3,11},{11,3},{4,12},{12,4},... | collective-permute-start | bytes 2949128 | tf_op jit(solution)/shard_map/ppermute | solution.py:630
  106.4 35.2 %all-to-all-start.1 = ((bf16[4,256,384]{2,1,0:T(8,128)(2,1)}), bf16[4,256,384]{2,1,0:T(8,128)(2,1)S(1)}, u32[]{:S(2)}, u32[]{:S(2)}) async-start(bf16[4,256,384]{2,1,0:T(8,128)(2,1)} %bitcast.90), calls=%async_computation.1 | async-start | bytes 1572864 | tf_op jit(solution)/shard_map/all_to_all | solution.py:699
  116.4 13.3 %collective-permute-start.14 = (bf16[1920,128]{1,0:T(8,128)(2,1)}, bf16[1920,128]{1,0:T(8,128)(2,1)}, u32[]{:S(2)}, u32[]{:S(2)}) collective-permute-start(bf16[1920,128]{1,0:T(8,128)(2,1)} %get-tuple-element.56), channel_id=1, source_target_pairs={{0,1},{1,0},{2,3},{3,2},{4,5},{5,4},{6,7},{7,6},{8,9},{9,8},{10,11... | collective-permute-start | bytes 1474568 | tf_op jit(solution)/shard_map/ppermute | solution.py:630
  118.2 13.0 %collective-permute-start.15 = (bf16[1920,128]{1,0:T(8,128)(2,1)}, bf16[1920,128]{1,0:T(8,128)(2,1)}, u32[]{:S(2)}, u32[]{:S(2)}) collective-permute-start(bf16[1920,128]{1,0:T(8,128)(2,1)} %get-tuple-element.57), channel_id=1, source_target_pairs={{0,16},{16,0},{1,17},{17,1},{2,18},{18,2},{3,19},{19,3},{4,20},{20... | collective-permute-start | bytes 1474568 | tf_op jit(solution)/shard_map/ppermute | solution.py:630
  131.1 2.1 collective-permute-start.19
  131.1 2.8 %collective-permute-start.20 = (bf16[1920,128]{1,0:T(8,128)(2,1)}, bf16[1920,128]{1,0:T(8,128)(2,1)S(1)}, u32[]{:S(2)}, u32[]{:S(2)}) collective-permute-start(bf16[1920,128]{1,0:T(8,128)(2,1)} %get-tuple-element.61.refs_1_), channel_id=1, source_target_pairs={{0,8},{8,0},{1,9},{9,1},{2,10},{10,2},{3,11},{11,3},{4,12},{12,4},... | collective-permute-start | bytes 1474568 | tf_op jit(solution)/shard_map/ppermute | solution.py:630
  142.5 18.6 %collective-permute-start.25 = (bf16[1024,384]{1,0:T(8,128)(2,1)}, bf16[1024,384]{1,0:T(8,128)(2,1)S(1)}, u32[]{:S(2)}, u32[]{:S(2)}) collective-permute-start(bf16[1024,384]{1,0:T(8,128)(2,1)} %tie.11.refs_0_), channel_id=1, source_target_pairs={{0,1},{1,0},{2,3},{3,2},{4,5},{5,4},{6,7},{7,6},{8,9},{9,8},{10,11... | collective-permute-start | bytes 2359304 | tf_op jit(solution)/shard_map/ppermute | solution.py:630
  142.8 19.5 %collective-permute-start.24 = (bf16[1024,384]{1,0:T(8,128)(2,1)}, bf16[1024,384]{1,0:T(8,128)(2,1)S(1)}, u32[]{:S(2)}, u32[]{:S(2)}) collective-permute-start(bf16[1024,384]{1,0:T(8,128)(2,1)} %tie.11.refs_0_), channel_id=1, source_target_pairs={{0,16},{16,0},{1,17},{17,1},{2,18},{18,2},{3,19},{19,3},{4,20},{20... | collective-permute-start | bytes 2359304 | tf_op jit(solution)/shard_map/ppermute | solution.py:630
  144.1 32.2 %collective-permute-start.21 = (f32[384,256]{1,0:T(8,128)}, f32[384,256]{1,0:T(8,128)S(1)}, u32[]{:S(2)}, u32[]{:S(2)}) collective-permute-start(f32[384,256]{1,0:T(8,128)} %get-tuple-element.63), channel_id=1, source_target_pairs={{0,4},{2,6},{4,0},{6,2},{1,5},{3,7},{5,1},{7,3},{8,12},{10,14},{12... | collective-permute-start | bytes 1179656 | tf_op jit(solution)/shard_map/ppermute | solution.py:626
  146.8 29.5 %collective-permute-start.22 = (f32[384,256]{1,0:T(8,128)}, f32[384,256]{1,0:T(8,128)}, u32[]{:S(2)}, u32[]{:S(2)}) collective-permute-start(f32[384,256]{1,0:T(8,128)} %get-tuple-element.64), channel_id=1, source_target_pairs={{0,2},{2,4},{4,6},{6,0},{1,3},{3,5},{5,7},{7,1},{8,10},{10,12},{12... | collective-permute-start | bytes 1179656 | tf_op jit(solution)/shard_map/ppermute | solution.py:626
  148.3 28.0 %collective-permute-start.23 = (f32[384,256]{1,0:T(8,128)}, f32[384,256]{1,0:T(8,128)}, u32[]{:S(2)}, u32[]{:S(2)}) collective-permute-start(f32[384,256]{1,0:T(8,128)} %get-tuple-element.65), channel_id=1, source_target_pairs={{0,6},{2,0},{4,2},{6,4},{1,7},{3,1},{5,3},{7,5},{8,14},{10,8},{12,... | collective-permute-start | bytes 1179656 | tf_op jit(solution)/shard_map/ppermute | solution.py:626
  161.1 1.3 copy-start.3
  165.3 11.1 %collective-permute-start.26 = (bf16[512,384]{1,0:T(8,128)(2,1)}, bf16[512,384]{1,0:T(8,128)(2,1)S(1)}, u32[]{:S(2)}, u32[]{:S(2)}) collective-permute-start(bf16[512,384]{1,0:T(8,128)(2,1)} %get-tuple-element.70), channel_id=1, source_target_pairs={{0,1},{1,0},{2,3},{3,2},{4,5},{5,4},{6,7},{7,6},{8,9},{9,8},{10,11... | collective-permute-start | bytes 1179656 | tf_op jit(solution)/shard_map/ppermute | solution.py:630
  166.6 10.2 %collective-permute-start.27 = (bf16[512,384]{1,0:T(8,128)(2,1)}, bf16[512,384]{1,0:T(8,128)(2,1)S(1)}, u32[]{:S(2)}, u32[]{:S(2)}) collective-permute-start(bf16[512,384]{1,0:T(8,128)(2,1)} %get-tuple-element.71), channel_id=1, source_target_pairs={{0,16},{16,0},{1,17},{17,1},{2,18},{18,2},{3,19},{19,3},{4,20},{20... | collective-permute-start | bytes 1179656 | tf_op jit(solution)/shard_map/ppermute | solution.py:630
  181.8 28.8 %all-to-all-start.2 = ((bf16[4,256,384]{2,1,0:T(8,128)(2,1)}), bf16[4,256,384]{2,1,0:T(8,128)(2,1)S(1)}, u32[]{:S(2)}, u32[]{:S(2)}) async-start(bf16[4,256,384]{2,1,0:T(8,128)(2,1)} %bitcast.96), calls=%async_computation.2 | async-start | bytes 1572864 | tf_op jit(solution)/shard_map/all_to_all | solution.py:699
  191.0 5.9 %collective-permute-start.28 = (f32[2,48,128]{2,1,0:T(8,128)S(1)}, f32[2,48,128]{2,1,0:T(8,128)S(1)}, u32[]{:S(2)}, u32[]{:S(2)}) collective-permute-start(f32[2,48,128]{2,1,0:T(8,128)S(1)} %bitcast.104), channel_id=1, source_target_pairs={{0,8},{8,16},{16,24},{1,9},{9,17},{17,25},{2,10},{10,18},{18,26},{... | collective-permute-start | bytes 147464 | tf_op jit(solution)/shard_map/ppermute | solution.py:611
  193.7 3.8 %collective-permute-start.29 = (f32[2,48,128]{2,1,0:T(8,128)S(1)}, f32[2,48,128]{2,1,0:T(8,128)S(1)}, u32[]{:S(2)}, u32[]{:S(2)}) collective-permute-start(f32[2,48,128]{2,1,0:T(8,128)S(1)} %bitcast.103), channel_id=1, source_target_pairs={{8,0},{16,8},{24,16},{9,1},{17,9},{25,17},{10,2},{18,10},{26,18},{... | collective-permute-start | bytes 147464 | tf_op jit(solution)/shard_map/ppermute | solution.py:612
  195.0 14.0 %collective-permute-start.35 = (bf16[512,384]{1,0:T(8,128)(2,1)}, bf16[512,384]{1,0:T(8,128)(2,1)S(1)}, u32[]{:S(2)}, u32[]{:S(2)}) collective-permute-start(bf16[512,384]{1,0:T(8,128)(2,1)} %get-tuple-element.77.refs_3_), channel_id=1, source_target_pairs={{0,8},{8,0},{1,9},{9,1},{2,10},{10,2},{3,11},{11,3},{4,12},{12,4},... | collective-permute-start | bytes 1179656 | tf_op jit(solution)/shard_map/ppermute | solution.py:630
  196.8 16.4 %collective-permute-start.36 = (bf16[512,384]{1,0:T(8,128)(2,1)}, bf16[512,384]{1,0:T(8,128)(2,1)}, u32[]{:S(2)}, u32[]{:S(2)}) collective-permute-start(bf16[512,384]{1,0:T(8,128)(2,1)} %get-tuple-element.78.refs_4_), channel_id=1, source_target_pairs={{0,8},{8,0},{1,9},{9,1},{2,10},{10,2},{3,11},{11,3},{4,12},{12,4},... | collective-permute-start | bytes 1179656 | tf_op jit(solution)/shard_map/ppermute | solution.py:630
  196.9 17.8 %copy-start.25 = (f32[2,48,128]{2,1,0:T(8,128)}, f32[2,48,128]{2,1,0:T(8,128)S(1)}, u32[]{:S(2)}) copy-start(f32[2,48,128]{2,1,0:T(8,128)S(1)} %collective-permute-done.28.refs_9_.refs_2_) | copy-start | bytes 147460
  197.4 13.2 %copy-start.26 = (f32[2,48,128]{2,1,0:T(8,128)}, f32[2,48,128]{2,1,0:T(8,128)S(1)}, u32[]{:S(2)}) copy-start(f32[2,48,128]{2,1,0:T(8,128)S(1)} %collective-permute-done.29.refs_10_.refs_3_) | copy-start | bytes 147460
  197.5 7.4 %collective-permute-start.30 = (f32[36,2,128]{2,1,0:T(2,128)S(1)}, f32[36,2,128]{2,1,0:T(2,128)S(1)}, u32[]{:S(2)}, u32[]{:S(2)}) collective-permute-start(f32[36,2,128]{2,1,0:T(2,128)S(1)} %pad_maximum_fusion), channel_id=1, source_target_pairs={{0,1},{1,2},{2,3},{3,4},{4,5},{5,6},{6,7},{8,9},{9,10},{10,11},{11... | collective-permute-start | bytes 110600 | tf_op jit(solution)/shard_map/ppermute | solution.py:617
  201.0 5.9 %collective-permute-start.31 = (f32[36,2,128]{2,1,0:T(2,128)S(1)}, f32[36,2,128]{2,1,0:T(2,128)S(1)}, u32[]{:S(2)}, u32[]{:S(2)}) collective-permute-start(f32[36,2,128]{2,1,0:T(2,128)S(1)} %pad_maximum_fusion.1), channel_id=1, source_target_pairs={{1,0},{2,1},{3,2},{4,3},{5,4},{6,5},{7,6},{9,8},{10,9},{11,10},{12... | collective-permute-start | bytes 110600 | tf_op jit(solution)/shard_map/ppermute | solution.py:618
  202.3 12.4 %collective-permute-start.32 = (bf16[1024,384]{1,0:T(8,128)(2,1)}, bf16[1024,384]{1,0:T(8,128)(2,1)}, u32[]{:S(2)}, u32[]{:S(2)}) collective-permute-start(bf16[1024,384]{1,0:T(8,128)(2,1)} %get-tuple-element.74), channel_id=1, source_target_pairs={{0,8},{8,0},{1,9},{9,1},{2,10},{10,2},{3,11},{11,3},{4,12},{12,4},... | collective-permute-start | bytes 2359304 | tf_op jit(solution)/shard_map/ppermute | solution.py:630
  204.9 5.7 %copy-start.27 = (f32[36,2,128]{2,1,0:T(2,128)}, f32[36,2,128]{2,1,0:T(2,128)S(1)}, u32[]{:S(2)}) copy-start(f32[36,2,128]{2,1,0:T(2,128)S(1)} %collective-permute-done.30.refs_11_.refs_4_) | copy-start | bytes 110596
  204.9 9.9 %collective-permute-start.33 = (bf16[1024,384]{1,0:T(8,128)(2,1)}, bf16[1024,384]{1,0:T(8,128)(2,1)}, u32[]{:S(2)}, u32[]{:S(2)}) collective-permute-start(bf16[1024,384]{1,0:T(8,128)(2,1)} %get-tuple-element.75), channel_id=1, source_target_pairs={{0,8},{8,0},{1,9},{9,1},{2,10},{10,2},{3,11},{11,3},{4,12},{12,4},... | collective-permute-start | bytes 2359304 | tf_op jit(solution)/shard_map/ppermute | solution.py:630
  206.8 3.8 %copy-start.28 = (f32[36,2,128]{2,1,0:T(2,128)}, f32[36,2,128]{2,1,0:T(2,128)S(1)}, u32[]{:S(2)}) copy-start(f32[36,2,128]{2,1,0:T(2,128)S(1)} %collective-permute-done.31.refs_12_.refs_5_) | copy-start | bytes 110596
  206.8 7.9 %collective-permute-start.34 = (bf16[1024,384]{1,0:T(8,128)(2,1)}, bf16[1024,384]{1,0:T(8,128)(2,1)}, u32[]{:S(2)}, u32[]{:S(2)}) collective-permute-start(bf16[1024,384]{1,0:T(8,128)(2,1)} %get-tuple-element.76), channel_id=1, source_target_pairs={{0,8},{8,0},{1,9},{9,1},{2,10},{10,2},{3,11},{11,3},{4,12},{12,4},... | collective-permute-start | bytes 2359304 | tf_op jit(solution)/shard_map/ppermute | solution.py:630
  209.0 5.8 %copy-start.21 = (bf16[512,384]{1,0:T(8,128)(2,1)}, bf16[512,384]{1,0:T(8,128)(2,1)S(1)}, u32[]{:S(2)}) copy-start(bf16[512,384]{1,0:T(8,128)(2,1)S(1)} %collective-permute-done.35.refs_5_) | copy-start | bytes 1179652
  210.6 4.2 %copy-start.2 = (bf16[4,256,384]{2,1,0:T(8,128)(2,1)}, bf16[4,256,384]{2,1,0:T(8,128)(2,1)S(1)}, u32[]{:S(2)}) copy-start(bf16[4,256,384]{2,1,0:T(8,128)(2,1)S(1)} %all-to-all-done.2) | copy-start | bytes 2359300
  210.6 23.4 %collective-permute-start.38 = (bf16[1024,384]{1,0:T(8,128)(2,1)S(1)}, bf16[1024,384]{1,0:T(8,128)(2,1)S(1)}, u32[]{:S(2)}, u32[]{:S(2)}) collective-permute-start(bf16[1024,384]{1,0:T(8,128)(2,1)S(1)} %bitcast.85), channel_id=1, source_target_pairs={{0,1},{1,0},{2,3},{3,2},{4,5},{5,4},{6,7},{7,6},{8,9},{9,8},{10,11... | collective-permute-start | bytes 2359304 | tf_op jit(solution)/shard_map/ppermute | solution.py:630
  213.3 20.8 %collective-permute-start.37 = (bf16[1024,384]{1,0:T(8,128)(2,1)S(1)}, bf16[1024,384]{1,0:T(8,128)(2,1)}, u32[]{:S(2)}, u32[]{:S(2)}) collective-permute-start(bf16[1024,384]{1,0:T(8,128)(2,1)S(1)} %bitcast.86), channel_id=1, source_target_pairs={{0,16},{16,0},{1,17},{17,1},{2,18},{18,2},{3,19},{19,3},{4,20},{20... | collective-permute-start | bytes 2359304 | tf_op jit(solution)/shard_map/ppermute | solution.py:630
  226.2 12.9 %collective-permute-start.41 = (bf16[1024,384]{1,0:T(8,128)(2,1)}, bf16[1024,384]{1,0:T(8,128)(2,1)}, u32[]{:S(2)}, u32[]{:S(2)}) collective-permute-start(bf16[1024,384]{1,0:T(8,128)(2,1)} %bitcast.88), channel_id=1, source_target_pairs={{0,8},{8,0},{1,9},{9,1},{2,10},{10,2},{3,11},{11,3},{4,12},{12,4},... | collective-permute-start | bytes 2359304 | tf_op jit(solution)/shard_map/ppermute | solution.py:630
  236.8 3.0 %collective-permute-start.42 = (bf16[1024,384]{1,0:T(8,128)(2,1)}, bf16[1024,384]{1,0:T(8,128)(2,1)S(1)}, u32[]{:S(2)}, u32[]{:S(2)}) collective-permute-start(bf16[1024,384]{1,0:T(8,128)(2,1)} %get-tuple-element.81.refs_2_), channel_id=1, source_target_pairs={{0,8},{8,0},{1,9},{9,1},{2,10},{10,2},{3,11},{11,3},{4,12},{12,4},... | collective-permute-start | bytes 2359304 | tf_op jit(solution)/shard_map/ppermute | solution.py:630
  237.4 3.4 %collective-permute-start.43 = (bf16[1024,384]{1,0:T(8,128)(2,1)}, bf16[1024,384]{1,0:T(8,128)(2,1)}, u32[]{:S(2)}, u32[]{:S(2)}) collective-permute-start(bf16[1024,384]{1,0:T(8,128)(2,1)} %get-tuple-element.82.refs_4_), channel_id=1, source_target_pairs={{0,8},{8,0},{1,9},{9,1},{2,10},{10,2},{3,11},{11,3},{4,12},{12,4},... | collective-permute-start | bytes 2359304 | tf_op jit(solution)/shard_map/ppermute | solution.py:630
  237.5 15.8 %collective-permute-start.39 = (bf16[512,384]{1,0:T(8,128)(2,1)}, bf16[512,384]{1,0:T(8,128)(2,1)S(1)}, u32[]{:S(2)}, u32[]{:S(2)}) collective-permute-start(bf16[512,384]{1,0:T(8,128)(2,1)} %get-tuple-element.79), channel_id=1, source_target_pairs={{0,1},{1,0},{2,3},{3,2},{4,5},{5,4},{6,7},{7,6},{8,9},{9,8},{10,11... | collective-permute-start | bytes 1179656 | tf_op jit(solution)/shard_map/ppermute | solution.py:630
  239.0 14.3 %collective-permute-start.40 = (bf16[512,384]{1,0:T(8,128)(2,1)}, bf16[512,384]{1,0:T(8,128)(2,1)S(1)}, u32[]{:S(2)}, u32[]{:S(2)}) collective-permute-start(bf16[512,384]{1,0:T(8,128)(2,1)} %get-tuple-element.80), channel_id=1, source_target_pairs={{0,16},{16,0},{1,17},{17,1},{2,18},{18,2},{3,19},{19,3},{4,20},{20... | collective-permute-start | bytes 1179656 | tf_op jit(solution)/shard_map/ppermute | solution.py:630
  239.9 0.9 copy-start.15
  254.8 1.9 collective-permute-start.44
  254.8 2.5 collective-permute-start.45
  (18 other events, 14.2 us)
